TPU v7x, 32 devices: a whole 2x2x4 slice. The times are simulated.
32 devices in a mesh: groups: 2 (over y), dp: 4 (over z), tensor: 4 (over x, core).
Axes of the slice: x: 2, y: 2, z: 4, core: 2. Of those that a mesh axis runs over, the one named last changes fastest.
Arguments:
- normed_input: bfloat16 [4096, 8192], P(('groups', 'dp'), 'tensor'), parts along dimension 0, may hold values from -6 to 6
- rotated_queries: bfloat16 [4096, 8192], P(('groups', 'dp'), 'tensor'), parts along dimension 0, may hold values from -6 to 6
- rotated_keys: bfloat16 [4096, 1024], P(('groups', 'dp'), 'tensor'), parts along dimension 0, may hold values from -6 to 6
- value_rows: bfloat16 [4096, 1024], P(('groups', 'dp'), 'tensor'), parts along dimension 0, may hold values from -6 to 6
- output_gradient: bfloat16 [4096, 8192], P(('groups', 'dp'), 'tensor'), parts along dimension 0, may hold values from -6 to 6
- document_length: int32 [8, 8], P(('groups', 'dp')), parts along dimension 0, may hold values from 1 to 256, 512 in all within a row
- document_adapter: int32 [8, 8], P(('groups', 'dp')), parts along dimension 0, may hold values from 0 to 3
- adapter_in_slot: int32 [4], replicated, may hold values from 0 to 3, each once
- down_weight: bfloat16 [8, 16, 8192], P(('groups', 'dp'), None, 'tensor'), parts along dimension 0, may hold values from -0.0625 to 0.0625
- up_weight: bfloat16 [8, 16, 8192], P(('groups', 'dp'), None, 'tensor'), parts along dimension 0, may hold values from -0.0625 to 0.0625
Outputs:
- input_gradient: bfloat16 [4096, 8192], P(('groups', 'dp'), 'tensor'), parts along dimension 0
- key_gradient: bfloat16 [4096, 1024], P(('groups', 'dp'), 'tensor'), parts along dimension 0
- value_gradient: bfloat16 [4096, 1024], P(('groups', 'dp'), 'tensor'), parts along dimension 0
- down_gradient: float32 [8, 16, 8192], P(('groups', 'dp'), None, 'tensor'), parts along dimension 0
- up_gradient: float32 [8, 16, 8192], P(('groups', 'dp'), None, 'tensor'), parts along dimension 0
There are 2 independent parts, one for each index of `groups`. A program takes and returns all parts, laid end to end along the dimension named above; an argument that names none is the same for every part. Nothing has to cross between parts.
Inputs may be any that keep to these rules, and one draw needn't show every extreme that they name: `document_length`: each row sums to 512. `adapter_in_slot`: each adapter once.
All inputs are finite; a program needn't handle non-finite values.
Results may differ from a plain program's by a relative error of at most 0.012.
The roundings to bfloat16 on the way count: a program that leaves them out, or rounds other values in their place, can miss the bound.
Values may be sent and summed in bfloat16 or wider, within the bound.
No kernel may reach another device: no remote copies, remote signals or barrier semaphores. Data moves between devices by JAX's collectives and lax.ppermute only.
A program may use at most 64 MiB of HBM per device.

v0:
```python
import math

import jax
import jax.numpy as jnp
from jax import lax
from jax.sharding import PartitionSpec as P

QUERY_HEAD_COUNT = 64
KEY_VALUE_HEADS = 8
HEAD_SIZE = 128


MASKED = -1e30
ADAPTER_SCALE = 2.0


def document_layout(lengths, adapters, row_count):
    position = jnp.arange(row_count, dtype=jnp.int32)
    ends = jnp.cumsum(lengths)
    starts = ends - lengths
    inside = ((position[:, None] >= starts[None, :]) & (position[:, None] < ends[None, :])).astype(
        jnp.int32
    )
    document = jnp.sum(inside * jnp.arange(lengths.shape[0], dtype=jnp.int32)[None, :], axis=1)
    adapter = jnp.sum(inside * adapters[None, :], axis=1)
    allowed = (document[:, None] == document[None, :]) & (position[None, :] <= position[:, None])
    return (allowed, adapter)


def head_backward(query_head, key_head, value_head, grad_head, allowed, score_scale):
    scores = (
        lax.dot_general(
            query_head, key_head, (((1,), (1,)), ((), ())), preferred_element_type=jnp.float32
        )
        * score_scale
    )
    scores = jnp.where(allowed, scores, MASKED)
    largest = jnp.max(scores, axis=1, keepdims=True)
    numerator = jnp.where(allowed, jnp.exp(scores - largest), 0.0)
    weights = numerator / jnp.sum(numerator, axis=1, keepdims=True)
    rounded = weights.astype(jnp.bfloat16)
    attended = jnp.dot(rounded, value_head, preferred_element_type=jnp.float32)
    row_delta = jnp.sum(grad_head.astype(jnp.float32) * attended, axis=1, keepdims=True)
    grad_value = lax.dot_general(
        rounded, grad_head, (((0,), (0,)), ((), ())), preferred_element_type=jnp.float32
    )
    grad_weights = lax.dot_general(
        grad_head, value_head, (((1,), (1,)), ((), ())), preferred_element_type=jnp.float32
    )
    grad_scores = (weights * (grad_weights - row_delta)).astype(jnp.bfloat16)
    grad_query = (
        jnp.dot(grad_scores, key_head, preferred_element_type=jnp.float32) * score_scale
    ).astype(jnp.bfloat16)
    grad_key = (
        lax.dot_general(
            grad_scores, query_head, (((0,), (0,)), ((), ())), preferred_element_type=jnp.float32
        )
        * score_scale
    )
    return (grad_query, grad_key, grad_value)


def attention_backward(rotated_queries, rotated_keys, value_rows, output_gradient, allowed):
    row_count = rotated_queries.shape[0]
    head_total = rotated_queries.shape[1] // HEAD_SIZE
    kv_total = rotated_keys.shape[1] // HEAD_SIZE
    group_share = QUERY_HEAD_COUNT // KEY_VALUE_HEADS
    score_scale = 1.0 / math.sqrt(HEAD_SIZE)
    query_heads = rotated_queries.reshape(row_count, head_total, HEAD_SIZE).transpose(1, 0, 2)
    grad_heads = output_gradient.reshape(row_count, head_total, HEAD_SIZE).transpose(1, 0, 2)
    key_heads = rotated_keys.reshape(row_count, kv_total, HEAD_SIZE).transpose(1, 0, 2)
    value_heads = value_rows.reshape(row_count, kv_total, HEAD_SIZE).transpose(1, 0, 2)
    kv_index = jnp.arange(head_total, dtype=jnp.int32) // group_share

    def one_head(items):
        query_head, grad_head, index = items
        return head_backward(
            query_head, key_heads[index], value_heads[index], grad_head, allowed, score_scale
        )

    grad_query, grad_key, grad_value = lax.map(one_head, (query_heads, grad_heads, kv_index))
    grad_query = grad_query.transpose(1, 0, 2).reshape(row_count, head_total * HEAD_SIZE)
    grad_key = jnp.sum(
        grad_key.reshape(kv_total, group_share, row_count, HEAD_SIZE), axis=1
    ).astype(jnp.bfloat16)
    grad_value = jnp.sum(
        grad_value.reshape(kv_total, group_share, row_count, HEAD_SIZE), axis=1
    ).astype(jnp.bfloat16)
    grad_key = grad_key.transpose(1, 0, 2).reshape(row_count, kv_total * HEAD_SIZE)
    grad_value = grad_value.transpose(1, 0, 2).reshape(row_count, kv_total * HEAD_SIZE)
    return (grad_query, grad_key, grad_value)


def select_rank(wide_terms, onehot, adapter_count, low_rank):
    row_count = wide_terms.shape[0]
    return jnp.sum(
        wide_terms.reshape(row_count, adapter_count, low_rank) * onehot[:, :, None], axis=1
    )


def spread_rank(low_values, onehot, adapter_count, low_rank):
    row_count = low_values.shape[0]
    rounded = low_values.astype(jnp.bfloat16).astype(jnp.float32)
    return (
        (onehot[:, :, None] * rounded[:, None, :])
        .reshape(row_count, adapter_count * low_rank)
        .astype(jnp.bfloat16)
    )


def local(
    normed_input,
    rotated_queries,
    rotated_keys,
    value_rows,
    output_gradient,
    document_length,
    document_adapter,
    adapter_in_slot,
    down_weight,
    up_weight,
):
    row_count = normed_input.shape[0]
    local_rows = down_weight.shape[0]
    all_down, all_up = (
        lax.all_gather(down_weight, "dp", axis=0, tiled=True),
        lax.all_gather(up_weight, "dp", axis=0, tiled=True),
    )
    adapter_count = all_down.shape[0]
    low_rank = all_down.shape[1]
    down_matrix = all_down.reshape(adapter_count * low_rank, all_down.shape[2])
    up_matrix = all_up.reshape(adapter_count * low_rank, all_up.shape[2])
    allowed, adapter_of_token = document_layout(document_length[0], document_adapter[0], row_count)
    onehot = (adapter_in_slot[None, :] == adapter_of_token[:, None]).astype(jnp.float32)
    input_all = lax.dot_general(
        normed_input, down_matrix, (((1,), (1,)), ((), ())), preferred_element_type=jnp.float32
    )
    input_part = select_rank(input_all, onehot, adapter_count, low_rank)
    low_inputs = lax.psum(input_part, "tensor")
    query_gradient, key_gradient, value_gradient = attention_backward(
        rotated_queries, rotated_keys, value_rows, output_gradient, allowed
    )
    grad_all = lax.dot_general(
        query_gradient, up_matrix, (((1,), (1,)), ((), ())), preferred_element_type=jnp.float32
    )
    grad_part = select_rank(grad_all, onehot, adapter_count, low_rank)
    low_grads = lax.psum(grad_part, "tensor")
    input_wide_rows = spread_rank(low_inputs, onehot, adapter_count, low_rank)
    gradient_wide_rows = spread_rank(low_grads, onehot, adapter_count, low_rank)
    input_gradient = (
        ADAPTER_SCALE * jnp.dot(gradient_wide_rows, down_matrix, preferred_element_type=jnp.float32)
    ).astype(jnp.bfloat16)
    columns = input_wide_rows
    product = lax.dot_general(
        columns, query_gradient, (((0,), (0,)), ((), ())), preferred_element_type=jnp.float32
    )
    up_gradient = lax.psum_scatter(
        ADAPTER_SCALE
        * product.reshape(local_rows * lax.axis_size("dp"), low_rank, query_gradient.shape[1]),
        "dp",
        scatter_dimension=0,
        tiled=True,
    )
    columns = gradient_wide_rows
    product = lax.dot_general(
        columns, normed_input, (((0,), (0,)), ((), ())), preferred_element_type=jnp.float32
    )
    down_gradient = lax.psum_scatter(
        ADAPTER_SCALE
        * product.reshape(local_rows * lax.axis_size("dp"), low_rank, normed_input.shape[1]),
        "dp",
        scatter_dimension=0,
        tiled=True,
    )
    return (input_gradient, key_gradient, value_gradient, down_gradient, up_gradient)


def solution(mesh):
    return jax.shard_map(
        local,
        mesh=mesh,
        in_specs=(
            P(("groups", "dp"), "tensor"),
            P(("groups", "dp"), "tensor"),
            P(("groups", "dp"), "tensor"),
            P(("groups", "dp"), "tensor"),
            P(("groups", "dp"), "tensor"),
            P(("groups", "dp"), None),
            P(("groups", "dp"), None),
            P(),
            P(("groups", "dp"), None, "tensor"),
            P(("groups", "dp"), None, "tensor"),
        ),
        out_specs=(
            P(("groups", "dp"), "tensor"),
            P(("groups", "dp"), "tensor"),
            P(("groups", "dp"), "tensor"),
            P(("groups", "dp"), None, "tensor"),
            P(("groups", "dp"), None, "tensor"),
        ),
        check_vma=False,
    )
```

profile of v0, /device:TPU:0, one launch (start us, length us, event | category | flops | bytes accessed | tf_op | source)
XLA Modules:
  0.0 305.3 jit_solution(12176815669662407550)
XLA Ops:
  8.9 3.9 %copy.57 = bf16[512,2048]{0,1:T(8,128)(2,1)} copy(bf16[512,2048]{1,0:T(8,128)(2,1)} %param.16) | data formatting | bytes 4194304 | tf_op args[4]
  12.8 4.0 %copy.55 = bf16[512,2048]{0,1:T(8,128)(2,1)} copy(bf16[512,2048]{1,0:T(8,128)(2,1)} %param.13) | data formatting | bytes 4194304 | tf_op args[1]
  17.2 188.3 %while.15 = (s32[]{:T(128)}, bf16[16,512,128]{1,2,0:T(8,128)(2,1)}, f32[16,512,128]{2,1,0:T(8,128)}, f32[16,512,128]{2,1,0:T(8,128)}, bf16[16,512,128]{1,2,0:T(8...) while((s32[]{:T(128)}, bf16[16,512,128]{1,2,0:T(8,128)(2,1)}, ...), condition=%wide.region_7.8_spmd.clone, body=%wide.region_3.7_spmd.clone.sunk | while | flops 412219904 | bytes 9219775 | solution.py:81
  44.8 2.0 fusion.104
  56.6 2.0 fusion.104
  68.4 2.0 fusion.104
  80.1 2.0 fusion.104
  91.9 2.0 fusion.104
  103.7 2.0 fusion.104
  115.5 2.0 fusion.104
  127.3 2.0 fusion.104
  139.0 2.0 fusion.104
  150.8 2.0 fusion.104
  162.6 2.0 fusion.104
  197.9 2.0 fusion.104
  205.6 15.6 %all_gather.6 = bf16[4,16,2048]{2,1,0:T(8,128)(2,1)S(1)} all-gather(bf16[1,16,2048]{2,1,0:T(8,128)(2,1)S(1)} %copy-done.3), channel_id=1, replica_groups=mesh['groups'=2,'dp'=4,'tensor'=4] {'dp'}, dimensions={0}, use_global_device_ids=true | all-gather | bytes 327680 | tf_op jit(solution)/shard_map/all_gather | solution.py:127
  221.2 14.6 %all_gather.7 = bf16[4,16,2048]{2,1,0:T(8,128)(2,1)S(1)} all-gather(bf16[1,16,2048]{2,1,0:T(8,128)(2,1)S(1)} %copy-done.4), channel_id=1, replica_groups=mesh['groups'=2,'dp'=4,'tensor'=4] {'dp'}, dimensions={0}, use_global_device_ids=true | all-gather | bytes 327680 | tf_op jit(solution)/shard_map/all_gather | solution.py:126
  235.8 2.1 fusion.47
  238.7 10.7 %all-reduce = (bf16[512,16]{0,1:T(8,128)(2,1)S(1)}, bf16[512,16]{0,1:T(8,128)(2,1)S(1)}) all-reduce(f32[512,16]{0,1:T(8,128)S(1)} %fusion.47, f32[512,16]{0,1:T(8,128)S(1)} %fusion.48), channel_id=1, replica_groups=mesh['groups'=2,'dp'=4,'tensor'=4] {'tensor'}, use_global_device_ids=true, to_apply=%region_9.10 | all-reduce | flops 16384 | bytes 98304 | tf_op jit(solution)/shard_map/psum | solution.py:147
  249.4 3.2 %convolution_multiply_fusion.4 = f32[4,16,2048]{2,1,0:T(8,128)} fusion(bf16[512,2048,1]{0,1,2:T(8,128)(2,1)} %bitcast.149, f32[512,16]{0,1:T(8,128)S(1)} %convert_element_type.106, f32[512,4]{0,1:T(4,128)S(1)} %compare_convert_fusion), kind=kOutput, calls=%fused_computation.50 | convolution fusion | flops 134414336 | bytes 2662400 | tf_op jit(solution)/shard_map/dot_general | solution.py:154
  254.1 4.1 %bitcast_reduce_fusion = (bf16[2,512,128]{2,1,0:T(8,128)(2,1)S(1)}, bf16[2,512,128]{2,1,0:T(8,128)(2,1)S(1)}) fusion(f32[16,512,128]{2,1,0:T(8,128)} %get-tuple-element.61, f32[16,512,128]{2,1,0:T(8,128)} %get-tuple-element.60), kind=kLoop, calls=%fused_computation.46 | loop fusion | flops 1835008 | bytes 8912896 | tf_op jit(solution)/shard_map/reduce_sum | solution.py:86
  260.2 2.0 fusion.40
  262.2 13.4 %reduce-scatter.5.cloned.1.call-done = f32[1,16,2048]{2,1,0:T(8,128)} async-done(((f32[4,16,2048]{2,1,0:T(8,128)}), f32[1,16,2048]{2,1,0:T(8,128)}) %reduce-scatter.5.cloned.1.call-update) | async-done | bytes 131088 | tf_op jit(solution)/shard_map/reduce_scatter | solution.py:157
  275.6 22.8 %reduce-scatter.3.cloned.1.call-done = f32[1,16,2048]{2,1,0:T(8,128)} async-done(((f32[4,16,2048]{2,1,0:T(8,128)}), f32[1,16,2048]{2,1,0:T(8,128)}) %reduce-scatter.3.cloned.1.call-update) | async-done | bytes 131088 | tf_op jit(solution)/shard_map/reduce_scatter | solution.py:168
  (184 shorter events, 139.1 us)
Async XLA Ops:
  7.2 230.8 %copy-start = (bf16[512,2048]{1,0:T(8,128)(2,1)S(1)}, bf16[512,2048]{1,0:T(8,128)(2,1)}, u32[]{:S(2)}) copy-start(bf16[512,2048]{1,0:T(8,128)(2,1)} %param.12) | copy-start | bytes 6291460
  7.2 268.4 %reduce-scatter.5.cloned.1.call-start = ((), (), s32[]{:S(2)}) async-start(), calls=%async_computation.3 | async-start | bytes 655360 | tf_op jit(solution)/shard_map/reduce_scatter | solution.py:157
  12.8 4.0 %copy-start.1 = (bf16[512,256]{1,0:T(8,128)(2,1)S(1)}, bf16[512,256]{1,0:T(8,128)(2,1)}, u32[]{:S(2)}) copy-start(bf16[512,256]{1,0:T(8,128)(2,1)} %param.15) | copy-start | bytes 786436
  12.8 4.1 %copy-start.2 = (bf16[512,256]{1,0:T(8,128)(2,1)S(1)}, bf16[512,256]{1,0:T(8,128)(2,1)}, u32[]{:S(2)}) copy-start(bf16[512,256]{1,0:T(8,128)(2,1)} %param.14) | copy-start | bytes 786436
  12.8 4.3 %copy-start.5 = (s32[1,8]{1,0:T(1,128)S(1)}, s32[1,8]{1,0:T(1,128)}, u32[]{:S(2)}) copy-start(s32[1,8]{1,0:T(1,128)} %param.18) | copy-start | bytes 100
  17.2 188.4 %copy-start.3 = (bf16[1,16,2048]{2,1,0:T(8,128)(2,1)S(1)}, bf16[1,16,2048]{2,1,0:T(8,128)(2,1)}, u32[]{:S(2)}) copy-start(bf16[1,16,2048]{2,1,0:T(8,128)(2,1)} %param.21) | copy-start | bytes 196612
  17.2 204.0 %copy-start.4 = (bf16[1,16,2048]{2,1,0:T(8,128)(2,1)S(1)}, bf16[1,16,2048]{2,1,0:T(8,128)(2,1)}, u32[]{:S(2)}) copy-start(bf16[1,16,2048]{2,1,0:T(8,128)(2,1)} %param.20) | copy-start | bytes 196612
  17.2 218.5 %copy-start.6 = (s32[4]{0:T(128)S(1)}, s32[4]{0:T(128)}, u32[]{:S(2)}) copy-start(s32[4]{0:T(128)} %param.19) | copy-start | bytes 52
  252.7 45.8 %reduce-scatter.3.cloned.1.call-start = ((), (), s32[]{:S(2)}) async-start(), calls=%async_computation.2 | async-start | bytes 655360 | tf_op jit(solution)/shard_map/reduce_scatter | solution.py:168
Sparse Core Ops, SparseCore 0:
  252.8 22.7 reduce-scatter.4
  278.5 19.9 reduce-scatter.2
where the time goes:
time: 308 us; the launch traced here: 305 us
  matrix products  141 us (46%)
  blocking collectives  40.9 us (13%)
  waiting for transfers between devices  36.2 us (12%)
  local copies, waits for them, and re-layouts  32.1 us (10%)
  loops' own time  31.6 us (10%)
  between operations  14.2 us (5%)
  other arithmetic  9.7 us (3%)
    reduce_scatter x2, waiting for transfers between devices, local(): lax.psum_scatter(ADAPTER_SCALE * product.reshape(local_rows * lax.axis_si...  36.2 us
    dot_general x16, matrix products, head_backward(): lax.dot_general(rounded, grad_head, (((0,), (0,)), ((), ())), preferred_e...  31.9 us
    another operation x1, loops' own time, attention_backward(): lax.map(one_head, (query_heads, grad_heads, kv_index))  31.6 us
    dot_general x16, matrix products, head_backward(): lax.dot_general(grad_scores, query_head, (((0,), (0,)), ((), ())), prefer...  30.6 us
    dot_general x16, matrix products, head_backward(): lax.dot_general(grad_head, value_head, (((1,), (1,)), ((), ())), preferre...  21.2 us
    dot_general x16, matrix products, head_backward(): attended = jnp.dot(rounded, value_head, preferred_element_type=jnp.float32)  21.1 us
    dot_general x16, matrix products, head_backward(): lax.dot_general(query_head, key_head, (((1,), (1,)), ((), ())), preferred...  20.8 us
    all_gather x1, blocking collectives, local(): lax.all_gather(up_weight, 'dp', axis=0, tiled=True)  15.6 us
  transfers between devices with their start and end apart: 2, of which 2 were waited for; matrix products, arithmetic and copies ran while one was open for 3% of the time, Pallas kernels for 0%

commit v1 on v0

v1 whole, which is shorter than its diff:
```python
import functools
import math

import jax
import jax.numpy as jnp
from jax import lax
from jax.experimental import pallas as pl
from jax.experimental.pallas import tpu as pltpu
from jax.sharding import PartitionSpec as P

QUERY_HEAD_COUNT = 64
KEY_VALUE_HEADS = 8
HEAD_SIZE = 128
GROUP_SHARE = QUERY_HEAD_COUNT // KEY_VALUE_HEADS
DOCUMENT_REACH = 256
BLOCK = 128

MASKED = -1e30
ADAPTER_SCALE = 2.0
LOG2_E = 1.4426950408889634
VMEM_BYTES = 40 * 1024 * 1024

NN = (((1,), (0,)), ((), ()))
NT = (((1,), (1,)), ((), ()))
TN = (((0,), (0,)), ((), ()))


def mxu(a, b, dims):
    return lax.dot_general(a, b, dims, preferred_element_type=jnp.float32)


def query_spans(row_count):
    return [
        (at, max(0, (at - (DOCUMENT_REACH - 1)) // BLOCK * BLOCK), at + BLOCK)
        for at in range(0, row_count, BLOCK)
    ]


def attention_kernel(
    len_ref, q_ref, g_ref, k_ref, v_ref, gq_ref, gk_ref, gv_ref, bias_ref
):
    row_count = q_ref.shape[0]
    scale = 1.0 / math.sqrt(HEAD_SIZE)

    @pl.when(pl.program_id(0) == 0)
    def _():
        at = 0
        for first, low, high in query_spans(row_count):
            width = high - low
            query = lax.broadcasted_iota(jnp.int32, (1, BLOCK), 1) + first
            start = jnp.zeros((1, BLOCK), jnp.int32)
            end = jnp.int32(0)
            for index in range(len_ref.shape[1] - 1):
                end = end + len_ref[0, index]
                start = jnp.where(query >= end, end, start)
            key = lax.broadcasted_iota(jnp.int32, (width, BLOCK), 0) + low
            bias_ref[at : at + width, :] = jnp.where((key >= start) & (key <= query), 0.0, MASKED)
            at += width

    heads = [slice(h * HEAD_SIZE, (h + 1) * HEAD_SIZE) for h in range(GROUP_SHARE)]
    key_t = k_ref[...].T
    grad_key = [None] * (row_count // BLOCK)
    grad_value = [None] * (row_count // BLOCK)
    at = 0
    for first, low, high in query_spans(row_count):
        width = high - low
        rows = slice(first, first + BLOCK)
        query = jnp.concatenate([q_ref[rows, head] for head in heads], axis=0)
        grad = jnp.concatenate([g_ref[rows, head] for head in heads], axis=0)
        scores = mxu(k_ref[low:high, :], query, NT)
        grad_weights = mxu(v_ref[low:high, :], grad, NT)
        bias = bias_ref[at : at + width, :]
        at += width
        scores = scores * (scale * LOG2_E) + jnp.concatenate([bias] * GROUP_SHARE, axis=1)
        largest = jnp.max(scores, axis=0, keepdims=True)
        numerator = jnp.exp2(scores - largest)
        weights = numerator * (1.0 / jnp.sum(numerator, axis=0, keepdims=True))
        rounded = weights.astype(jnp.bfloat16)
        delta = jnp.sum(rounded.astype(jnp.float32) * grad_weights, axis=0, keepdims=True)
        grad_scores = (weights * (grad_weights - delta)).astype(jnp.bfloat16)
        value_terms = mxu(rounded, grad, NN)
        key_terms = mxu(grad_scores, query, NN)
        for block in range(low // BLOCK, high // BLOCK):
            part = slice(block * BLOCK - low, (block + 1) * BLOCK - low)
            for total, terms in ((grad_value, value_terms), (grad_key, key_terms)):
                total[block] = (
                    terms[part] if total[block] is None else total[block] + terms[part]
                )
        grad_query = (mxu(key_t[:, low:high], grad_scores, NN) * scale).astype(jnp.bfloat16)
        for h, head in enumerate(heads):
            gq_ref[head, rows] = grad_query[:, h * BLOCK : (h + 1) * BLOCK]
    for block in range(row_count // BLOCK):
        rows = slice(block * BLOCK, (block + 1) * BLOCK)
        gk_ref[rows, :] = (grad_key[block] * scale).astype(jnp.bfloat16)
        gv_ref[rows, :] = grad_value[block].astype(jnp.bfloat16)


def attention_backward(queries, keys, values, output_gradient, lengths):
    row_count = queries.shape[0]
    wide = GROUP_SHARE * HEAD_SIZE
    pair_rows = sum(high - low for _, low, high in query_spans(row_count))
    by_columns = lambda width: pl.BlockSpec((row_count, width), lambda j: (0, j))
    return pl.pallas_call(
        attention_kernel,
        grid=(keys.shape[1] // HEAD_SIZE,),
        in_specs=[
            pl.BlockSpec(memory_space=pltpu.SMEM),
            by_columns(wide),
            by_columns(wide),
            by_columns(HEAD_SIZE),
            by_columns(HEAD_SIZE),
        ],
        out_specs=[
            pl.BlockSpec((wide, row_count), lambda j: (j, 0)),
            by_columns(HEAD_SIZE),
            by_columns(HEAD_SIZE),
        ],
        out_shape=[
            jax.ShapeDtypeStruct((queries.shape[1], row_count), jnp.bfloat16),
            jax.ShapeDtypeStruct(keys.shape, jnp.bfloat16),
            jax.ShapeDtypeStruct(values.shape, jnp.bfloat16),
        ],
        scratch_shapes=[pltpu.VMEM((pair_rows, BLOCK), jnp.float32)],
        compiler_params=pltpu.CompilerParams(vmem_limit_bytes=VMEM_BYTES),
        cost_estimate=pl.CostEstimate(
            flops=16 * 10**9, bytes_accessed=8 * 2**20, transcendentals=0
        ),
        name="attention_backward",
    )(lengths, queries, output_gradient, keys, values)


def slot_masks(len_ref, adapter_ref, slot_ref, row_count, slots):
    token = lax.broadcasted_iota(jnp.int32, (1, row_count), 1)
    adapter = jnp.full((1, row_count), adapter_ref[0, 0], jnp.int32)
    end = jnp.int32(0)
    for index in range(len_ref.shape[1] - 1):
        end = end + len_ref[0, index]
        adapter = jnp.where(token >= end, adapter_ref[0, index + 1], adapter)
    return [adapter == slot_ref[slot] for slot in slots]


def peer_slots(me, peers, local_slots, sign):
    return [
        lax.rem(me + sign * shift + peers, peers) * local_slots + own
        for shift in range(peers)
        for own in range(local_slots)
    ]


def select(wide, masks, rank):
    total = None
    for index, mask in enumerate(masks):
        part = jnp.where(mask, wide[index * rank : (index + 1) * rank], 0.0)
        total = part if total is None else total + part
    return total


def low_kernel(peers, local_slots, len_ref, adapter_ref, slot_ref, me_ref, x_ref, gq_ref, *refs):
    factors, out_ref = refs[:peers], refs[peers]
    rank = factors[0].shape[0] // (2 * local_slots)
    share = rank * local_slots
    row_count = x_ref.shape[0]
    masks = slot_masks(
        len_ref, adapter_ref, slot_ref, row_count, peer_slots(me_ref[0], peers, local_slots, -1)
    )
    down = jnp.concatenate([ref[:share] for ref in factors], axis=0)
    up = jnp.concatenate([ref[share:] for ref in factors], axis=0)
    out_ref[:rank] = select(mxu(down, x_ref[...], NT), masks, rank)
    out_ref[rank:] = select(mxu(up, gq_ref[...], NN), masks, rank)


def spread(low, masks):
    zero = jnp.zeros_like(low)
    return jnp.concatenate([jnp.where(mask, low, zero) for mask in masks], axis=0).astype(
        jnp.bfloat16
    )


def product_kernel(peers, local_slots, parts, len_ref, adapter_ref, slot_ref, me_ref, *refs):
    lows, (x_ref, gq_ref), outs = refs[:parts], refs[parts : parts + 2], refs[parts + 2 :]
    low = lows[0][...]
    for ref in lows[1:]:
        low = low + ref[...]
    rank = low.shape[0] // 2
    share = rank * local_slots
    low = low.astype(jnp.bfloat16).astype(jnp.float32)
    masks = slot_masks(
        len_ref,
        adapter_ref,
        slot_ref,
        x_ref.shape[0],
        peer_slots(me_ref[0], peers, local_slots, 1),
    )
    wide_in, wide_grad = spread(low[:rank], masks), spread(low[rank:], masks)
    down = mxu(wide_grad, x_ref[...], NN) * ADAPTER_SCALE
    up = mxu(wide_in, gq_ref[...], NT) * ADAPTER_SCALE
    for shift, ref in enumerate(outs[:peers]):
        rows = slice(shift * share, (shift + 1) * share)
        ref[:share] = down[rows].astype(ref.dtype)
        ref[share:] = up[rows].astype(ref.dtype)
    outs[peers][...] = low[rank:].astype(jnp.bfloat16)


def input_kernel(peers, local_slots, len_ref, adapter_ref, slot_ref, me_ref, low_ref, *refs):
    factors, out_ref = refs[:peers], refs[peers]
    rank = low_ref.shape[0]
    masks = slot_masks(
        len_ref,
        adapter_ref,
        slot_ref,
        low_ref.shape[1],
        peer_slots(me_ref[0], peers, local_slots, -1),
    )
    wide = spread(low_ref[...].astype(jnp.float32), masks)
    down = jnp.concatenate([ref[: rank * local_slots] for ref in factors], axis=0)
    out_ref[...] = (mxu(wide, down, TN) * ADAPTER_SCALE).astype(jnp.bfloat16)


def call(kernel, scalars, arrays, out_shape, flops, name):
    return pl.pallas_call(
        kernel,
        in_specs=[pl.BlockSpec(memory_space=pltpu.SMEM)] * len(scalars)
        + [pl.BlockSpec(memory_space=pltpu.VMEM)] * len(arrays),
        out_specs=jax.tree.map(lambda _: pl.BlockSpec(memory_space=pltpu.VMEM), out_shape),
        out_shape=out_shape,
        compiler_params=pltpu.CompilerParams(vmem_limit_bytes=VMEM_BYTES),
        cost_estimate=pl.CostEstimate(flops=flops, bytes_accessed=4 * 2**20, transcendentals=0),
        name=name,
    )(*scalars, *arrays)


def send(array, axis, shift):
    size = lax.axis_size(axis)
    return lax.ppermute(array, axis, [(i, (i + shift) % size) for i in range(size)])


def local(
    normed_input,
    rotated_queries,
    rotated_keys,
    value_rows,
    output_gradient,
    document_length,
    document_adapter,
    adapter_in_slot,
    down_weight,
    up_weight,
):
    row_count, width = normed_input.shape
    local_slots, rank, _ = down_weight.shape
    share = local_slots * rank
    peers, parts = lax.axis_size("dp"), lax.axis_size("tensor")
    me = lax.axis_index("dp").astype(jnp.int32).reshape(1)
    scalars = (document_length, document_adapter, adapter_in_slot, me)
    own = jnp.concatenate(
        [down_weight.reshape(share, width), up_weight.reshape(share, width)], axis=0
    )
    factors = [own] + [send(own, "dp", shift) for shift in range(1, peers)]
    query_gradient, key_gradient, value_gradient = attention_backward(
        rotated_queries, rotated_keys, value_rows, output_gradient, document_length
    )
    low = call(
        functools.partial(low_kernel, peers, local_slots),
        scalars,
        (normed_input, query_gradient, *factors),
        jax.ShapeDtypeStruct((2 * rank, row_count), jnp.float32),
        10**9,
        "low",
    )
    lows = [low] + [send(low, "tensor", shift) for shift in range(1, parts)]
    *terms, low_grads = call(
        functools.partial(product_kernel, peers, local_slots, parts),
        scalars,
        (*lows, normed_input, query_gradient),
        [
            jax.ShapeDtypeStruct((2 * share, width), jnp.float32 if shift == 0 else jnp.bfloat16)
            for shift in range(peers)
        ]
        + [jax.ShapeDtypeStruct((rank, row_count), jnp.bfloat16)],
        10**9,
        "product",
    )
    received = [send(terms[shift], "dp", shift) for shift in range(1, peers)]
    input_gradient = call(
        functools.partial(input_kernel, peers, local_slots),
        scalars,
        (low_grads, *factors),
        jax.ShapeDtypeStruct((row_count, width), jnp.bfloat16),
        10**9,
        "input_gradient",
    )
    total = terms[0]
    for part in received:
        total = total + part.astype(jnp.float32)
    down_gradient = total[:share].reshape(local_slots, rank, width)
    up_gradient = total[share:].reshape(local_slots, rank, width)
    return (input_gradient, key_gradient, value_gradient, down_gradient, up_gradient)


def solution(mesh):
    return jax.shard_map(
        local,
        mesh=mesh,
        in_specs=(
            P(("groups", "dp"), "tensor"),
            P(("groups", "dp"), "tensor"),
            P(("groups", "dp"), "tensor"),
            P(("groups", "dp"), "tensor"),
            P(("groups", "dp"), "tensor"),
            P(("groups", "dp"), None),
            P(("groups", "dp"), None),
            P(),
            P(("groups", "dp"), None, "tensor"),
            P(("groups", "dp"), None, "tensor"),
        ),
        out_specs=(
            P(("groups", "dp"), "tensor"),
            P(("groups", "dp"), "tensor"),
            P(("groups", "dp"), "tensor"),
            P(("groups", "dp"), None, "tensor"),
            P(("groups", "dp"), None, "tensor"),
        ),
        check_vma=False,
    )
```

time: 308 us -> 49.2 us (0.16)
  matrix products: 141 us -> 0 us
  blocking collectives: 40.9 us -> 0 us
  loops' own time: 31.6 us -> 0 us
  waiting for transfers between devices: 36.2 us -> 8.41 us
  local copies, waits for them, and re-layouts: 32.1 us -> 9.38 us
  Pallas kernels: 0 us -> 16.4 us
  between operations: 14.2 us -> 0.74 us
  starting transfers between devices: 0.08 us -> 12.9 us
  other arithmetic: 9.7 us -> 0.95 us
    dot_general x101 -> x0, matrix products: 141 us -> none  [the longest x16 31.9 us: head_backward(): lax.dot_general(rounded, grad_head, (((0,), (0,)), ((), ())), preferred_e...]
    reduce_scatter x2 -> x0, waiting for transfers between devices: 36.2 us -> none  [local(): lax.psum_scatter(ADAPTER_SCALE * product.reshape(local_rows * lax.axis_si...]
    another operation x1 -> x0, loops' own time: 31.6 us -> none  [attention_backward(): lax.map(one_head, (query_heads, grad_heads, kv_index))]
    all_gather x2 -> x0, blocking collectives: 30.2 us -> none  [the longest x1 15.6 us: local(): lax.all_gather(up_weight, 'dp', axis=0, tiled=True)]
    pallas_call x0 -> x4, Pallas kernels: none -> 16.4 us  [the longest x1 10.4 us: attention_backward(): pl.pallas_call(attention_kernel, grid=(keys.shape[1] // HEAD_SIZE,), in_s...]
    ppermute x0 -> x9, starting transfers between devices: none -> 12.9 us  [send(): lax.ppermute(array, axis, [(i, (i + shift) % size) for i in range(size)])]
    dynamic_update_slice x32 -> x0, local copies, waits for them, and re-layouts: 12.5 us -> none  [attention_backward(): lax.map(one_head, (query_heads, grad_heads, kv_index))]
    psum x1 -> x0, blocking collectives: 10.7 us -> none  [local(): low_grads = lax.psum(grad_part, 'tensor')]
  transfers between devices with their start and end apart: 2 -> 9, of which waited for: 2 -> 5; matrix products, arithmetic and copies ran while one was open for 3% -> 0% of each run, Pallas kernels for 0% -> 27%
where the time goes in v1:
time: 49.2 us; the launch traced here: 48.7 us
  Pallas kernels  16.4 us (33%)
  starting transfers between devices  12.9 us (26%)
  local copies, waits for them, and re-layouts  9.38 us (19%)
  waiting for transfers between devices  8.41 us (17%)
  other arithmetic  0.95 us (2%)
  between operations  0.74 us (2%)
    ppermute x9, starting transfers between devices, send(): lax.ppermute(array, axis, [(i, (i + shift) % size) for i in range(size)])  12.9 us
    pallas_call x1, Pallas kernels, attention_backward(): pl.pallas_call(attention_kernel, grid=(keys.shape[1] // HEAD_SIZE,), in_s...  10.4 us
    unnamed x22, local copies, waits for them, and re-layouts  8.66 us
    ppermute x9, waiting for transfers between devices, send(): lax.ppermute(array, axis, [(i, (i + shift) % size) for i in range(size)])  8.41 us
    pallas_call x3, Pallas kernels, call(): pl.pallas_call(kernel, in_specs=[pl.BlockSpec(memory_space=pltpu.SMEM)] *...  5.96 us
  transfers between devices with their start and end apart: 9, of which 5 were waited for; matrix products, arithmetic and copies ran while one was open for 0% of the time, Pallas kernels for 27%

profile of v1, /device:TPU:0, one launch (start us, length us, event | category | flops | bytes accessed | tf_op | source)
XLA Modules:
  0.0 48.7 jit_solution(3674566442215848903)
XLA Ops:
  0.7 0.9 %pad_maximum_fusion.refs_0_ = bf16[32,2048]{1,0:T(8,128)(2,1)S(1)} fusion(bf16[16,2048]{1,0:T(8,128)(2,1)} %bitcast.7, bf16[16,2048]{1,0:T(8,128)(2,1)} %bitcast.8), kind=kLoop, calls=%fused_computation.3 | loop fusion | flops 262144 | bytes 262144 | tf_op jit(solution)/shard_map/concatenate | solution.py:255
  1.6 5.1 %collective-permute-start.2 = (bf16[32,2048]{1,0:T(8,128)(2,1)S(1)}, bf16[32,2048]{1,0:T(8,128)(2,1)S(1)}, u32[]{:S(2)}, u32[]{:S(2)}) collective-permute-start(bf16[32,2048]{1,0:T(8,128)(2,1)S(1)} %pad_maximum_fusion.refs_0_), channel_id=1, source_target_pairs={{0,12},{4,0},{8,4},{12,8},{1,13},{5,1},{9,5},{13,9},{2,14},{6,2},{... | collective-permute-start | bytes 393224 | tf_op jit(solution)/shard_map/ppermute | solution.py:234
  6.7 1.0 %collective-permute-start = (bf16[32,2048]{1,0:T(8,128)(2,1)S(1)}, bf16[32,2048]{1,0:T(8,128)(2,1)S(1)}, u32[]{:S(2)}, u32[]{:S(2)}) collective-permute-start(bf16[32,2048]{1,0:T(8,128)(2,1)S(1)} %pad_maximum_fusion.refs_0_), channel_id=1, source_target_pairs={{0,4},{4,8},{8,12},{12,0},{1,5},{5,9},{9,13},{13,1},{2,6},{6,10},{... | collective-permute-start | bytes 393224 | tf_op jit(solution)/shard_map/ppermute | solution.py:234
  7.7 0.7 %copy-done.3 = s32[1,8]{1,0:T(1,128)S(1)} copy-done((s32[1,8]{1,0:T(1,128)S(1)}, s32[1,8]{1,0:T(1,128)}, u32[]{:S(2)}) %copy-start.3) | copy-done | bytes 56
  8.4 1.6 %copy-done.7 = bf16[512,2048]{1,0:T(8,128)(2,1)S(1)} copy-done((bf16[512,2048]{1,0:T(8,128)(2,1)S(1)}, bf16[512,2048]{1,0:T(8,128)(2,1)}, u32[]{:S(2)}) %copy-start.7) | copy-done | bytes 2097176
  9.9 1.6 %copy-done.8 = bf16[512,2048]{1,0:T(8,128)(2,1)S(1)} copy-done((bf16[512,2048]{1,0:T(8,128)(2,1)S(1)}, bf16[512,2048]{1,0:T(8,128)(2,1)}, u32[]{:S(2)}) %copy-start.8) | copy-done | bytes 2097176
  11.5 0.9 %copy-done.9 = bf16[512,256]{1,0:T(8,128)(2,1)S(1)} copy-done((bf16[512,256]{1,0:T(8,128)(2,1)S(1)}, bf16[512,256]{1,0:T(8,128)(2,1)}, u32[]{:S(2)}) %copy-start.9) | copy-done | bytes 262168
  12.5 0.9 %copy-done.10 = bf16[512,256]{1,0:T(8,128)(2,1)S(1)} copy-done((bf16[512,256]{1,0:T(8,128)(2,1)S(1)}, bf16[512,256]{1,0:T(8,128)(2,1)}, u32[]{:S(2)}) %copy-start.10) | copy-done | bytes 262168
  13.4 10.4 %attention_backward.1 = (bf16[2048,512]{1,0:T(8,128)(2,1)S(1)}, bf16[512,256]{1,0:T(8,128)(2,1)}, bf16[512,256]{1,0:T(8,128)(2,1)}) custom-call(s32[1,8]{1,0:T(1,128)S(1)} %copy-done.3, bf16[512,2048]{1,0:T(8,128)(2,1)S(1)} %copy-done.7, bf16[512,2048]{1,0:T(8,128)(2,1)S(1)} %copy-done.8, bf16[512,256]{1,0:T(8,128)(2,1)S(1)} %copy-done.9, ...), custom_call_target="tpu_custom_call" | custom-call | flops 16000000000 | bytes 8388608 | tf_op jit(solution)/shard_map/attention_backward/pallas_call | solution.py:103
  23.8 1.3 %copy-done.1 = bf16[2048,512]{1,0:T(8,128)(2,1)} copy-done((bf16[2048,512]{1,0:T(8,128)(2,1)}, bf16[2048,512]{1,0:T(8,128)(2,1)S(1)}, u32[]{:S(2)}) %copy-start.1) | copy-done | bytes 2097176
  25.2 1.6 %copy-done.2 = bf16[2048,512]{1,0:T(8,128)(2,1)S(1)} copy-done((bf16[2048,512]{1,0:T(8,128)(2,1)S(1)}, bf16[2048,512]{1,0:T(8,128)(2,1)}, u32[]{:S(2)}) %copy-start.2) | copy-done | bytes 2097176
  26.8 1.7 %low.1.refs_0_ = f32[32,512]{1,0:T(8,128)S(1)} custom-call(s32[1,8]{1,0:T(1,128)S(1)} %copy-done.4, s32[1,8]{1,0:T(1,128)S(1)} %copy-done.5, s32[4]{0:T(128)S(1)} %copy-done.6, s32[1]{0:T(128)} %bitcast.me_ref, bf16[512,2048]{1,0:T(8,128)(2,1)S(1)} %copy-done, bf16[2048,512]{1,0:T(8,128)(2,1)S(1)} %copy-done.2, ...), custom_call_target="tpu_custom_call" | custom-call | flops 1000000000 | bytes 4194304 | tf_op jit(solution)/shard_map/low/pallas_call | solution.py:220
  28.6 1.5 %collective-permute-start.4 = (f32[32,512]{1,0:T(8,128)S(1)}, f32[32,512]{1,0:T(8,128)S(1)}, u32[]{:S(2)}, u32[]{:S(2)}) collective-permute-start(f32[32,512]{1,0:T(8,128)S(1)} %low.1.refs_0_), channel_id=1, source_target_pairs={{0,2},{1,3},{2,0},{3,1},{4,6},{5,7},{6,4},{7,5},{8,10},{9,11},{10,... | collective-permute-start | bytes 196616 | tf_op jit(solution)/shard_map/ppermute | solution.py:234
  30.3 0.3 collective-permute-done.5.refs_3_
  30.5 3.7 %collective-permute-done.4.refs_2_ = f32[32,512]{1,0:T(8,128)S(1)} collective-permute-done((f32[32,512]{1,0:T(8,128)S(1)}, f32[32,512]{1,0:T(8,128)S(1)}, u32[]{:S(2)}, u32[]{:S(2)}) %collective-permute-start.4) | collective-permute-done | bytes 65568 | tf_op jit(solution)/shard_map/ppermute | solution.py:234
  34.2 0.2 collective-permute-done.3.refs_1_
  34.4 1.7 %product.1 = (f32[32,2048]{1,0:T(8,128)S(1)}, bf16[32,2048]{1,0:T(8,128)(2,1)S(1)}, bf16[32,2048]{1,0:T(8,128)(2,1)S(1)}, bf16[32,2048]{1,0:T(8,128)(2,1)S(1)}, bf16[16,512]{1,0:T(8,128)(2,1)S(1)}) custom-call(s32[1,8]{1,0:T(1,128)S(1)} %copy-done.4, s32[1,8]{1,0:T(1,128)S(1)} %copy-done.5, s32[4]{0:T(128)S(1)} %copy-done.6, s32[1]{0:T(128)} %bitcast.me_ref, ...), custom_call_target="tpu_custom_call" | custom-call | flops 1000000000 | bytes 4194304 | tf_op jit(solution)/shard_map/product/pallas_call | solution.py:220
  36.0 2.5 %collective-permute-start.6 = (bf16[32,2048]{1,0:T(8,128)(2,1)S(1)}, bf16[32,2048]{1,0:T(8,128)(2,1)S(1)}, u32[]{:S(2)}, u32[]{:S(2)}) collective-permute-start(bf16[32,2048]{1,0:T(8,128)(2,1)S(1)} %get-tuple-element.18), channel_id=1, source_target_pairs={{0,4},{4,8},{8,12},{12,0},{1,5},{5,9},{9,13},{13,1},{2,6},{6,10},{... | collective-permute-start | bytes 393224 | tf_op jit(solution)/shard_map/ppermute | solution.py:234
  38.6 0.9 %collective-permute-start.7 = (bf16[32,2048]{1,0:T(8,128)(2,1)S(1)}, bf16[32,2048]{1,0:T(8,128)(2,1)S(1)}, u32[]{:S(2)}, u32[]{:S(2)}) collective-permute-start(bf16[32,2048]{1,0:T(8,128)(2,1)S(1)} %get-tuple-element.19), channel_id=1, source_target_pairs={{0,8},{4,12},{8,0},{12,4},{1,9},{5,13},{9,1},{13,5},{2,10},{6,14},... | collective-permute-start | bytes 393224 | tf_op jit(solution)/shard_map/ppermute | solution.py:234
  39.5 1.5 %collective-permute-start.8 = (bf16[32,2048]{1,0:T(8,128)(2,1)S(1)}, bf16[32,2048]{1,0:T(8,128)(2,1)S(1)}, u32[]{:S(2)}, u32[]{:S(2)}) collective-permute-start(bf16[32,2048]{1,0:T(8,128)(2,1)S(1)} %get-tuple-element.20), channel_id=1, source_target_pairs={{0,12},{4,0},{8,4},{12,8},{1,13},{5,1},{9,5},{13,9},{2,14},{6,2},{... | collective-permute-start | bytes 393224 | tf_op jit(solution)/shard_map/ppermute | solution.py:234
  41.0 2.6 %input_gradient.1 = bf16[512,2048]{1,0:T(8,128)(2,1)} custom-call(s32[1,8]{1,0:T(1,128)S(1)} %copy-done.4, s32[1,8]{1,0:T(1,128)S(1)} %copy-done.5, s32[4]{0:T(128)S(1)} %copy-done.6, s32[1]{0:T(128)} %bitcast.me_ref, bf16[16,512]{1,0:T(8,128)(2,1)S(1)} %get-tuple-element.14.low_ref, bf16[32,2048]{1,0:T(8,128)(2,1)S(1)} %pad_maximum_fusion.refs_0_, ...), custom_call_target="tpu_custom_call" | custom-call | flops 1000000000 | bytes 4194304 | tf_op jit(solution)/shard_map/input_gradient/pallas_call | solution.py:220
  43.6 0.8 %collective-permute-done.6 = bf16[32,2048]{1,0:T(8,128)(2,1)S(1)} collective-permute-done((bf16[32,2048]{1,0:T(8,128)(2,1)S(1)}, bf16[32,2048]{1,0:T(8,128)(2,1)S(1)}, u32[]{:S(2)}, u32[]{:S(2)}) %collective-permute-start.6) | collective-permute-done | bytes 131104 | tf_op jit(solution)/shard_map/ppermute | solution.py:234
  44.4 3.5 %collective-permute-done.7 = bf16[32,2048]{1,0:T(8,128)(2,1)S(1)} collective-permute-done((bf16[32,2048]{1,0:T(8,128)(2,1)S(1)}, bf16[32,2048]{1,0:T(8,128)(2,1)S(1)}, u32[]{:S(2)}, u32[]{:S(2)}) %collective-permute-start.7) | collective-permute-done | bytes 131104 | tf_op jit(solution)/shard_map/ppermute | solution.py:234
  48.0 0.7 %slice_bitcast_fusion = (f32[1,16,2048]{2,1,0:T(8,128)}, f32[1,16,2048]{2,1,0:T(8,128)}) fusion(f32[32,2048]{1,0:T(8,128)S(1)} %convert_add_fusion), kind=kLoop, calls=%fused_computation.1 | loop fusion | bytes 524288 | tf_op jit(solution)/shard_map/reshape | solution.py:296
  (23 shorter events, 0.4 us)
Async XLA Ops:
  0.6 24.5 %copy-start.4 = (s32[1,8]{1,0:T(1,128)S(1)}, s32[1,8]{1,0:T(1,128)}, u32[]{:S(2)}) copy-start(s32[1,8]{1,0:T(1,128)} %len_ref.7) | copy-start | bytes 100
  0.6 24.5 %copy-start.5 = (s32[1,8]{1,0:T(1,128)S(1)}, s32[1,8]{1,0:T(1,128)}, u32[]{:S(2)}) copy-start(s32[1,8]{1,0:T(1,128)} %adapter_ref.5) | copy-start | bytes 100
  0.7 24.5 %copy-start.6 = (s32[4]{0:T(128)S(1)}, s32[4]{0:T(128)}, u32[]{:S(2)}) copy-start(s32[4]{0:T(128)} %slot_ref.5) | copy-start | bytes 52
  1.6 23.6 %copy-start = (bf16[512,2048]{1,0:T(8,128)(2,1)S(1)}, bf16[512,2048]{1,0:T(8,128)(2,1)}, u32[]{:S(2)}) copy-start(bf16[512,2048]{1,0:T(8,128)(2,1)} %refs_4_.1) | copy-start | bytes 6291460
  1.6 23.6 %collective-permute-start.2 = (bf16[32,2048]{1,0:T(8,128)(2,1)S(1)}, bf16[32,2048]{1,0:T(8,128)(2,1)S(1)}, u32[]{:S(2)}, u32[]{:S(2)}) collective-permute-start(bf16[32,2048]{1,0:T(8,128)(2,1)S(1)} %pad_maximum_fusion.refs_0_), channel_id=1, source_target_pairs={{0,12},{4,0},{8,4},{12,8},{1,13},{5,1},{9,5},{13,9},{2,14},{6,2},{... | collective-permute-start | bytes 393224 | tf_op jit(solution)/shard_map/ppermute | solution.py:234
  6.7 18.5 %collective-permute-start.1 = (bf16[32,2048]{1,0:T(8,128)(2,1)S(1)}, bf16[32,2048]{1,0:T(8,128)(2,1)S(1)}, u32[]{:S(2)}, u32[]{:S(2)}) collective-permute-start(bf16[32,2048]{1,0:T(8,128)(2,1)S(1)} %pad_maximum_fusion.refs_0_), channel_id=1, source_target_pairs={{0,8},{4,12},{8,0},{12,4},{1,9},{5,13},{9,1},{13,5},{2,10},{6,14},... | collective-permute-start | bytes 393224 | tf_op jit(solution)/shard_map/ppermute | solution.py:234
  6.7 18.5 %collective-permute-start = (bf16[32,2048]{1,0:T(8,128)(2,1)S(1)}, bf16[32,2048]{1,0:T(8,128)(2,1)S(1)}, u32[]{:S(2)}, u32[]{:S(2)}) collective-permute-start(bf16[32,2048]{1,0:T(8,128)(2,1)S(1)} %pad_maximum_fusion.refs_0_), channel_id=1, source_target_pairs={{0,4},{4,8},{8,12},{12,0},{1,5},{5,9},{9,13},{13,1},{2,6},{6,10},{... | collective-permute-start | bytes 393224 | tf_op jit(solution)/shard_map/ppermute | solution.py:234
  7.7 0.7 %copy-start.3 = (s32[1,8]{1,0:T(1,128)S(1)}, s32[1,8]{1,0:T(1,128)}, u32[]{:S(2)}) copy-start(s32[1,8]{1,0:T(1,128)} %len_ref.7) | copy-start | bytes 100
  8.3 1.6 %copy-start.7 = (bf16[512,2048]{1,0:T(8,128)(2,1)S(1)}, bf16[512,2048]{1,0:T(8,128)(2,1)}, u32[]{:S(2)}) copy-start(bf16[512,2048]{1,0:T(8,128)(2,1)} %q_ref.1) | copy-start | bytes 6291460
  9.9 1.6 %copy-start.8 = (bf16[512,2048]{1,0:T(8,128)(2,1)S(1)}, bf16[512,2048]{1,0:T(8,128)(2,1)}, u32[]{:S(2)}) copy-start(bf16[512,2048]{1,0:T(8,128)(2,1)} %g_ref.1) | copy-start | bytes 6291460
  11.5 0.9 %copy-start.9 = (bf16[512,256]{1,0:T(8,128)(2,1)S(1)}, bf16[512,256]{1,0:T(8,128)(2,1)}, u32[]{:S(2)}) copy-start(bf16[512,256]{1,0:T(8,128)(2,1)} %k_ref.1) | copy-start | bytes 786436
  12.5 0.9 %copy-start.10 = (bf16[512,256]{1,0:T(8,128)(2,1)S(1)}, bf16[512,256]{1,0:T(8,128)(2,1)}, u32[]{:S(2)}) copy-start(bf16[512,256]{1,0:T(8,128)(2,1)} %v_ref.1) | copy-start | bytes 786436
  23.8 1.3 %copy-start.1 = (bf16[2048,512]{1,0:T(8,128)(2,1)}, bf16[2048,512]{1,0:T(8,128)(2,1)S(1)}, u32[]{:S(2)}) copy-start(bf16[2048,512]{1,0:T(8,128)(2,1)S(1)} %get-tuple-element.13.gq_ref.refs_5_) | copy-start | bytes 6291460
  25.2 1.6 %copy-start.2 = (bf16[2048,512]{1,0:T(8,128)(2,1)S(1)}, bf16[2048,512]{1,0:T(8,128)(2,1)}, u32[]{:S(2)}) copy-start(bf16[2048,512]{1,0:T(8,128)(2,1)} %copy-done.1) | copy-start | bytes 6291460
  28.5 2.0 %collective-permute-start.5 = (f32[32,512]{1,0:T(8,128)S(1)}, f32[32,512]{1,0:T(8,128)S(1)}, u32[]{:S(2)}, u32[]{:S(2)}) collective-permute-start(f32[32,512]{1,0:T(8,128)S(1)} %low.1.refs_0_), channel_id=1, source_target_pairs={{0,3},{1,0},{2,1},{3,2},{4,7},{5,4},{6,5},{7,6},{8,11},{9,8},{10,9... | collective-permute-start | bytes 196616 | tf_op jit(solution)/shard_map/ppermute | solution.py:234
  28.6 5.6 %collective-permute-start.4 = (f32[32,512]{1,0:T(8,128)S(1)}, f32[32,512]{1,0:T(8,128)S(1)}, u32[]{:S(2)}, u32[]{:S(2)}) collective-permute-start(f32[32,512]{1,0:T(8,128)S(1)} %low.1.refs_0_), channel_id=1, source_target_pairs={{0,2},{1,3},{2,0},{3,1},{4,6},{5,7},{6,4},{7,5},{8,10},{9,11},{10,... | collective-permute-start | bytes 196616 | tf_op jit(solution)/shard_map/ppermute | solution.py:234
  30.1 4.3 %collective-permute-start.3 = (f32[32,512]{1,0:T(8,128)S(1)}, f32[32,512]{1,0:T(8,128)S(1)}, u32[]{:S(2)}, u32[]{:S(2)}) collective-permute-start(f32[32,512]{1,0:T(8,128)S(1)} %low.1.refs_0_), channel_id=1, source_target_pairs={{0,1},{1,2},{2,3},{3,0},{4,5},{5,6},{6,7},{7,4},{8,9},{9,10},{10,1... | collective-permute-start | bytes 196616 | tf_op jit(solution)/shard_map/ppermute | solution.py:234
  36.0 8.4 %collective-permute-start.6 = (bf16[32,2048]{1,0:T(8,128)(2,1)S(1)}, bf16[32,2048]{1,0:T(8,128)(2,1)S(1)}, u32[]{:S(2)}, u32[]{:S(2)}) collective-permute-start(bf16[32,2048]{1,0:T(8,128)(2,1)S(1)} %get-tuple-element.18), channel_id=1, source_target_pairs={{0,4},{4,8},{8,12},{12,0},{1,5},{5,9},{9,13},{13,1},{2,6},{6,10},{... | collective-permute-start | bytes 393224 | tf_op jit(solution)/shard_map/ppermute | solution.py:234
  38.6 9.3 %collective-permute-start.7 = (bf16[32,2048]{1,0:T(8,128)(2,1)S(1)}, bf16[32,2048]{1,0:T(8,128)(2,1)S(1)}, u32[]{:S(2)}, u32[]{:S(2)}) collective-permute-start(bf16[32,2048]{1,0:T(8,128)(2,1)S(1)} %get-tuple-element.19), channel_id=1, source_target_pairs={{0,8},{4,12},{8,0},{12,4},{1,9},{5,13},{9,1},{13,5},{2,10},{6,14},... | collective-permute-start | bytes 393224 | tf_op jit(solution)/shard_map/ppermute | solution.py:234
  39.5 8.4 %collective-permute-start.8 = (bf16[32,2048]{1,0:T(8,128)(2,1)S(1)}, bf16[32,2048]{1,0:T(8,128)(2,1)S(1)}, u32[]{:S(2)}, u32[]{:S(2)}) collective-permute-start(bf16[32,2048]{1,0:T(8,128)(2,1)S(1)} %get-tuple-element.20), channel_id=1, source_target_pairs={{0,12},{4,0},{8,4},{12,8},{1,13},{5,1},{9,5},{13,9},{2,14},{6,2},{... | collective-permute-start | bytes 393224 | tf_op jit(solution)/shard_map/ppermute | solution.py:234

commit v2 on v1

--- a/solution.py
+++ b/solution.py
@@ -18,7 +18,8 @@
 MASKED = -1e30
 ADAPTER_SCALE = 2.0
 LOG2_E = 1.4426950408889634
-VMEM_BYTES = 40 * 1024 * 1024
+ATTENTION_VMEM = 24 * 1024 * 1024
+VMEM_BYTES = 16 * 1024 * 1024
 
 NN = (((1,), (0,)), ((), ()))
 NT = (((1,), (1,)), ((), ()))
@@ -37,96 +38,158 @@
 
 
 def attention_kernel(
-    len_ref, q_ref, g_ref, k_ref, v_ref, gq_ref, gk_ref, gv_ref, bias_ref
+    len_ref,
+    q_hbm,
+    g_hbm,
+    k_hbm,
+    v_hbm,
+    gq_ref,
+    gk_ref,
+    gv_ref,
+    bias_ref,
+    q_ref,
+    g_ref,
+    k_ref,
+    v_ref,
+    row_sem,
+    group_sem,
 ):
-    row_count = q_ref.shape[0]
+    row_count = q_hbm.shape[0]
+    groups = k_hbm.shape[1] // HEAD_SIZE
+    wide = GROUP_SHARE * HEAD_SIZE
     scale = 1.0 / math.sqrt(HEAD_SIZE)
-
-    @pl.when(pl.program_id(0) == 0)
-    def _():
+    spans = query_spans(row_count)
+
+    def group_copy(which, group):
+        source, target = ((k_hbm, k_ref), (v_hbm, v_ref))[which]
+        columns = pl.ds(group * HEAD_SIZE, HEAD_SIZE)
+        return pltpu.make_async_copy(
+            source.at[:, columns], target.at[group], group_sem.at[which, group]
+        )
+
+    def row_copy(which, group, block):
+        source, target = ((q_hbm, q_ref), (g_hbm, g_ref))[which]
+        rows = pl.ds(block * BLOCK, BLOCK)
+        return pltpu.make_async_copy(
+            source.at[rows, pl.ds(group * wide, wide)],
+            target.at[group, rows],
+            row_sem.at[which, group, block],
+        )
+
+    for group in range(groups):
+        group_copy(0, group).start()
+        group_copy(1, group).start()
+        for block in range(len(spans)):
+            row_copy(0, group, block).start()
+            row_copy(1, group, block).start()
+
+    at = 0
+    for first, low, high in spans:
+        width = high - low
+        query = lax.broadcasted_iota(jnp.int32, (1, BLOCK), 1) + first
+        start = jnp.zeros((1, BLOCK), jnp.int32)
+        end = jnp.int32(0)
+        for index in range(len_ref.shape[1] - 1):
+            end = end + len_ref[0, index]
+            start = jnp.where(query >= end, end, start)
+        key = lax.broadcasted_iota(jnp.int32, (width, BLOCK), 0) + low
+        bias_ref[at : at + width, :] = jnp.where((key >= start) & (key <= query), 0.0, MASKED)
+        at += width
+
+    heads = [slice(h * HEAD_SIZE, (h + 1) * HEAD_SIZE) for h in range(GROUP_SHARE)]
+
+    def one_group(group):
+        group_copy(0, group).wait()
+        group_copy(1, group).wait()
+        key_t = k_ref[group].T
+        grad_key = [None] * len(spans)
+        grad_value = [None] * len(spans)
         at = 0
-        for first, low, high in query_spans(row_count):
+        for block, (first, low, high) in enumerate(spans):
             width = high - low
-            query = lax.broadcasted_iota(jnp.int32, (1, BLOCK), 1) + first
-            start = jnp.zeros((1, BLOCK), jnp.int32)
-            end = jnp.int32(0)
-            for index in range(len_ref.shape[1] - 1):
-                end = end + len_ref[0, index]
-                start = jnp.where(query >= end, end, start)
-            key = lax.broadcasted_iota(jnp.int32, (width, BLOCK), 0) + low
-            bias_ref[at : at + width, :] = jnp.where((key >= start) & (key <= query), 0.0, MASKED)
+            rows = slice(first, first + BLOCK)
+            row_copy(0, group, block).wait()
+            row_copy(1, group, block).wait()
+            query = jnp.concatenate([q_ref[group, rows, head] for head in heads], axis=0)
+            grad = jnp.concatenate([g_ref[group, rows, head] for head in heads], axis=0)
+            all_scores = mxu(k_ref[group, low:high, :], query, NT)
+            all_grad_weights = mxu(v_ref[group, low:high, :], grad, NT)
+            bias = bias_ref[at : at + width, :]
             at += width
-
-    heads = [slice(h * HEAD_SIZE, (h + 1) * HEAD_SIZE) for h in range(GROUP_SHARE)]
-    key_t = k_ref[...].T
-    grad_key = [None] * (row_count // BLOCK)
-    grad_value = [None] * (row_count // BLOCK)
-    at = 0
-    for first, low, high in query_spans(row_count):
-        width = high - low
-        rows = slice(first, first + BLOCK)
-        query = jnp.concatenate([q_ref[rows, head] for head in heads], axis=0)
-        grad = jnp.concatenate([g_ref[rows, head] for head in heads], axis=0)
-        scores = mxu(k_ref[low:high, :], query, NT)
-        grad_weights = mxu(v_ref[low:high, :], grad, NT)
-        bias = bias_ref[at : at + width, :]
-        at += width
-        scores = scores * (scale * LOG2_E) + jnp.concatenate([bias] * GROUP_SHARE, axis=1)
-        largest = jnp.max(scores, axis=0, keepdims=True)
-        numerator = jnp.exp2(scores - largest)
-        weights = numerator * (1.0 / jnp.sum(numerator, axis=0, keepdims=True))
-        rounded = weights.astype(jnp.bfloat16)
-        delta = jnp.sum(rounded.astype(jnp.float32) * grad_weights, axis=0, keepdims=True)
-        grad_scores = (weights * (grad_weights - delta)).astype(jnp.bfloat16)
-        value_terms = mxu(rounded, grad, NN)
-        key_terms = mxu(grad_scores, query, NN)
-        for block in range(low // BLOCK, high // BLOCK):
-            part = slice(block * BLOCK - low, (block + 1) * BLOCK - low)
-            for total, terms in ((grad_value, value_terms), (grad_key, key_terms)):
-                total[block] = (
-                    terms[part] if total[block] is None else total[block] + terms[part]
+            rounded, grad_scores = [], []
+            for h in range(GROUP_SHARE):
+                part = slice(h * BLOCK, (h + 1) * BLOCK)
+                scores = all_scores[:, part] * (scale * LOG2_E) + bias
+                grad_weights = all_grad_weights[:, part]
+                largest = jnp.max(scores, axis=0, keepdims=True)
+                numerator = jnp.exp2(scores - largest)
+                weights = numerator * (1.0 / jnp.sum(numerator, axis=0, keepdims=True))
+                rounded.append(weights.astype(jnp.bfloat16))
+                delta = jnp.sum(
+                    rounded[-1].astype(jnp.float32) * grad_weights, axis=0, keepdims=True
                 )
-        grad_query = (mxu(key_t[:, low:high], grad_scores, NN) * scale).astype(jnp.bfloat16)
-        for h, head in enumerate(heads):
-            gq_ref[head, rows] = grad_query[:, h * BLOCK : (h + 1) * BLOCK]
-    for block in range(row_count // BLOCK):
-        rows = slice(block * BLOCK, (block + 1) * BLOCK)
-        gk_ref[rows, :] = (grad_key[block] * scale).astype(jnp.bfloat16)
-        gv_ref[rows, :] = grad_value[block].astype(jnp.bfloat16)
+                grad_scores.append((weights * (grad_weights - delta)).astype(jnp.bfloat16))
+            rounded = jnp.concatenate(rounded, axis=1)
+            grad_scores = jnp.concatenate(grad_scores, axis=1)
+            value_terms = mxu(rounded, grad, NN)
+            key_terms = mxu(grad_scores, query, NN)
+            for index in range(low // BLOCK, high // BLOCK):
+                part = slice(index * BLOCK - low, (index + 1) * BLOCK - low)
+                for total, terms in ((grad_value, value_terms), (grad_key, key_terms)):
+                    total[index] = (
+                        terms[part] if total[index] is None else total[index] + terms[part]
+                    )
+            grad_query = (mxu(key_t[:, low:high], grad_scores, NN) * scale).astype(jnp.bfloat16)
+            for h in range(GROUP_SHARE):
+                gq_ref[pl.ds(group * wide + h * HEAD_SIZE, HEAD_SIZE), rows] = grad_query[
+                    :, h * BLOCK : (h + 1) * BLOCK
+                ]
+        columns = pl.ds(group * HEAD_SIZE, HEAD_SIZE)
+        for index in range(len(spans)):
+            rows = slice(index * BLOCK, (index + 1) * BLOCK)
+            gk_ref[rows, columns] = (grad_key[index] * scale).astype(jnp.bfloat16)
+            gv_ref[rows, columns] = grad_value[index].astype(jnp.bfloat16)
+
+    for group in range(groups):
+        one_group(group)
 
 
 def attention_backward(queries, keys, values, output_gradient, lengths):
     row_count = queries.shape[0]
-    wide = GROUP_SHARE * HEAD_SIZE
+    groups = keys.shape[1] // HEAD_SIZE
+    blocks = row_count // BLOCK
     pair_rows = sum(high - low for _, low, high in query_spans(row_count))
-    by_columns = lambda width: pl.BlockSpec((row_count, width), lambda j: (0, j))
+    wide = (groups, row_count, GROUP_SHARE * HEAD_SIZE)
+    narrow = (groups, row_count, HEAD_SIZE)
+    arrays = [
+        pltpu.with_memory_space_constraint(array, pltpu.HBM)
+        for array in (lengths, queries, output_gradient, keys, values)
+    ]
     return pl.pallas_call(
         attention_kernel,
-        grid=(keys.shape[1] // HEAD_SIZE,),
-        in_specs=[
-            pl.BlockSpec(memory_space=pltpu.SMEM),
-            by_columns(wide),
-            by_columns(wide),
-            by_columns(HEAD_SIZE),
-            by_columns(HEAD_SIZE),
-        ],
-        out_specs=[
-            pl.BlockSpec((wide, row_count), lambda j: (j, 0)),
-            by_columns(HEAD_SIZE),
-            by_columns(HEAD_SIZE),
-        ],
+        in_specs=[pl.BlockSpec(memory_space=pltpu.SMEM)]
+        + [pl.BlockSpec(memory_space=pltpu.HBM)] * 4,
+        out_specs=[pl.BlockSpec(memory_space=pltpu.VMEM)] * 3,
         out_shape=[
             jax.ShapeDtypeStruct((queries.shape[1], row_count), jnp.bfloat16),
             jax.ShapeDtypeStruct(keys.shape, jnp.bfloat16),
             jax.ShapeDtypeStruct(values.shape, jnp.bfloat16),
         ],
-        scratch_shapes=[pltpu.VMEM((pair_rows, BLOCK), jnp.float32)],
-        compiler_params=pltpu.CompilerParams(vmem_limit_bytes=VMEM_BYTES),
+        scratch_shapes=[
+            pltpu.VMEM((pair_rows, BLOCK), jnp.float32),
+            pltpu.VMEM(wide, jnp.bfloat16),
+            pltpu.VMEM(wide, jnp.bfloat16),
+            pltpu.VMEM(narrow, jnp.bfloat16),
+            pltpu.VMEM(narrow, jnp.bfloat16),
+            pltpu.SemaphoreType.DMA((2, groups, blocks)),
+            pltpu.SemaphoreType.DMA((2, groups)),
+        ],
+        compiler_params=pltpu.CompilerParams(vmem_limit_bytes=ATTENTION_VMEM),
         cost_estimate=pl.CostEstimate(
-            flops=16 * 10**9, bytes_accessed=8 * 2**20, transcendentals=0
+            flops=8 * 10**9, bytes_accessed=8 * 2**20, transcendentals=0
         ),
         name="attention_backward",
-    )(lengths, queries, output_gradient, keys, values)
+    )(*arrays)
 
 
 def slot_masks(len_ref, adapter_ref, slot_ref, row_count, slots):

time: 49.2 us -> 46.9 us (0.953)
  local copies, waits for them, and re-layouts: 9.38 us -> 3.64 us
  Pallas kernels: 16.4 us -> 19.8 us
    unnamed x22 -> x12, local copies, waits for them, and re-layouts: 8.66 us -> 2.92 us
    pallas_call x1, Pallas kernels: 10.4 us -> 13.9 us  [attention_backward(): pl.pallas_call(attention_kernel, in_specs=[pl.BlockSpec(memory_space=pltp...]
  transfers between devices with their start and end apart: 9 -> 9, of which waited for: 5 -> 5; matrix products, arithmetic and copies ran while one was open for 0% -> 0% of each run, Pallas kernels for 27% -> 36%
where the time goes in v2:
time: 46.9 us; the launch traced here: 46.4 us
  Pallas kernels  19.8 us (42%)
  starting transfers between devices  12.9 us (28%)
  waiting for transfers between devices  8.41 us (18%)
  local copies, waits for them, and re-layouts  3.64 us (8%)
  other arithmetic  0.94 us (2%)
  between operations  0.75 us (2%)
    pallas_call x1, Pallas kernels, attention_backward(): pl.pallas_call(attention_kernel, in_specs=[pl.BlockSpec(memory_space=pltp...  13.9 us
    ppermute x9, starting transfers between devices, send(): lax.ppermute(array, axis, [(i, (i + shift) % size) for i in range(size)])  12.9 us
    ppermute x9, waiting for transfers between devices, send(): lax.ppermute(array, axis, [(i, (i + shift) % size) for i in range(size)])  8.41 us
    pallas_call x3, Pallas kernels, call(): pl.pallas_call(kernel, in_specs=[pl.BlockSpec(memory_space=pltpu.SMEM)] *...  5.96 us
    unnamed x12, local copies, waits for them, and re-layouts  2.92 us
  transfers between devices with their start and end apart: 9, of which 5 were waited for; matrix products, arithmetic and copies ran while one was open for 0% of the time, Pallas kernels for 36%

profile of v2, /device:TPU:0, one launch (start us, length us, event | category | flops | bytes accessed | tf_op | source)
XLA Modules:
  0.0 46.4 jit_solution(1445166399327333051)
XLA Ops:
  0.6 0.9 %pad_maximum_fusion.refs_0_ = bf16[32,2048]{1,0:T(8,128)(2,1)S(1)} fusion(bf16[16,2048]{1,0:T(8,128)(2,1)} %bitcast.7, bf16[16,2048]{1,0:T(8,128)(2,1)} %bitcast.8), kind=kLoop, calls=%fused_computation.3 | loop fusion | flops 262144 | bytes 262144 | tf_op jit(solution)/shard_map/concatenate | solution.py:318
  1.5 0.0 copy-start
  1.5 0.0 copy-start.3
  1.6 5.1 %collective-permute-start.2 = (bf16[32,2048]{1,0:T(8,128)(2,1)S(1)}, bf16[32,2048]{1,0:T(8,128)(2,1)S(1)}, u32[]{:S(2)}, u32[]{:S(2)}) collective-permute-start(bf16[32,2048]{1,0:T(8,128)(2,1)S(1)} %pad_maximum_fusion.refs_0_), channel_id=1, source_target_pairs={{0,12},{4,0},{8,4},{12,8},{1,13},{5,1},{9,5},{13,9},{2,14},{6,2},{... | collective-permute-start | bytes 393224 | tf_op jit(solution)/shard_map/ppermute | solution.py:297
  6.7 1.0 %collective-permute-start = (bf16[32,2048]{1,0:T(8,128)(2,1)S(1)}, bf16[32,2048]{1,0:T(8,128)(2,1)S(1)}, u32[]{:S(2)}, u32[]{:S(2)}) collective-permute-start(bf16[32,2048]{1,0:T(8,128)(2,1)S(1)} %pad_maximum_fusion.refs_0_), channel_id=1, source_target_pairs={{0,4},{4,8},{8,12},{12,0},{1,5},{5,9},{9,13},{13,1},{2,6},{6,10},{... | collective-permute-start | bytes 393224 | tf_op jit(solution)/shard_map/ppermute | solution.py:297
  7.7 13.9 %attention_backward.1 = (bf16[2048,512]{1,0:T(8,128)(2,1)S(1)}, bf16[512,256]{1,0:T(8,128)(2,1)}, bf16[512,256]{1,0:T(8,128)(2,1)}) custom-call(s32[1,8]{1,0:T(1,128)} %len_ref.7, bf16[512,2048]{1,0:T(8,128)(2,1)} %q_hbm.1, bf16[512,2048]{1,0:T(8,128)(2,1)} %g_hbm.1, bf16[512,256]{1,0:T(8,128)(2,1)} %k_hbm.1, bf16[512,256]{1,0:T(8,128)(2,1)} %v_hbm.1), custom_call_target="tpu_custom_call" | custom-call | flops 8000000000 | bytes 8388608 | tf_op jit(solution)/shard_map/attention_backward/pallas_call | solution.py:168
  21.6 1.3 %copy-done.1 = bf16[2048,512]{1,0:T(8,128)(2,1)} copy-done((bf16[2048,512]{1,0:T(8,128)(2,1)}, bf16[2048,512]{1,0:T(8,128)(2,1)S(1)}, u32[]{:S(2)}) %copy-start.1) | copy-done | bytes 2097176
  23.0 1.6 %copy-done.2 = bf16[2048,512]{1,0:T(8,128)(2,1)S(1)} copy-done((bf16[2048,512]{1,0:T(8,128)(2,1)S(1)}, bf16[2048,512]{1,0:T(8,128)(2,1)}, u32[]{:S(2)}) %copy-start.2) | copy-done | bytes 2097176
  24.5 1.7 %low.1.refs_0_ = f32[32,512]{1,0:T(8,128)S(1)} custom-call(s32[1,8]{1,0:T(1,128)S(1)} %copy-done.3, s32[1,8]{1,0:T(1,128)S(1)} %copy-done.4, s32[4]{0:T(128)S(1)} %copy-done.5, s32[1]{0:T(128)} %bitcast.me_ref, bf16[512,2048]{1,0:T(8,128)(2,1)S(1)} %copy-done, bf16[2048,512]{1,0:T(8,128)(2,1)S(1)} %copy-done.2, ...), custom_call_target="tpu_custom_call" | custom-call | flops 1000000000 | bytes 4194304 | tf_op jit(solution)/shard_map/low/pallas_call | solution.py:283
  26.2 0.1 collective-permute-start.5
  26.4 1.5 %collective-permute-start.4 = (f32[32,512]{1,0:T(8,128)S(1)}, f32[32,512]{1,0:T(8,128)S(1)}, u32[]{:S(2)}, u32[]{:S(2)}) collective-permute-start(f32[32,512]{1,0:T(8,128)S(1)} %low.1.refs_0_), channel_id=1, source_target_pairs={{0,2},{1,3},{2,0},{3,1},{4,6},{5,7},{6,4},{7,5},{8,10},{9,11},{10,... | collective-permute-start | bytes 196616 | tf_op jit(solution)/shard_map/ppermute | solution.py:297
  27.8 0.2 collective-permute-start.3
  28.0 0.3 collective-permute-done.5.refs_3_
  28.3 3.7 %collective-permute-done.4.refs_2_ = f32[32,512]{1,0:T(8,128)S(1)} collective-permute-done((f32[32,512]{1,0:T(8,128)S(1)}, f32[32,512]{1,0:T(8,128)S(1)}, u32[]{:S(2)}, u32[]{:S(2)}) %collective-permute-start.4) | collective-permute-done | bytes 65568 | tf_op jit(solution)/shard_map/ppermute | solution.py:297
  31.9 0.2 collective-permute-done.3.refs_1_
  32.1 1.7 %product.1 = (f32[32,2048]{1,0:T(8,128)S(1)}, bf16[32,2048]{1,0:T(8,128)(2,1)S(1)}, bf16[32,2048]{1,0:T(8,128)(2,1)S(1)}, bf16[32,2048]{1,0:T(8,128)(2,1)S(1)}, bf16[16,512]{1,0:T(8,128)(2,1)S(1)}) custom-call(s32[1,8]{1,0:T(1,128)S(1)} %copy-done.3, s32[1,8]{1,0:T(1,128)S(1)} %copy-done.4, s32[4]{0:T(128)S(1)} %copy-done.5, s32[1]{0:T(128)} %bitcast.me_ref, ...), custom_call_target="tpu_custom_call" | custom-call | flops 1000000000 | bytes 4194304 | tf_op jit(solution)/shard_map/product/pallas_call | solution.py:283
  33.8 2.5 %collective-permute-start.6 = (bf16[32,2048]{1,0:T(8,128)(2,1)S(1)}, bf16[32,2048]{1,0:T(8,128)(2,1)S(1)}, u32[]{:S(2)}, u32[]{:S(2)}) collective-permute-start(bf16[32,2048]{1,0:T(8,128)(2,1)S(1)} %get-tuple-element.18), channel_id=1, source_target_pairs={{0,4},{4,8},{8,12},{12,0},{1,5},{5,9},{9,13},{13,1},{2,6},{6,10},{... | collective-permute-start | bytes 393224 | tf_op jit(solution)/shard_map/ppermute | solution.py:297
  36.3 0.9 %collective-permute-start.7 = (bf16[32,2048]{1,0:T(8,128)(2,1)S(1)}, bf16[32,2048]{1,0:T(8,128)(2,1)S(1)}, u32[]{:S(2)}, u32[]{:S(2)}) collective-permute-start(bf16[32,2048]{1,0:T(8,128)(2,1)S(1)} %get-tuple-element.19), channel_id=1, source_target_pairs={{0,8},{4,12},{8,0},{12,4},{1,9},{5,13},{9,1},{13,5},{2,10},{6,14},... | collective-permute-start | bytes 393224 | tf_op jit(solution)/shard_map/ppermute | solution.py:297
  37.2 1.5 %collective-permute-start.8 = (bf16[32,2048]{1,0:T(8,128)(2,1)S(1)}, bf16[32,2048]{1,0:T(8,128)(2,1)S(1)}, u32[]{:S(2)}, u32[]{:S(2)}) collective-permute-start(bf16[32,2048]{1,0:T(8,128)(2,1)S(1)} %get-tuple-element.20), channel_id=1, source_target_pairs={{0,12},{4,0},{8,4},{12,8},{1,13},{5,1},{9,5},{13,9},{2,14},{6,2},{... | collective-permute-start | bytes 393224 | tf_op jit(solution)/shard_map/ppermute | solution.py:297
  38.7 2.6 %input_gradient.1 = bf16[512,2048]{1,0:T(8,128)(2,1)} custom-call(s32[1,8]{1,0:T(1,128)S(1)} %copy-done.3, s32[1,8]{1,0:T(1,128)S(1)} %copy-done.4, s32[4]{0:T(128)S(1)} %copy-done.5, s32[1]{0:T(128)} %bitcast.me_ref, bf16[16,512]{1,0:T(8,128)(2,1)S(1)} %get-tuple-element.14.low_ref, bf16[32,2048]{1,0:T(8,128)(2,1)S(1)} %pad_maximum_fusion.refs_0_, ...), custom_call_target="tpu_custom_call" | custom-call | flops 1000000000 | bytes 4194304 | tf_op jit(solution)/shard_map/input_gradient/pallas_call | solution.py:283
  41.4 0.8 %collective-permute-done.6 = bf16[32,2048]{1,0:T(8,128)(2,1)S(1)} collective-permute-done((bf16[32,2048]{1,0:T(8,128)(2,1)S(1)}, bf16[32,2048]{1,0:T(8,128)(2,1)S(1)}, u32[]{:S(2)}, u32[]{:S(2)}) %collective-permute-start.6) | collective-permute-done | bytes 131104 | tf_op jit(solution)/shard_map/ppermute | solution.py:297
  42.2 3.5 %collective-permute-done.7 = bf16[32,2048]{1,0:T(8,128)(2,1)S(1)} collective-permute-done((bf16[32,2048]{1,0:T(8,128)(2,1)S(1)}, bf16[32,2048]{1,0:T(8,128)(2,1)S(1)}, u32[]{:S(2)}, u32[]{:S(2)}) %collective-permute-start.7) | collective-permute-done | bytes 131104 | tf_op jit(solution)/shard_map/ppermute | solution.py:297
  45.7 0.1 convert_add_fusion
  45.7 0.7 %slice_bitcast_fusion = (f32[1,16,2048]{2,1,0:T(8,128)}, f32[1,16,2048]{2,1,0:T(8,128)}) fusion(f32[32,2048]{1,0:T(8,128)S(1)} %convert_add_fusion), kind=kLoop, calls=%fused_computation.1 | loop fusion | bytes 524288 | tf_op jit(solution)/shard_map/reshape | solution.py:359
  (13 shorter events, 0.0 us)
Async XLA Ops:
  1.5 21.4 %copy-start = (bf16[512,2048]{1,0:T(8,128)(2,1)S(1)}, bf16[512,2048]{1,0:T(8,128)(2,1)}, u32[]{:S(2)}) copy-start(bf16[512,2048]{1,0:T(8,128)(2,1)} %refs_4_.1) | copy-start | bytes 6291460
  1.5 21.4 %copy-start.3 = (s32[1,8]{1,0:T(1,128)S(1)}, s32[1,8]{1,0:T(1,128)}, u32[]{:S(2)}) copy-start(s32[1,8]{1,0:T(1,128)} %len_ref.7) | copy-start | bytes 100
  1.5 21.4 %copy-start.4 = (s32[1,8]{1,0:T(1,128)S(1)}, s32[1,8]{1,0:T(1,128)}, u32[]{:S(2)}) copy-start(s32[1,8]{1,0:T(1,128)} %adapter_ref.5) | copy-start | bytes 100
  1.6 21.4 %copy-start.5 = (s32[4]{0:T(128)S(1)}, s32[4]{0:T(128)}, u32[]{:S(2)}) copy-start(s32[4]{0:T(128)} %slot_ref.5) | copy-start | bytes 52
  1.6 21.3 %collective-permute-start.2 = (bf16[32,2048]{1,0:T(8,128)(2,1)S(1)}, bf16[32,2048]{1,0:T(8,128)(2,1)S(1)}, u32[]{:S(2)}, u32[]{:S(2)}) collective-permute-start(bf16[32,2048]{1,0:T(8,128)(2,1)S(1)} %pad_maximum_fusion.refs_0_), channel_id=1, source_target_pairs={{0,12},{4,0},{8,4},{12,8},{1,13},{5,1},{9,5},{13,9},{2,14},{6,2},{... | collective-permute-start | bytes 393224 | tf_op jit(solution)/shard_map/ppermute | solution.py:297
  6.7 16.2 %collective-permute-start.1 = (bf16[32,2048]{1,0:T(8,128)(2,1)S(1)}, bf16[32,2048]{1,0:T(8,128)(2,1)S(1)}, u32[]{:S(2)}, u32[]{:S(2)}) collective-permute-start(bf16[32,2048]{1,0:T(8,128)(2,1)S(1)} %pad_maximum_fusion.refs_0_), channel_id=1, source_target_pairs={{0,8},{4,12},{8,0},{12,4},{1,9},{5,13},{9,1},{13,5},{2,10},{6,14},... | collective-permute-start | bytes 393224 | tf_op jit(solution)/shard_map/ppermute | solution.py:297
  6.7 16.2 %collective-permute-start = (bf16[32,2048]{1,0:T(8,128)(2,1)S(1)}, bf16[32,2048]{1,0:T(8,128)(2,1)S(1)}, u32[]{:S(2)}, u32[]{:S(2)}) collective-permute-start(bf16[32,2048]{1,0:T(8,128)(2,1)S(1)} %pad_maximum_fusion.refs_0_), channel_id=1, source_target_pairs={{0,4},{4,8},{8,12},{12,0},{1,5},{5,9},{9,13},{13,1},{2,6},{6,10},{... | collective-permute-start | bytes 393224 | tf_op jit(solution)/shard_map/ppermute | solution.py:297
  21.6 1.3 %copy-start.1 = (bf16[2048,512]{1,0:T(8,128)(2,1)}, bf16[2048,512]{1,0:T(8,128)(2,1)S(1)}, u32[]{:S(2)}) copy-start(bf16[2048,512]{1,0:T(8,128)(2,1)S(1)} %get-tuple-element.13.gq_ref.refs_5_) | copy-start | bytes 6291460
  22.9 1.6 %copy-start.2 = (bf16[2048,512]{1,0:T(8,128)(2,1)S(1)}, bf16[2048,512]{1,0:T(8,128)(2,1)}, u32[]{:S(2)}) copy-start(bf16[2048,512]{1,0:T(8,128)(2,1)} %copy-done.1) | copy-start | bytes 6291460
  26.2 2.0 %collective-permute-start.5 = (f32[32,512]{1,0:T(8,128)S(1)}, f32[32,512]{1,0:T(8,128)S(1)}, u32[]{:S(2)}, u32[]{:S(2)}) collective-permute-start(f32[32,512]{1,0:T(8,128)S(1)} %low.1.refs_0_), channel_id=1, source_target_pairs={{0,3},{1,0},{2,1},{3,2},{4,7},{5,4},{6,5},{7,6},{8,11},{9,8},{10,9... | collective-permute-start | bytes 196616 | tf_op jit(solution)/shard_map/ppermute | solution.py:297
  26.4 5.6 %collective-permute-start.4 = (f32[32,512]{1,0:T(8,128)S(1)}, f32[32,512]{1,0:T(8,128)S(1)}, u32[]{:S(2)}, u32[]{:S(2)}) collective-permute-start(f32[32,512]{1,0:T(8,128)S(1)} %low.1.refs_0_), channel_id=1, source_target_pairs={{0,2},{1,3},{2,0},{3,1},{4,6},{5,7},{6,4},{7,5},{8,10},{9,11},{10,... | collective-permute-start | bytes 196616 | tf_op jit(solution)/shard_map/ppermute | solution.py:297
  27.8 4.3 %collective-permute-start.3 = (f32[32,512]{1,0:T(8,128)S(1)}, f32[32,512]{1,0:T(8,128)S(1)}, u32[]{:S(2)}, u32[]{:S(2)}) collective-permute-start(f32[32,512]{1,0:T(8,128)S(1)} %low.1.refs_0_), channel_id=1, source_target_pairs={{0,1},{1,2},{2,3},{3,0},{4,5},{5,6},{6,7},{7,4},{8,9},{9,10},{10,1... | collective-permute-start | bytes 196616 | tf_op jit(solution)/shard_map/ppermute | solution.py:297
  33.8 8.4 %collective-permute-start.6 = (bf16[32,2048]{1,0:T(8,128)(2,1)S(1)}, bf16[32,2048]{1,0:T(8,128)(2,1)S(1)}, u32[]{:S(2)}, u32[]{:S(2)}) collective-permute-start(bf16[32,2048]{1,0:T(8,128)(2,1)S(1)} %get-tuple-element.18), channel_id=1, source_target_pairs={{0,4},{4,8},{8,12},{12,0},{1,5},{5,9},{9,13},{13,1},{2,6},{6,10},{... | collective-permute-start | bytes 393224 | tf_op jit(solution)/shard_map/ppermute | solution.py:297
  36.3 9.3 %collective-permute-start.7 = (bf16[32,2048]{1,0:T(8,128)(2,1)S(1)}, bf16[32,2048]{1,0:T(8,128)(2,1)S(1)}, u32[]{:S(2)}, u32[]{:S(2)}) collective-permute-start(bf16[32,2048]{1,0:T(8,128)(2,1)S(1)} %get-tuple-element.19), channel_id=1, source_target_pairs={{0,8},{4,12},{8,0},{12,4},{1,9},{5,13},{9,1},{13,5},{2,10},{6,14},... | collective-permute-start | bytes 393224 | tf_op jit(solution)/shard_map/ppermute | solution.py:297
  37.2 8.4 %collective-permute-start.8 = (bf16[32,2048]{1,0:T(8,128)(2,1)S(1)}, bf16[32,2048]{1,0:T(8,128)(2,1)S(1)}, u32[]{:S(2)}, u32[]{:S(2)}) collective-permute-start(bf16[32,2048]{1,0:T(8,128)(2,1)S(1)} %get-tuple-element.20), channel_id=1, source_target_pairs={{0,12},{4,0},{8,4},{12,8},{1,13},{5,1},{9,5},{13,9},{2,14},{6,2},{... | collective-permute-start | bytes 393224 | tf_op jit(solution)/shard_map/ppermute | solution.py:297

commit v3 on v2

--- a/solution.py
+++ b/solution.py
@@ -19,6 +19,7 @@
 ADAPTER_SCALE = 2.0
 LOG2_E = 1.4426950408889634
 ATTENTION_VMEM = 24 * 1024 * 1024
+LOW_STEPS = 4
 VMEM_BYTES = 16 * 1024 * 1024
 
 NN = (((1,), (0,)), ((), ()))
@@ -37,54 +38,16 @@
     ]
 
 
-def attention_kernel(
-    len_ref,
-    q_hbm,
-    g_hbm,
-    k_hbm,
-    v_hbm,
-    gq_ref,
-    gk_ref,
-    gv_ref,
-    bias_ref,
-    q_ref,
-    g_ref,
-    k_ref,
-    v_ref,
-    row_sem,
-    group_sem,
-):
-    row_count = q_hbm.shape[0]
-    groups = k_hbm.shape[1] // HEAD_SIZE
-    wide = GROUP_SHARE * HEAD_SIZE
-    scale = 1.0 / math.sqrt(HEAD_SIZE)
-    spans = query_spans(row_count)
-
-    def group_copy(which, group):
-        source, target = ((k_hbm, k_ref), (v_hbm, v_ref))[which]
-        columns = pl.ds(group * HEAD_SIZE, HEAD_SIZE)
-        return pltpu.make_async_copy(
-            source.at[:, columns], target.at[group], group_sem.at[which, group]
-        )
-
-    def row_copy(which, group, block):
-        source, target = ((q_hbm, q_ref), (g_hbm, g_ref))[which]
-        rows = pl.ds(block * BLOCK, BLOCK)
-        return pltpu.make_async_copy(
-            source.at[rows, pl.ds(group * wide, wide)],
-            target.at[group, rows],
-            row_sem.at[which, group, block],
-        )
-
-    for group in range(groups):
-        group_copy(0, group).start()
-        group_copy(1, group).start()
-        for block in range(len(spans)):
-            row_copy(0, group, block).start()
-            row_copy(1, group, block).start()
-
+def pack_kernel(row_count, len_ref, down_hbm, up_hbm, own_ref, bias_ref, sems):
+    share = down_hbm.shape[0]
+    copies = [
+        pltpu.make_async_copy(down_hbm, own_ref.at[:share], sems.at[0]),
+        pltpu.make_async_copy(up_hbm, own_ref.at[share:], sems.at[1]),
+    ]
+    for copy in copies:
+        copy.start()
     at = 0
-    for first, low, high in spans:
+    for first, low, high in query_spans(row_count):
         width = high - low
         query = lax.broadcasted_iota(jnp.int32, (1, BLOCK), 1) + first
         start = jnp.zeros((1, BLOCK), jnp.int32)
@@ -95,25 +58,34 @@
         key = lax.broadcasted_iota(jnp.int32, (width, BLOCK), 0) + low
         bias_ref[at : at + width, :] = jnp.where((key >= start) & (key <= query), 0.0, MASKED)
         at += width
-
-    heads = [slice(h * HEAD_SIZE, (h + 1) * HEAD_SIZE) for h in range(GROUP_SHARE)]
-
-    def one_group(group):
-        group_copy(0, group).wait()
-        group_copy(1, group).wait()
-        key_t = k_ref[group].T
+    for copy in copies:
+        copy.wait()
+
+
+def attention_kernel(
+    bias_ref, q_ref, g_ref, k_ref, v_ref, gq_hbm, gk_ref, gv_ref, gq_ref, sems
+):
+    row_count = q_ref.shape[0]
+    scale = 1.0 / math.sqrt(HEAD_SIZE)
+    spans = query_spans(row_count)
+    copies = []
+    for group in range(k_ref.shape[1] // HEAD_SIZE):
+        columns = slice(group * HEAD_SIZE, (group + 1) * HEAD_SIZE)
+        heads = [
+            slice(h * HEAD_SIZE, (h + 1) * HEAD_SIZE)
+            for h in range(group * GROUP_SHARE, (group + 1) * GROUP_SHARE)
+        ]
+        key_t = k_ref[:, columns].T
         grad_key = [None] * len(spans)
         grad_value = [None] * len(spans)
         at = 0
-        for block, (first, low, high) in enumerate(spans):
+        for first, low, high in spans:
             width = high - low
             rows = slice(first, first + BLOCK)
-            row_copy(0, group, block).wait()
-            row_copy(1, group, block).wait()
-            query = jnp.concatenate([q_ref[group, rows, head] for head in heads], axis=0)
-            grad = jnp.concatenate([g_ref[group, rows, head] for head in heads], axis=0)
-            all_scores = mxu(k_ref[group, low:high, :], query, NT)
-            all_grad_weights = mxu(v_ref[group, low:high, :], grad, NT)
+            query = jnp.concatenate([q_ref[rows, head] for head in heads], axis=0)
+            grad = jnp.concatenate([g_ref[rows, head] for head in heads], axis=0)
+            all_scores = mxu(k_ref[low:high, columns], query, NT)
+            all_grad_weights = mxu(v_ref[low:high, columns], grad, NT)
             bias = bias_ref[at : at + width, :]
             at += width
             rounded, grad_scores = [], []
@@ -140,56 +112,44 @@
                         terms[part] if total[index] is None else total[index] + terms[part]
                     )
             grad_query = (mxu(key_t[:, low:high], grad_scores, NN) * scale).astype(jnp.bfloat16)
-            for h in range(GROUP_SHARE):
-                gq_ref[pl.ds(group * wide + h * HEAD_SIZE, HEAD_SIZE), rows] = grad_query[
-                    :, h * BLOCK : (h + 1) * BLOCK
-                ]
-        columns = pl.ds(group * HEAD_SIZE, HEAD_SIZE)
+            for h, head in enumerate(heads):
+                gq_ref[head, rows] = grad_query[:, h * BLOCK : (h + 1) * BLOCK]
+            block = (slice(heads[0].start, heads[-1].stop), rows)
+            copies.append(
+                pltpu.make_async_copy(gq_ref.at[block], gq_hbm.at[block], sems.at[len(copies)])
+            )
+            copies[-1].start()
         for index in range(len(spans)):
             rows = slice(index * BLOCK, (index + 1) * BLOCK)
             gk_ref[rows, columns] = (grad_key[index] * scale).astype(jnp.bfloat16)
             gv_ref[rows, columns] = grad_value[index].astype(jnp.bfloat16)
-
-    for group in range(groups):
-        one_group(group)
-
-
-def attention_backward(queries, keys, values, output_gradient, lengths):
-    row_count = queries.shape[0]
-    groups = keys.shape[1] // HEAD_SIZE
-    blocks = row_count // BLOCK
-    pair_rows = sum(high - low for _, low, high in query_spans(row_count))
-    wide = (groups, row_count, GROUP_SHARE * HEAD_SIZE)
-    narrow = (groups, row_count, HEAD_SIZE)
-    arrays = [
-        pltpu.with_memory_space_constraint(array, pltpu.HBM)
-        for array in (lengths, queries, output_gradient, keys, values)
-    ]
+    for copy in copies:
+        copy.wait()
+
+
+def attention_backward(bias, queries, output_gradient, keys, values):
+    turned = (queries.shape[1], queries.shape[0])
+    chunks = keys.shape[1] // HEAD_SIZE * (queries.shape[0] // BLOCK)
+    vmem = pl.BlockSpec(memory_space=pltpu.VMEM)
     return pl.pallas_call(
         attention_kernel,
-        in_specs=[pl.BlockSpec(memory_space=pltpu.SMEM)]
-        + [pl.BlockSpec(memory_space=pltpu.HBM)] * 4,
-        out_specs=[pl.BlockSpec(memory_space=pltpu.VMEM)] * 3,
+        in_specs=[vmem] * 5,
+        out_specs=[pl.BlockSpec(memory_space=pltpu.HBM), vmem, vmem],
         out_shape=[
-            jax.ShapeDtypeStruct((queries.shape[1], row_count), jnp.bfloat16),
+            pltpu.HBM(turned, jnp.bfloat16),
             jax.ShapeDtypeStruct(keys.shape, jnp.bfloat16),
             jax.ShapeDtypeStruct(values.shape, jnp.bfloat16),
         ],
         scratch_shapes=[
-            pltpu.VMEM((pair_rows, BLOCK), jnp.float32),
-            pltpu.VMEM(wide, jnp.bfloat16),
-            pltpu.VMEM(wide, jnp.bfloat16),
-            pltpu.VMEM(narrow, jnp.bfloat16),
-            pltpu.VMEM(narrow, jnp.bfloat16),
-            pltpu.SemaphoreType.DMA((2, groups, blocks)),
-            pltpu.SemaphoreType.DMA((2, groups)),
+            pltpu.VMEM(turned, jnp.bfloat16),
+            pltpu.SemaphoreType.DMA((chunks,)),
         ],
         compiler_params=pltpu.CompilerParams(vmem_limit_bytes=ATTENTION_VMEM),
         cost_estimate=pl.CostEstimate(
             flops=8 * 10**9, bytes_accessed=8 * 2**20, transcendentals=0
         ),
         name="attention_backward",
-    )(*arrays)
+    )(bias, queries, output_gradient, keys, values)
 
 
 def slot_masks(len_ref, adapter_ref, slot_ref, row_count, slots):
@@ -218,8 +178,16 @@
     return total
 
 
-def low_kernel(peers, local_slots, len_ref, adapter_ref, slot_ref, me_ref, x_ref, gq_ref, *refs):
-    factors, out_ref = refs[:peers], refs[peers]
+def low_kernel(peers, local_slots, len_ref, adapter_ref, slot_ref, me_ref, x_ref, gq_hbm, *refs):
+    factors, (out_ref, gq_ref, sems) = refs[:peers], refs[peers:]
+    step = gq_ref.shape[0] // LOW_STEPS
+    pieces = [pl.ds(index * step, step) for index in range(LOW_STEPS)]
+    copies = [
+        pltpu.make_async_copy(gq_hbm.at[piece], gq_ref.at[piece], sems.at[index])
+        for index, piece in enumerate(pieces)
+    ]
+    for copy in copies:
+        copy.start()
     rank = factors[0].shape[0] // (2 * local_slots)
     share = rank * local_slots
     row_count = x_ref.shape[0]
@@ -227,9 +195,14 @@
         len_ref, adapter_ref, slot_ref, row_count, peer_slots(me_ref[0], peers, local_slots, -1)
     )
     down = jnp.concatenate([ref[:share] for ref in factors], axis=0)
-    up = jnp.concatenate([ref[share:] for ref in factors], axis=0)
     out_ref[:rank] = select(mxu(down, x_ref[...], NT), masks, rank)
-    out_ref[rank:] = select(mxu(up, gq_ref[...], NN), masks, rank)
+    total = None
+    for piece, copy in zip(pieces, copies):
+        up = jnp.concatenate([ref[share:, piece] for ref in factors], axis=0)
+        copy.wait()
+        part = mxu(up, gq_ref[piece], NN)
+        total = part if total is None else total + part
+    out_ref[rank:] = select(total, masks, rank)
 
 
 def spread(low, masks):
@@ -279,13 +252,17 @@
     out_ref[...] = (mxu(wide, down, TN) * ADAPTER_SCALE).astype(jnp.bfloat16)
 
 
-def call(kernel, scalars, arrays, out_shape, flops, name):
+def call(kernel, scalars, arrays, out_shape, flops, name, in_hbm=(), scratch=()):
     return pl.pallas_call(
         kernel,
         in_specs=[pl.BlockSpec(memory_space=pltpu.SMEM)] * len(scalars)
-        + [pl.BlockSpec(memory_space=pltpu.VMEM)] * len(arrays),
+        + [
+            pl.BlockSpec(memory_space=pltpu.HBM if index in in_hbm else pltpu.VMEM)
+            for index in range(len(arrays))
+        ],
         out_specs=jax.tree.map(lambda _: pl.BlockSpec(memory_space=pltpu.VMEM), out_shape),
         out_shape=out_shape,
+        scratch_shapes=scratch,
         compiler_params=pltpu.CompilerParams(vmem_limit_bytes=VMEM_BYTES),
         cost_estimate=pl.CostEstimate(flops=flops, bytes_accessed=4 * 2**20, transcendentals=0),
         name=name,
@@ -315,20 +292,50 @@
     peers, parts = lax.axis_size("dp"), lax.axis_size("tensor")
     me = lax.axis_index("dp").astype(jnp.int32).reshape(1)
     scalars = (document_length, document_adapter, adapter_in_slot, me)
-    own = jnp.concatenate(
-        [down_weight.reshape(share, width), up_weight.reshape(share, width)], axis=0
+    pair_rows = sum(high - low for _, low, high in query_spans(row_count))
+    own, bias = pl.pallas_call(
+        functools.partial(pack_kernel, row_count),
+        in_specs=[pl.BlockSpec(memory_space=pltpu.SMEM)]
+        + [pl.BlockSpec(memory_space=pltpu.HBM)] * 2,
+        out_specs=[pl.BlockSpec(memory_space=pltpu.VMEM)] * 2,
+        out_shape=[
+            jax.ShapeDtypeStruct((2 * share, width), down_weight.dtype),
+            jax.ShapeDtypeStruct((pair_rows, BLOCK), jnp.float32),
+        ],
+        scratch_shapes=[pltpu.SemaphoreType.DMA((2,))],
+        compiler_params=pltpu.CompilerParams(vmem_limit_bytes=VMEM_BYTES),
+        cost_estimate=pl.CostEstimate(flops=10**10, bytes_accessed=2**20, transcendentals=0),
+        name="pack",
+    )(
+        *(
+            pltpu.with_memory_space_constraint(array, pltpu.HBM)
+            for array in (
+                document_length,
+                down_weight.reshape(share, width),
+                up_weight.reshape(share, width),
+            )
+        )
     )
     factors = [own] + [send(own, "dp", shift) for shift in range(1, peers)]
     query_gradient, key_gradient, value_gradient = attention_backward(
-        rotated_queries, rotated_keys, value_rows, output_gradient, document_length
+        bias, rotated_queries, output_gradient, rotated_keys, value_rows
     )
     low = call(
         functools.partial(low_kernel, peers, local_slots),
         scalars,
-        (normed_input, query_gradient, *factors),
+        (
+            normed_input,
+            pltpu.with_memory_space_constraint(query_gradient, pltpu.HBM),
+            *factors,
+        ),
         jax.ShapeDtypeStruct((2 * rank, row_count), jnp.float32),
         10**9,
         "low",
+        in_hbm=(1,),
+        scratch=[
+            pltpu.VMEM((width, row_count), jnp.bfloat16),
+            pltpu.SemaphoreType.DMA((LOW_STEPS,)),
+        ],
     )
     lows = [low] + [send(low, "tensor", shift) for shift in range(1, parts)]
     *terms, low_grads = call(

time: 46.9 us -> 42.2 us (0.90)
  local copies, waits for them, and re-layouts: 3.64 us -> 0.77 us
  Pallas kernels: 19.8 us -> 18.9 us
  other arithmetic: 0.94 us -> 0.06 us
  waiting for transfers between devices: 8.41 us -> 7.86 us
  starting transfers between devices: 12.9 us -> 13.4 us
    unnamed x12 -> x18, local copies, waits for them, and re-layouts: 2.92 us -> 0.05 us
    pallas_call x1 -> x2, Pallas kernels: 13.9 us -> 12.2 us  [the longest x1 10.2 us: attention_backward(): pl.pallas_call(attention_kernel, in_specs=[vmem] * 5, out_specs=[pl.Block...]
    concatenate x1 -> x0, other arithmetic: 0.88 us -> none  [local(): jnp.concatenate([down_weight.reshape(share, width), up_weight.reshape(sha...]
    pallas_call x3, Pallas kernels: 5.96 us -> 6.66 us  [call(): pl.pallas_call(kernel, in_specs=[pl.BlockSpec(memory_space=pltpu.SMEM)] *...]
    ppermute x9, starting transfers between devices: 12.9 us -> 13.4 us  [send(): lax.ppermute(array, axis, [(i, (i + shift) % size) for i in range(size)])]
    ppermute x9, waiting for transfers between devices: 8.41 us -> 7.86 us  [send(): lax.ppermute(array, axis, [(i, (i + shift) % size) for i in range(size)])]
  transfers between devices with their start and end apart: 9 -> 9, of which waited for: 5 -> 5; matrix products, arithmetic and copies ran while one was open for 0% -> 0% of each run, Pallas kernels for 36% -> 31%
where the time goes in v3:
time: 42.2 us; the launch traced here: 41.8 us
  Pallas kernels  18.9 us (45%)
  starting transfers between devices  13.4 us (32%)
  waiting for transfers between devices  7.86 us (19%)
  between operations  0.81 us (2%)
  local copies, waits for them, and re-layouts  0.77 us (2%)
    ppermute x9, starting transfers between devices, send(): lax.ppermute(array, axis, [(i, (i + shift) % size) for i in range(size)])  13.4 us
    pallas_call x1, Pallas kernels, attention_backward(): pl.pallas_call(attention_kernel, in_specs=[vmem] * 5, out_specs=[pl.Block...  10.2 us
    ppermute x9, waiting for transfers between devices, send(): lax.ppermute(array, axis, [(i, (i + shift) % size) for i in range(size)])  7.86 us
    pallas_call x3, Pallas kernels, call(): pl.pallas_call(kernel, in_specs=[pl.BlockSpec(memory_space=pltpu.SMEM)] *...  6.66 us
    pallas_call x1, Pallas kernels, local(): pl.pallas_call(functools.partial(pack_kernel, row_count), in_specs=[pl.Bl...  2.09 us
  transfers between devices with their start and end apart: 9, of which 5 were waited for; matrix products, arithmetic and copies ran while one was open for 0% of the time, Pallas kernels for 31%

profile of v3, /device:TPU:0, one launch (start us, length us, event | category | flops | bytes accessed | tf_op | source)
XLA Modules:
  0.0 41.8 jit_solution(10996410631825080663)
XLA Ops:
  0.7 2.1 %pack.1 = (bf16[32,2048]{1,0:T(8,128)(2,1)S(1)}, f32[1152,128]{1,0:T(8,128)S(1)}) custom-call(s32[1,8]{1,0:T(1,128)} %len_ref.7, bf16[16,2048]{1,0:T(8,128)(2,1)} %bitcast.7, bf16[16,2048]{1,0:T(8,128)(2,1)} %bitcast.8), custom_call_target="tpu_custom_call" | custom-call | flops 10000000000 | bytes 1048576 | tf_op jit(solution)/shard_map/pack/pallas_call | solution.py:296
  2.8 5.1 %collective-permute-start.2 = (bf16[32,2048]{1,0:T(8,128)(2,1)S(1)}, bf16[32,2048]{1,0:T(8,128)(2,1)S(1)}, u32[]{:S(2)}, u32[]{:S(2)}) collective-permute-start(bf16[32,2048]{1,0:T(8,128)(2,1)S(1)} %get-tuple-element.17.refs_0_), channel_id=1, source_target_pairs={{0,12},{4,0},{8,4},{12,8},{1,13},{5,1},{9,5},{13,9},{2,14},{6,2},{... | collective-permute-start | bytes 393224 | tf_op jit(solution)/shard_map/ppermute | solution.py:274
  7.9 1.0 %collective-permute-start = (bf16[32,2048]{1,0:T(8,128)(2,1)S(1)}, bf16[32,2048]{1,0:T(8,128)(2,1)S(1)}, u32[]{:S(2)}, u32[]{:S(2)}) collective-permute-start(bf16[32,2048]{1,0:T(8,128)(2,1)S(1)} %get-tuple-element.17.refs_0_), channel_id=1, source_target_pairs={{0,4},{4,8},{8,12},{12,0},{1,5},{5,9},{9,13},{13,1},{2,6},{6,10},{... | collective-permute-start | bytes 393224 | tf_op jit(solution)/shard_map/ppermute | solution.py:274
  8.9 0.0 copy-start
  8.9 0.0 copy-start.2
  8.9 0.0 copy-start.3
  8.9 0.0 copy-start.4
  8.9 10.2 %attention_backward.1 = (bf16[2048,512]{1,0:T(8,128)(2,1)}, bf16[512,256]{1,0:T(8,128)(2,1)}, bf16[512,256]{1,0:T(8,128)(2,1)}) custom-call(f32[1152,128]{1,0:T(8,128)S(1)} %get-tuple-element.15.bias_ref, bf16[512,2048]{1,0:T(8,128)(2,1)S(1)} %copy-done.5, bf16[512,2048]{1,0:T(8,128)(2,1)S(1)} %copy-done.6, bf16[512,256]{1,0:T(8,128)(2,1)S(1)} %copy-done.7, ...), custom_call_target="tpu_custom_call" | custom-call | flops 8000000000 | bytes 8388608 | tf_op jit(solution)/shard_map/attention_backward/pallas_call | solution.py:134
  19.2 2.4 %low.1.refs_0_ = f32[32,512]{1,0:T(8,128)S(1)} custom-call(s32[1,8]{1,0:T(1,128)S(1)} %copy-done.2, s32[1,8]{1,0:T(1,128)S(1)} %copy-done.3, s32[4]{0:T(128)S(1)} %copy-done.4, s32[1]{0:T(128)} %bitcast.me_ref, bf16[512,2048]{1,0:T(8,128)(2,1)S(1)} %copy-done, bf16[2048,512]{1,0:T(8,128)(2,1)} %get-tuple-element.16.gq_hbm.refs_5_, ...), custom_call_target="tpu_custom_call" | custom-call | flops 1000000000 | bytes 4194304 | tf_op jit(solution)/shard_map/low/pallas_call | solution.py:256
  21.6 0.4 %collective-permute-start.5 = (f32[32,512]{1,0:T(8,128)S(1)}, f32[32,512]{1,0:T(8,128)S(1)}, u32[]{:S(2)}, u32[]{:S(2)}) collective-permute-start(f32[32,512]{1,0:T(8,128)S(1)} %low.1.refs_0_), channel_id=1, source_target_pairs={{0,3},{1,0},{2,1},{3,2},{4,7},{5,4},{6,5},{7,6},{8,11},{9,8},{10,9... | collective-permute-start | bytes 196616 | tf_op jit(solution)/shard_map/ppermute | solution.py:274
  22.0 1.2 %collective-permute-start.4 = (f32[32,512]{1,0:T(8,128)S(1)}, f32[32,512]{1,0:T(8,128)S(1)}, u32[]{:S(2)}, u32[]{:S(2)}) collective-permute-start(f32[32,512]{1,0:T(8,128)S(1)} %low.1.refs_0_), channel_id=1, source_target_pairs={{0,2},{1,3},{2,0},{3,1},{4,6},{5,7},{6,4},{7,5},{8,10},{9,11},{10,... | collective-permute-start | bytes 196616 | tf_op jit(solution)/shard_map/ppermute | solution.py:274
  23.2 0.2 collective-permute-start.3
  23.4 0.5 %collective-permute-done.5.refs_3_ = f32[32,512]{1,0:T(8,128)S(1)} collective-permute-done((f32[32,512]{1,0:T(8,128)S(1)}, f32[32,512]{1,0:T(8,128)S(1)}, u32[]{:S(2)}, u32[]{:S(2)}) %collective-permute-start.5) | collective-permute-done | bytes 65568 | tf_op jit(solution)/shard_map/ppermute | solution.py:274
  23.9 3.4 %collective-permute-done.4.refs_2_ = f32[32,512]{1,0:T(8,128)S(1)} collective-permute-done((f32[32,512]{1,0:T(8,128)S(1)}, f32[32,512]{1,0:T(8,128)S(1)}, u32[]{:S(2)}, u32[]{:S(2)}) %collective-permute-start.4) | collective-permute-done | bytes 65568 | tf_op jit(solution)/shard_map/ppermute | solution.py:274
  27.3 0.2 collective-permute-done.3.refs_1_
  27.5 1.7 %product.1 = (f32[32,2048]{1,0:T(8,128)S(1)}, bf16[32,2048]{1,0:T(8,128)(2,1)S(1)}, bf16[32,2048]{1,0:T(8,128)(2,1)S(1)}, bf16[32,2048]{1,0:T(8,128)(2,1)S(1)}, bf16[16,512]{1,0:T(8,128)(2,1)S(1)}) custom-call(s32[1,8]{1,0:T(1,128)S(1)} %copy-done.2, s32[1,8]{1,0:T(1,128)S(1)} %copy-done.3, s32[4]{0:T(128)S(1)} %copy-done.4, s32[1]{0:T(128)} %bitcast.me_ref, ...), custom_call_target="tpu_custom_call" | custom-call | flops 1000000000 | bytes 4194304 | tf_op jit(solution)/shard_map/product/pallas_call | solution.py:256
  29.2 2.5 %collective-permute-start.6 = (bf16[32,2048]{1,0:T(8,128)(2,1)S(1)}, bf16[32,2048]{1,0:T(8,128)(2,1)S(1)}, u32[]{:S(2)}, u32[]{:S(2)}) collective-permute-start(bf16[32,2048]{1,0:T(8,128)(2,1)S(1)} %get-tuple-element.22), channel_id=1, source_target_pairs={{0,4},{4,8},{8,12},{12,0},{1,5},{5,9},{9,13},{13,1},{2,6},{6,10},{... | collective-permute-start | bytes 393224 | tf_op jit(solution)/shard_map/ppermute | solution.py:274
  31.7 0.9 %collective-permute-start.7 = (bf16[32,2048]{1,0:T(8,128)(2,1)S(1)}, bf16[32,2048]{1,0:T(8,128)(2,1)S(1)}, u32[]{:S(2)}, u32[]{:S(2)}) collective-permute-start(bf16[32,2048]{1,0:T(8,128)(2,1)S(1)} %get-tuple-element.23), channel_id=1, source_target_pairs={{0,8},{4,12},{8,0},{12,4},{1,9},{5,13},{9,1},{13,5},{2,10},{6,14},... | collective-permute-start | bytes 393224 | tf_op jit(solution)/shard_map/ppermute | solution.py:274
  32.6 2.1 %collective-permute-start.8 = (bf16[32,2048]{1,0:T(8,128)(2,1)S(1)}, bf16[32,2048]{1,0:T(8,128)(2,1)S(1)}, u32[]{:S(2)}, u32[]{:S(2)}) collective-permute-start(bf16[32,2048]{1,0:T(8,128)(2,1)S(1)} %get-tuple-element.24), channel_id=1, source_target_pairs={{0,12},{4,0},{8,4},{12,8},{1,13},{5,1},{9,5},{13,9},{2,14},{6,2},{... | collective-permute-start | bytes 393224 | tf_op jit(solution)/shard_map/ppermute | solution.py:274
  34.7 2.6 %input_gradient.1 = bf16[512,2048]{1,0:T(8,128)(2,1)} custom-call(s32[1,8]{1,0:T(1,128)S(1)} %copy-done.2, s32[1,8]{1,0:T(1,128)S(1)} %copy-done.3, s32[4]{0:T(128)S(1)} %copy-done.4, s32[1]{0:T(128)} %bitcast.me_ref, bf16[16,512]{1,0:T(8,128)(2,1)S(1)} %get-tuple-element.18.low_ref, bf16[32,2048]{1,0:T(8,128)(2,1)S(1)} %get-tuple-element.17.refs_0_, ...), custom_call_target="tpu_custom_call" | custom-call | flops 1000000000 | bytes 4194304 | tf_op jit(solution)/shard_map/input_gradient/pallas_call | solution.py:256
  37.3 0.3 collective-permute-done.6
  37.5 3.5 %collective-permute-done.7 = bf16[32,2048]{1,0:T(8,128)(2,1)S(1)} collective-permute-done((bf16[32,2048]{1,0:T(8,128)(2,1)S(1)}, bf16[32,2048]{1,0:T(8,128)(2,1)S(1)}, u32[]{:S(2)}, u32[]{:S(2)}) %collective-permute-start.7) | collective-permute-done | bytes 131104 | tf_op jit(solution)/shard_map/ppermute | solution.py:274
  41.0 0.1 convert_add_fusion
  41.1 0.7 %slice_bitcast_fusion = (f32[1,16,2048]{2,1,0:T(8,128)}, f32[1,16,2048]{2,1,0:T(8,128)}) fusion(f32[32,2048]{1,0:T(8,128)S(1)} %convert_add_fusion), kind=kLoop, calls=%fused_computation.1 | loop fusion | bytes 524288 | tf_op jit(solution)/shard_map/reshape | solution.py:366
  (19 shorter events, 0.0 us)
Async XLA Ops:
  0.6 8.3 %copy-start.5 = (bf16[512,2048]{1,0:T(8,128)(2,1)S(1)}, bf16[512,2048]{1,0:T(8,128)(2,1)}, u32[]{:S(2)}) copy-start(bf16[512,2048]{1,0:T(8,128)(2,1)} %q_ref.1) | copy-start | bytes 6291460
  0.6 8.2 %copy-start.6 = (bf16[512,2048]{1,0:T(8,128)(2,1)S(1)}, bf16[512,2048]{1,0:T(8,128)(2,1)}, u32[]{:S(2)}) copy-start(bf16[512,2048]{1,0:T(8,128)(2,1)} %g_ref.1) | copy-start | bytes 6291460
  0.7 8.2 %copy-start.7 = (bf16[512,256]{1,0:T(8,128)(2,1)S(1)}, bf16[512,256]{1,0:T(8,128)(2,1)}, u32[]{:S(2)}) copy-start(bf16[512,256]{1,0:T(8,128)(2,1)} %k_ref.1) | copy-start | bytes 786436
  0.7 8.2 %copy-start.8 = (bf16[512,256]{1,0:T(8,128)(2,1)S(1)}, bf16[512,256]{1,0:T(8,128)(2,1)}, u32[]{:S(2)}) copy-start(bf16[512,256]{1,0:T(8,128)(2,1)} %v_ref.1) | copy-start | bytes 786436
  2.8 16.4 %collective-permute-start.2 = (bf16[32,2048]{1,0:T(8,128)(2,1)S(1)}, bf16[32,2048]{1,0:T(8,128)(2,1)S(1)}, u32[]{:S(2)}, u32[]{:S(2)}) collective-permute-start(bf16[32,2048]{1,0:T(8,128)(2,1)S(1)} %get-tuple-element.17.refs_0_), channel_id=1, source_target_pairs={{0,12},{4,0},{8,4},{12,8},{1,13},{5,1},{9,5},{13,9},{2,14},{6,2},{... | collective-permute-start | bytes 393224 | tf_op jit(solution)/shard_map/ppermute | solution.py:274
  7.9 11.3 %collective-permute-start.1 = (bf16[32,2048]{1,0:T(8,128)(2,1)S(1)}, bf16[32,2048]{1,0:T(8,128)(2,1)S(1)}, u32[]{:S(2)}, u32[]{:S(2)}) collective-permute-start(bf16[32,2048]{1,0:T(8,128)(2,1)S(1)} %get-tuple-element.17.refs_0_), channel_id=1, source_target_pairs={{0,8},{4,12},{8,0},{12,4},{1,9},{5,13},{9,1},{13,5},{2,10},{6,14},... | collective-permute-start | bytes 393224 | tf_op jit(solution)/shard_map/ppermute | solution.py:274
  7.9 11.3 %collective-permute-start = (bf16[32,2048]{1,0:T(8,128)(2,1)S(1)}, bf16[32,2048]{1,0:T(8,128)(2,1)S(1)}, u32[]{:S(2)}, u32[]{:S(2)}) collective-permute-start(bf16[32,2048]{1,0:T(8,128)(2,1)S(1)} %get-tuple-element.17.refs_0_), channel_id=1, source_target_pairs={{0,4},{4,8},{8,12},{12,0},{1,5},{5,9},{9,13},{13,1},{2,6},{6,10},{... | collective-permute-start | bytes 393224 | tf_op jit(solution)/shard_map/ppermute | solution.py:274
  8.9 10.3 %copy-start = (bf16[512,2048]{1,0:T(8,128)(2,1)S(1)}, bf16[512,2048]{1,0:T(8,128)(2,1)}, u32[]{:S(2)}) copy-start(bf16[512,2048]{1,0:T(8,128)(2,1)} %refs_4_.1) | copy-start | bytes 6291460
  8.9 10.3 %copy-start.2 = (s32[1,8]{1,0:T(1,128)S(1)}, s32[1,8]{1,0:T(1,128)}, u32[]{:S(2)}) copy-start(s32[1,8]{1,0:T(1,128)} %len_ref.7) | copy-start | bytes 100
  8.9 10.2 %copy-start.3 = (s32[1,8]{1,0:T(1,128)S(1)}, s32[1,8]{1,0:T(1,128)}, u32[]{:S(2)}) copy-start(s32[1,8]{1,0:T(1,128)} %adapter_ref.5) | copy-start | bytes 100
  8.9 10.2 %copy-start.4 = (s32[4]{0:T(128)S(1)}, s32[4]{0:T(128)}, u32[]{:S(2)}) copy-start(s32[4]{0:T(128)} %slot_ref.5) | copy-start | bytes 52
  19.2 8.3 %copy-start.1 = (bf16[2048,512]{1,0:T(8,128)(2,1)S(1)}, bf16[2048,512]{1,0:T(8,128)(2,1)}, u32[]{:S(2)}) copy-start(bf16[2048,512]{1,0:T(8,128)(2,1)} %get-tuple-element.16.gq_hbm.refs_5_) | copy-start | bytes 6291460
  21.6 2.3 %collective-permute-start.5 = (f32[32,512]{1,0:T(8,128)S(1)}, f32[32,512]{1,0:T(8,128)S(1)}, u32[]{:S(2)}, u32[]{:S(2)}) collective-permute-start(f32[32,512]{1,0:T(8,128)S(1)} %low.1.refs_0_), channel_id=1, source_target_pairs={{0,3},{1,0},{2,1},{3,2},{4,7},{5,4},{6,5},{7,6},{8,11},{9,8},{10,9... | collective-permute-start | bytes 196616 | tf_op jit(solution)/shard_map/ppermute | solution.py:274
  22.0 5.3 %collective-permute-start.4 = (f32[32,512]{1,0:T(8,128)S(1)}, f32[32,512]{1,0:T(8,128)S(1)}, u32[]{:S(2)}, u32[]{:S(2)}) collective-permute-start(f32[32,512]{1,0:T(8,128)S(1)} %low.1.refs_0_), channel_id=1, source_target_pairs={{0,2},{1,3},{2,0},{3,1},{4,6},{5,7},{6,4},{7,5},{8,10},{9,11},{10,... | collective-permute-start | bytes 196616 | tf_op jit(solution)/shard_map/ppermute | solution.py:274
  23.2 4.3 %collective-permute-start.3 = (f32[32,512]{1,0:T(8,128)S(1)}, f32[32,512]{1,0:T(8,128)S(1)}, u32[]{:S(2)}, u32[]{:S(2)}) collective-permute-start(f32[32,512]{1,0:T(8,128)S(1)} %low.1.refs_0_), channel_id=1, source_target_pairs={{0,1},{1,2},{2,3},{3,0},{4,5},{5,6},{6,7},{7,4},{8,9},{9,10},{10,1... | collective-permute-start | bytes 196616 | tf_op jit(solution)/shard_map/ppermute | solution.py:274
  29.2 8.4 %collective-permute-start.6 = (bf16[32,2048]{1,0:T(8,128)(2,1)S(1)}, bf16[32,2048]{1,0:T(8,128)(2,1)S(1)}, u32[]{:S(2)}, u32[]{:S(2)}) collective-permute-start(bf16[32,2048]{1,0:T(8,128)(2,1)S(1)} %get-tuple-element.22), channel_id=1, source_target_pairs={{0,4},{4,8},{8,12},{12,0},{1,5},{5,9},{9,13},{13,1},{2,6},{6,10},{... | collective-permute-start | bytes 393224 | tf_op jit(solution)/shard_map/ppermute | solution.py:274
  31.7 9.3 %collective-permute-start.7 = (bf16[32,2048]{1,0:T(8,128)(2,1)S(1)}, bf16[32,2048]{1,0:T(8,128)(2,1)S(1)}, u32[]{:S(2)}, u32[]{:S(2)}) collective-permute-start(bf16[32,2048]{1,0:T(8,128)(2,1)S(1)} %get-tuple-element.23), channel_id=1, source_target_pairs={{0,8},{4,12},{8,0},{12,4},{1,9},{5,13},{9,1},{13,5},{2,10},{6,14},... | collective-permute-start | bytes 393224 | tf_op jit(solution)/shard_map/ppermute | solution.py:274
  32.6 8.4 %collective-permute-start.8 = (bf16[32,2048]{1,0:T(8,128)(2,1)S(1)}, bf16[32,2048]{1,0:T(8,128)(2,1)S(1)}, u32[]{:S(2)}, u32[]{:S(2)}) collective-permute-start(bf16[32,2048]{1,0:T(8,128)(2,1)S(1)} %get-tuple-element.24), channel_id=1, source_target_pairs={{0,12},{4,0},{8,4},{12,8},{1,13},{5,1},{9,5},{13,9},{2,14},{6,2},{... | collective-permute-start | bytes 393224 | tf_op jit(solution)/shard_map/ppermute | solution.py:274

commit v4 on v3

--- a/solution.py
+++ b/solution.py
@@ -162,10 +162,10 @@
     return [adapter == slot_ref[slot] for slot in slots]
 
 
-def peer_slots(me, peers, local_slots, sign):
+def peer_slots(me, peers, local_slots):
     return [
-        lax.rem(me + sign * shift + peers, peers) * local_slots + own
-        for shift in range(peers)
+        (me ^ distance) * local_slots + own
+        for distance in range(peers)
         for own in range(local_slots)
     ]
 
@@ -179,7 +179,7 @@
 
 
 def low_kernel(peers, local_slots, len_ref, adapter_ref, slot_ref, me_ref, x_ref, gq_hbm, *refs):
-    factors, (out_ref, gq_ref, sems) = refs[:peers], refs[peers:]
+    factors, (out_ref, sent_ref, gq_ref, sems) = refs[:peers], refs[peers:]
     step = gq_ref.shape[0] // LOW_STEPS
     pieces = [pl.ds(index * step, step) for index in range(LOW_STEPS)]
     copies = [
@@ -192,7 +192,7 @@
     share = rank * local_slots
     row_count = x_ref.shape[0]
     masks = slot_masks(
-        len_ref, adapter_ref, slot_ref, row_count, peer_slots(me_ref[0], peers, local_slots, -1)
+        len_ref, adapter_ref, slot_ref, row_count, peer_slots(me_ref[0], peers, local_slots)
     )
     down = jnp.concatenate([ref[:share] for ref in factors], axis=0)
     out_ref[:rank] = select(mxu(down, x_ref[...], NT), masks, rank)
@@ -203,6 +203,7 @@
         part = mxu(up, gq_ref[piece], NN)
         total = part if total is None else total + part
     out_ref[rank:] = select(total, masks, rank)
+    sent_ref[...] = out_ref[...].astype(jnp.bfloat16)
 
 
 def spread(low, masks):
@@ -216,7 +217,7 @@
     lows, (x_ref, gq_ref), outs = refs[:parts], refs[parts : parts + 2], refs[parts + 2 :]
     low = lows[0][...]
     for ref in lows[1:]:
-        low = low + ref[...]
+        low = low + ref[...].astype(jnp.float32)
     rank = low.shape[0] // 2
     share = rank * local_slots
     low = low.astype(jnp.bfloat16).astype(jnp.float32)
@@ -225,13 +226,13 @@
         adapter_ref,
         slot_ref,
         x_ref.shape[0],
-        peer_slots(me_ref[0], peers, local_slots, 1),
+        peer_slots(me_ref[0], peers, local_slots),
     )
     wide_in, wide_grad = spread(low[:rank], masks), spread(low[rank:], masks)
     down = mxu(wide_grad, x_ref[...], NN) * ADAPTER_SCALE
     up = mxu(wide_in, gq_ref[...], NT) * ADAPTER_SCALE
-    for shift, ref in enumerate(outs[:peers]):
-        rows = slice(shift * share, (shift + 1) * share)
+    for distance, ref in enumerate(outs[:peers]):
+        rows = slice(distance * share, (distance + 1) * share)
         ref[:share] = down[rows].astype(ref.dtype)
         ref[share:] = up[rows].astype(ref.dtype)
     outs[peers][...] = low[rank:].astype(jnp.bfloat16)
@@ -245,7 +246,7 @@
         adapter_ref,
         slot_ref,
         low_ref.shape[1],
-        peer_slots(me_ref[0], peers, local_slots, -1),
+        peer_slots(me_ref[0], peers, local_slots),
     )
     wide = spread(low_ref[...].astype(jnp.float32), masks)
     down = jnp.concatenate([ref[: rank * local_slots] for ref in factors], axis=0)
@@ -269,9 +270,9 @@
     )(*scalars, *arrays)
 
 
-def send(array, axis, shift):
+def swap(array, axis, distance):
     size = lax.axis_size(axis)
-    return lax.ppermute(array, axis, [(i, (i + shift) % size) for i in range(size)])
+    return lax.ppermute(array, axis, [(i, i ^ distance) for i in range(size)])
 
 
 def local(
@@ -316,11 +317,11 @@
             )
         )
     )
-    factors = [own] + [send(own, "dp", shift) for shift in range(1, peers)]
+    factors = [own] + [swap(own, "dp", distance) for distance in range(1, peers)]
     query_gradient, key_gradient, value_gradient = attention_backward(
         bias, rotated_queries, output_gradient, rotated_keys, value_rows
     )
-    low = call(
+    low, low_sent = call(
         functools.partial(low_kernel, peers, local_slots),
         scalars,
         (
@@ -328,7 +329,10 @@
             pltpu.with_memory_space_constraint(query_gradient, pltpu.HBM),
             *factors,
         ),
-        jax.ShapeDtypeStruct((2 * rank, row_count), jnp.float32),
+        [
+            jax.ShapeDtypeStruct((2 * rank, row_count), dtype)
+            for dtype in (jnp.float32, jnp.bfloat16)
+        ],
         10**9,
         "low",
         in_hbm=(1,),
@@ -337,20 +341,20 @@
             pltpu.SemaphoreType.DMA((LOW_STEPS,)),
         ],
     )
-    lows = [low] + [send(low, "tensor", shift) for shift in range(1, parts)]
+    lows = [low] + [swap(low_sent, "tensor", distance) for distance in range(1, parts)]
     *terms, low_grads = call(
         functools.partial(product_kernel, peers, local_slots, parts),
         scalars,
         (*lows, normed_input, query_gradient),
         [
-            jax.ShapeDtypeStruct((2 * share, width), jnp.float32 if shift == 0 else jnp.bfloat16)
-            for shift in range(peers)
+            jax.ShapeDtypeStruct((2 * share, width), jnp.bfloat16 if distance else jnp.float32)
+            for distance in range(peers)
         ]
         + [jax.ShapeDtypeStruct((rank, row_count), jnp.bfloat16)],
         10**9,
         "product",
     )
-    received = [send(terms[shift], "dp", shift) for shift in range(1, peers)]
+    received = [swap(terms[distance], "dp", distance) for distance in range(1, peers)]
     input_gradient = call(
         functools.partial(input_kernel, peers, local_slots),
         scalars,

time: 42.2 us -> 42.7 us (1.012)
  waiting for transfers between devices: 7.86 us -> 9.85 us
  starting transfers between devices: 13.4 us -> 12.1 us
    ppermute x9, waiting for transfers between devices: 7.86 us -> 9.85 us  [swap(): return lax.ppermute(array, axis, [(i, i ^ distance) for i in range(size)])]
    ppermute x9, starting transfers between devices: 13.4 us -> 12.1 us  [swap(): return lax.ppermute(array, axis, [(i, i ^ distance) for i in range(size)])]
  transfers between devices with their start and end apart: 9 -> 9, of which waited for: 5 -> 5; matrix products, arithmetic and copies ran while one was open for 0% -> 0% of each run, Pallas kernels for 31% -> 30%
where the time goes in v4:
time: 42.7 us; the launch traced here: 42.5 us
  Pallas kernels  18.9 us (44%)
  starting transfers between devices  12.1 us (28%)
  waiting for transfers between devices  9.85 us (23%)
  between operations  0.79 us (2%)
  local copies, waits for them, and re-layouts  0.77 us (2%)
    ppermute x9, starting transfers between devices, swap(): return lax.ppermute(array, axis, [(i, i ^ distance) for i in range(size)])  12.1 us
    pallas_call x1, Pallas kernels, attention_backward(): pl.pallas_call(attention_kernel, in_specs=[vmem] * 5, out_specs=[pl.Block...  10.2 us
    ppermute x9, waiting for transfers between devices, swap(): return lax.ppermute(array, axis, [(i, i ^ distance) for i in range(size)])  9.85 us
    pallas_call x3, Pallas kernels, call(): pl.pallas_call(kernel, in_specs=[pl.BlockSpec(memory_space=pltpu.SMEM)] *...  6.66 us
    pallas_call x1, Pallas kernels, local(): pl.pallas_call(functools.partial(pack_kernel, row_count), in_specs=[pl.Bl...  2.09 us
  transfers between devices with their start and end apart: 9, of which 5 were waited for; matrix products, arithmetic and copies ran while one was open for 0% of the time, Pallas kernels for 30%

profile of v4, /device:TPU:0, one launch (start us, length us, event | category | flops | bytes accessed | tf_op | source)
XLA Modules:
  0.0 42.5 jit_solution(8609207782089764930)
XLA Ops:
  0.7 2.1 %pack.1 = (bf16[32,2048]{1,0:T(8,128)(2,1)S(1)}, f32[1152,128]{1,0:T(8,128)S(1)}) custom-call(s32[1,8]{1,0:T(1,128)} %len_ref.7, bf16[16,2048]{1,0:T(8,128)(2,1)} %bitcast.7, bf16[16,2048]{1,0:T(8,128)(2,1)} %bitcast.8), custom_call_target="tpu_custom_call" | custom-call | flops 10000000000 | bytes 1048576 | tf_op jit(solution)/shard_map/pack/pallas_call | solution.py:297
  2.8 5.1 %collective-permute-start.2 = (bf16[32,2048]{1,0:T(8,128)(2,1)S(1)}, bf16[32,2048]{1,0:T(8,128)(2,1)S(1)}, u32[]{:S(2)}, u32[]{:S(2)}) collective-permute-start(bf16[32,2048]{1,0:T(8,128)(2,1)S(1)} %get-tuple-element.19.refs_0_), channel_id=1, source_target_pairs={{0,12},{4,8},{8,4},{12,0},{1,13},{5,9},{9,5},{13,1},{2,14},{6,10},... | collective-permute-start | bytes 393224 | tf_op jit(solution)/shard_map/ppermute | solution.py:275
  7.9 0.6 %collective-permute-start = (bf16[32,2048]{1,0:T(8,128)(2,1)S(1)}, bf16[32,2048]{1,0:T(8,128)(2,1)S(1)}, u32[]{:S(2)}, u32[]{:S(2)}) collective-permute-start(bf16[32,2048]{1,0:T(8,128)(2,1)S(1)} %get-tuple-element.19.refs_0_), channel_id=1, source_target_pairs={{0,4},{4,0},{8,12},{12,8},{1,5},{5,1},{9,13},{13,9},{2,6},{6,2},{1... | collective-permute-start | bytes 393224 | tf_op jit(solution)/shard_map/ppermute | solution.py:275
  8.5 0.0 copy-start
  8.6 0.0 copy-start.2
  8.6 0.0 copy-start.3
  8.6 0.0 copy-start.4
  8.6 10.2 %attention_backward.1 = (bf16[2048,512]{1,0:T(8,128)(2,1)}, bf16[512,256]{1,0:T(8,128)(2,1)}, bf16[512,256]{1,0:T(8,128)(2,1)}) custom-call(f32[1152,128]{1,0:T(8,128)S(1)} %get-tuple-element.17.bias_ref, bf16[512,2048]{1,0:T(8,128)(2,1)S(1)} %copy-done.5, bf16[512,2048]{1,0:T(8,128)(2,1)S(1)} %copy-done.6, bf16[512,256]{1,0:T(8,128)(2,1)S(1)} %copy-done.7, ...), custom_call_target="tpu_custom_call" | custom-call | flops 8000000000 | bytes 8388608 | tf_op jit(solution)/shard_map/attention_backward/pallas_call | solution.py:134
  18.8 0.2 collective-permute-done.1.refs_2_
  19.0 2.4 %low.1 = (f32[32,512]{1,0:T(8,128)S(1)}, bf16[32,512]{1,0:T(8,128)(2,1)S(1)}) custom-call(s32[1,8]{1,0:T(1,128)S(1)} %copy-done.2, s32[1,8]{1,0:T(1,128)S(1)} %copy-done.3, s32[4]{0:T(128)S(1)} %copy-done.4, s32[1]{0:T(128)} %bitcast.me_ref, bf16[512,2048]{1,0:T(8,128)(2,1)S(1)} %copy-done, bf16[2048,512]{1,0:T(8,128)(2,1)} %get-tuple-element.18.gq_hbm.refs_5_, ...), custom_call_target="tpu_custom_call" | custom-call | flops 1000000000 | bytes 4194304 | tf_op jit(solution)/shard_map/low/pallas_call | solution.py:257
  21.4 0.3 collective-permute-start.5
  21.7 1.3 %collective-permute-start.4 = (bf16[32,512]{1,0:T(8,128)(2,1)S(1)}, bf16[32,512]{1,0:T(8,128)(2,1)S(1)}, u32[]{:S(2)}, u32[]{:S(2)}) collective-permute-start(bf16[32,512]{1,0:T(8,128)(2,1)S(1)} %get-tuple-element.21), channel_id=1, source_target_pairs={{0,2},{1,3},{2,0},{3,1},{4,6},{5,7},{6,4},{7,5},{8,10},{9,11},{10,... | collective-permute-start | bytes 98312 | tf_op jit(solution)/shard_map/ppermute | solution.py:275
  23.0 0.3 collective-permute-start.3
  23.3 1.8 %collective-permute-done.5.refs_3_ = bf16[32,512]{1,0:T(8,128)(2,1)S(1)} collective-permute-done((bf16[32,512]{1,0:T(8,128)(2,1)S(1)}, bf16[32,512]{1,0:T(8,128)(2,1)S(1)}, u32[]{:S(2)}, u32[]{:S(2)}) %collective-permute-start.5) | collective-permute-done | bytes 32800 | tf_op jit(solution)/shard_map/ppermute | solution.py:275
  25.1 0.5 %collective-permute-done.4.refs_2_ = bf16[32,512]{1,0:T(8,128)(2,1)S(1)} collective-permute-done((bf16[32,512]{1,0:T(8,128)(2,1)S(1)}, bf16[32,512]{1,0:T(8,128)(2,1)S(1)}, u32[]{:S(2)}, u32[]{:S(2)}) %collective-permute-start.4) | collective-permute-done | bytes 32800 | tf_op jit(solution)/shard_map/ppermute | solution.py:275
  25.6 1.7 %product.1 = (f32[32,2048]{1,0:T(8,128)S(1)}, bf16[32,2048]{1,0:T(8,128)(2,1)S(1)}, bf16[32,2048]{1,0:T(8,128)(2,1)S(1)}, bf16[32,2048]{1,0:T(8,128)(2,1)S(1)}, bf16[16,512]{1,0:T(8,128)(2,1)S(1)}) custom-call(s32[1,8]{1,0:T(1,128)S(1)} %copy-done.2, s32[1,8]{1,0:T(1,128)S(1)} %copy-done.3, s32[4]{0:T(128)S(1)} %copy-done.4, s32[1]{0:T(128)} %bitcast.me_ref, ...), custom_call_target="tpu_custom_call" | custom-call | flops 1000000000 | bytes 4194304 | tf_op jit(solution)/shard_map/product/pallas_call | solution.py:257
  27.3 1.5 %collective-permute-start.6 = (bf16[32,2048]{1,0:T(8,128)(2,1)S(1)}, bf16[32,2048]{1,0:T(8,128)(2,1)S(1)}, u32[]{:S(2)}, u32[]{:S(2)}) collective-permute-start(bf16[32,2048]{1,0:T(8,128)(2,1)S(1)} %get-tuple-element.26), channel_id=1, source_target_pairs={{0,4},{4,0},{8,12},{12,8},{1,5},{5,1},{9,13},{13,9},{2,6},{6,2},{1... | collective-permute-start | bytes 393224 | tf_op jit(solution)/shard_map/ppermute | solution.py:275
  28.8 2.6 %collective-permute-start.7 = (bf16[32,2048]{1,0:T(8,128)(2,1)S(1)}, bf16[32,2048]{1,0:T(8,128)(2,1)S(1)}, u32[]{:S(2)}, u32[]{:S(2)}) collective-permute-start(bf16[32,2048]{1,0:T(8,128)(2,1)S(1)} %get-tuple-element.27), channel_id=1, source_target_pairs={{0,8},{4,12},{8,0},{12,4},{1,9},{5,13},{9,1},{13,5},{2,10},{6,14},... | collective-permute-start | bytes 393224 | tf_op jit(solution)/shard_map/ppermute | solution.py:275
  31.4 0.4 collective-permute-start.8
  31.7 2.6 %input_gradient.1 = bf16[512,2048]{1,0:T(8,128)(2,1)} custom-call(s32[1,8]{1,0:T(1,128)S(1)} %copy-done.2, s32[1,8]{1,0:T(1,128)S(1)} %copy-done.3, s32[4]{0:T(128)S(1)} %copy-done.4, s32[1]{0:T(128)} %bitcast.me_ref, bf16[16,512]{1,0:T(8,128)(2,1)S(1)} %get-tuple-element.22.low_ref, bf16[32,2048]{1,0:T(8,128)(2,1)S(1)} %get-tuple-element.19.refs_0_, ...), custom_call_target="tpu_custom_call" | custom-call | flops 1000000000 | bytes 4194304 | tf_op jit(solution)/shard_map/input_gradient/pallas_call | solution.py:257
  34.4 0.7 %collective-permute-done.6 = bf16[32,2048]{1,0:T(8,128)(2,1)S(1)} collective-permute-done((bf16[32,2048]{1,0:T(8,128)(2,1)S(1)}, bf16[32,2048]{1,0:T(8,128)(2,1)S(1)}, u32[]{:S(2)}, u32[]{:S(2)}) %collective-permute-start.6) | collective-permute-done | bytes 131104 | tf_op jit(solution)/shard_map/ppermute | solution.py:275
  35.0 6.7 %collective-permute-done.7 = bf16[32,2048]{1,0:T(8,128)(2,1)S(1)} collective-permute-done((bf16[32,2048]{1,0:T(8,128)(2,1)S(1)}, bf16[32,2048]{1,0:T(8,128)(2,1)S(1)}, u32[]{:S(2)}, u32[]{:S(2)}) %collective-permute-start.7) | collective-permute-done | bytes 131104 | tf_op jit(solution)/shard_map/ppermute | solution.py:275
  41.7 0.1 convert_add_fusion
  41.8 0.7 %slice_bitcast_fusion = (f32[1,16,2048]{2,1,0:T(8,128)}, f32[1,16,2048]{2,1,0:T(8,128)}) fusion(f32[32,2048]{1,0:T(8,128)S(1)} %convert_add_fusion), kind=kLoop, calls=%fused_computation.1 | loop fusion | bytes 524288 | tf_op jit(solution)/shard_map/reshape | solution.py:370
  (19 shorter events, 0.0 us)
Async XLA Ops:
  0.6 7.9 %copy-start.5 = (bf16[512,2048]{1,0:T(8,128)(2,1)S(1)}, bf16[512,2048]{1,0:T(8,128)(2,1)}, u32[]{:S(2)}) copy-start(bf16[512,2048]{1,0:T(8,128)(2,1)} %q_ref.1) | copy-start | bytes 6291460
  0.6 7.9 %copy-start.6 = (bf16[512,2048]{1,0:T(8,128)(2,1)S(1)}, bf16[512,2048]{1,0:T(8,128)(2,1)}, u32[]{:S(2)}) copy-start(bf16[512,2048]{1,0:T(8,128)(2,1)} %g_ref.1) | copy-start | bytes 6291460
  0.7 7.9 %copy-start.7 = (bf16[512,256]{1,0:T(8,128)(2,1)S(1)}, bf16[512,256]{1,0:T(8,128)(2,1)}, u32[]{:S(2)}) copy-start(bf16[512,256]{1,0:T(8,128)(2,1)} %k_ref.1) | copy-start | bytes 786436
  0.7 7.9 %copy-start.8 = (bf16[512,256]{1,0:T(8,128)(2,1)S(1)}, bf16[512,256]{1,0:T(8,128)(2,1)}, u32[]{:S(2)}) copy-start(bf16[512,256]{1,0:T(8,128)(2,1)} %v_ref.1) | copy-start | bytes 786436
  2.8 16.0 %collective-permute-start.2 = (bf16[32,2048]{1,0:T(8,128)(2,1)S(1)}, bf16[32,2048]{1,0:T(8,128)(2,1)S(1)}, u32[]{:S(2)}, u32[]{:S(2)}) collective-permute-start(bf16[32,2048]{1,0:T(8,128)(2,1)S(1)} %get-tuple-element.19.refs_0_), channel_id=1, source_target_pairs={{0,12},{4,8},{8,4},{12,0},{1,13},{5,9},{9,5},{13,1},{2,14},{6,10},... | collective-permute-start | bytes 393224 | tf_op jit(solution)/shard_map/ppermute | solution.py:275
  7.9 11.1 %collective-permute-start.1 = (bf16[32,2048]{1,0:T(8,128)(2,1)S(1)}, bf16[32,2048]{1,0:T(8,128)(2,1)S(1)}, u32[]{:S(2)}, u32[]{:S(2)}) collective-permute-start(bf16[32,2048]{1,0:T(8,128)(2,1)S(1)} %get-tuple-element.19.refs_0_), channel_id=1, source_target_pairs={{0,8},{4,12},{8,0},{12,4},{1,9},{5,13},{9,1},{13,5},{2,10},{6,14},... | collective-permute-start | bytes 393224 | tf_op jit(solution)/shard_map/ppermute | solution.py:275
  7.9 11.1 %collective-permute-start = (bf16[32,2048]{1,0:T(8,128)(2,1)S(1)}, bf16[32,2048]{1,0:T(8,128)(2,1)S(1)}, u32[]{:S(2)}, u32[]{:S(2)}) collective-permute-start(bf16[32,2048]{1,0:T(8,128)(2,1)S(1)} %get-tuple-element.19.refs_0_), channel_id=1, source_target_pairs={{0,4},{4,0},{8,12},{12,8},{1,5},{5,1},{9,13},{13,9},{2,6},{6,2},{1... | collective-permute-start | bytes 393224 | tf_op jit(solution)/shard_map/ppermute | solution.py:275
  8.5 10.4 %copy-start = (bf16[512,2048]{1,0:T(8,128)(2,1)S(1)}, bf16[512,2048]{1,0:T(8,128)(2,1)}, u32[]{:S(2)}) copy-start(bf16[512,2048]{1,0:T(8,128)(2,1)} %refs_4_.1) | copy-start | bytes 6291460
  8.6 10.4 %copy-start.2 = (s32[1,8]{1,0:T(1,128)S(1)}, s32[1,8]{1,0:T(1,128)}, u32[]{:S(2)}) copy-start(s32[1,8]{1,0:T(1,128)} %len_ref.7) | copy-start | bytes 100
  8.6 10.4 %copy-start.3 = (s32[1,8]{1,0:T(1,128)S(1)}, s32[1,8]{1,0:T(1,128)}, u32[]{:S(2)}) copy-start(s32[1,8]{1,0:T(1,128)} %adapter_ref.5) | copy-start | bytes 100
  8.6 10.4 %copy-start.4 = (s32[4]{0:T(128)S(1)}, s32[4]{0:T(128)}, u32[]{:S(2)}) copy-start(s32[4]{0:T(128)} %slot_ref.5) | copy-start | bytes 52
  19.0 6.6 %copy-start.1 = (bf16[2048,512]{1,0:T(8,128)(2,1)S(1)}, bf16[2048,512]{1,0:T(8,128)(2,1)}, u32[]{:S(2)}) copy-start(bf16[2048,512]{1,0:T(8,128)(2,1)} %get-tuple-element.18.gq_hbm.refs_5_) | copy-start | bytes 6291460
  21.4 3.7 %collective-permute-start.5 = (bf16[32,512]{1,0:T(8,128)(2,1)S(1)}, bf16[32,512]{1,0:T(8,128)(2,1)S(1)}, u32[]{:S(2)}, u32[]{:S(2)}) collective-permute-start(bf16[32,512]{1,0:T(8,128)(2,1)S(1)} %get-tuple-element.21), channel_id=1, source_target_pairs={{0,3},{1,2},{2,1},{3,0},{4,7},{5,6},{6,5},{7,4},{8,11},{9,10},{10,... | collective-permute-start | bytes 98312 | tf_op jit(solution)/shard_map/ppermute | solution.py:275
  21.7 3.9 %collective-permute-start.4 = (bf16[32,512]{1,0:T(8,128)(2,1)S(1)}, bf16[32,512]{1,0:T(8,128)(2,1)S(1)}, u32[]{:S(2)}, u32[]{:S(2)}) collective-permute-start(bf16[32,512]{1,0:T(8,128)(2,1)S(1)} %get-tuple-element.21), channel_id=1, source_target_pairs={{0,2},{1,3},{2,0},{3,1},{4,6},{5,7},{6,4},{7,5},{8,10},{9,11},{10,... | collective-permute-start | bytes 98312 | tf_op jit(solution)/shard_map/ppermute | solution.py:275
  23.0 2.6 %collective-permute-start.3 = (bf16[32,512]{1,0:T(8,128)(2,1)S(1)}, bf16[32,512]{1,0:T(8,128)(2,1)S(1)}, u32[]{:S(2)}, u32[]{:S(2)}) collective-permute-start(bf16[32,512]{1,0:T(8,128)(2,1)S(1)} %get-tuple-element.21), channel_id=1, source_target_pairs={{0,1},{1,0},{2,3},{3,2},{4,5},{5,4},{6,7},{7,6},{8,9},{9,8},{10,11... | collective-permute-start | bytes 98312 | tf_op jit(solution)/shard_map/ppermute | solution.py:275
  27.3 7.7 %collective-permute-start.6 = (bf16[32,2048]{1,0:T(8,128)(2,1)S(1)}, bf16[32,2048]{1,0:T(8,128)(2,1)S(1)}, u32[]{:S(2)}, u32[]{:S(2)}) collective-permute-start(bf16[32,2048]{1,0:T(8,128)(2,1)S(1)} %get-tuple-element.26), channel_id=1, source_target_pairs={{0,4},{4,0},{8,12},{12,8},{1,5},{5,1},{9,13},{13,9},{2,6},{6,2},{1... | collective-permute-start | bytes 393224 | tf_op jit(solution)/shard_map/ppermute | solution.py:275
  28.8 12.9 %collective-permute-start.7 = (bf16[32,2048]{1,0:T(8,128)(2,1)S(1)}, bf16[32,2048]{1,0:T(8,128)(2,1)S(1)}, u32[]{:S(2)}, u32[]{:S(2)}) collective-permute-start(bf16[32,2048]{1,0:T(8,128)(2,1)S(1)} %get-tuple-element.27), channel_id=1, source_target_pairs={{0,8},{4,12},{8,0},{12,4},{1,9},{5,13},{9,1},{13,5},{2,10},{6,14},... | collective-permute-start | bytes 393224 | tf_op jit(solution)/shard_map/ppermute | solution.py:275
  31.4 10.3 %collective-permute-start.8 = (bf16[32,2048]{1,0:T(8,128)(2,1)S(1)}, bf16[32,2048]{1,0:T(8,128)(2,1)S(1)}, u32[]{:S(2)}, u32[]{:S(2)}) collective-permute-start(bf16[32,2048]{1,0:T(8,128)(2,1)S(1)} %get-tuple-element.28), channel_id=1, source_target_pairs={{0,12},{4,8},{8,4},{12,0},{1,13},{5,9},{9,5},{13,1},{2,14},{6,10},... | collective-permute-start | bytes 393224 | tf_op jit(solution)/shard_map/ppermute | solution.py:275

commit v5 on v4

--- a/solution.py
+++ b/solution.py
@@ -38,28 +38,92 @@
     ]
 
 
-def pack_kernel(row_count, len_ref, down_hbm, up_hbm, own_ref, bias_ref, sems):
+def pack_kernel(
+    row_count,
+    peers,
+    len_hbm,
+    adapter_hbm,
+    slot_hbm,
+    down_hbm,
+    up_hbm,
+    own_ref,
+    bias_ref,
+    mask_ref,
+    len_ref,
+    adapter_ref,
+    slot_ref,
+    sems,
+):
     share = down_hbm.shape[0]
+    local_slots = slot_hbm.shape[0] // peers
+    pairs = (
+        (len_hbm, len_ref),
+        (adapter_hbm, adapter_ref),
+        (slot_hbm, slot_ref),
+        (down_hbm, own_ref.at[:share]),
+        (up_hbm, own_ref.at[share:]),
+    )
     copies = [
-        pltpu.make_async_copy(down_hbm, own_ref.at[:share], sems.at[0]),
-        pltpu.make_async_copy(up_hbm, own_ref.at[share:], sems.at[1]),
+        pltpu.make_async_copy(source, target, sems.at[index])
+        for index, (source, target) in enumerate(pairs)
     ]
     for copy in copies:
         copy.start()
+    for copy in copies[:3]:
+        copy.wait()
+    lengths = [len_ref[0, index] for index in range(len_ref.shape[1] - 1)]
+
+    token = lax.broadcasted_iota(jnp.int32, (1, row_count), 1)
+    adapter = jnp.full((1, row_count), adapter_ref[0, 0], jnp.int32)
+    begin = jnp.zeros((1, row_count), jnp.int32)
+    end = jnp.int32(0)
+    for index, length in enumerate(lengths):
+        end = end + length
+        adapter = jnp.where(token >= end, adapter_ref[0, index + 1], adapter)
+        begin = jnp.where(token >= end, end, begin)
+    me = lax.axis_index("dp")
+    for distance in range(peers):
+        for own in range(local_slots):
+            row = distance * local_slots + own
+            held = slot_ref[(me ^ distance) * local_slots + own]
+            mask_ref[row : row + 1, :] = jnp.where(adapter == held, 1.0, 0.0)
     at = 0
     for first, low, high in query_spans(row_count):
         width = high - low
         query = lax.broadcasted_iota(jnp.int32, (1, BLOCK), 1) + first
-        start = jnp.zeros((1, BLOCK), jnp.int32)
-        end = jnp.int32(0)
-        for index in range(len_ref.shape[1] - 1):
-            end = end + len_ref[0, index]
-            start = jnp.where(query >= end, end, start)
+        start = begin[:, first : first + BLOCK]
         key = lax.broadcasted_iota(jnp.int32, (width, BLOCK), 0) + low
         bias_ref[at : at + width, :] = jnp.where((key >= start) & (key <= query), 0.0, MASKED)
         at += width
-    for copy in copies:
+    for copy in copies[3:]:
         copy.wait()
+
+
+def pack(row_count, peers, lengths, adapters, slots, down, up):
+    pair_rows = sum(high - low for _, low, high in query_spans(row_count))
+    arrays = [
+        pltpu.with_memory_space_constraint(array, pltpu.HBM)
+        for array in (lengths, adapters, slots, down, up)
+    ]
+    return pl.pallas_call(
+        functools.partial(pack_kernel, row_count, peers),
+        in_specs=[pl.BlockSpec(memory_space=pltpu.HBM)] * 5,
+        out_specs=[pl.BlockSpec(memory_space=pltpu.VMEM)] * 3,
+        out_shape=[
+            jax.ShapeDtypeStruct((2 * down.shape[0], down.shape[1]), down.dtype),
+            jax.ShapeDtypeStruct((pair_rows, BLOCK), jnp.float32),
+            jax.ShapeDtypeStruct((slots.shape[0], row_count), jnp.float32),
+        ],
+        scratch_shapes=[
+            pltpu.SMEM(lengths.shape, jnp.int32),
+            pltpu.SMEM(adapters.shape, jnp.int32),
+            pltpu.SMEM(slots.shape, jnp.int32),
+            pltpu.SemaphoreType.DMA((5,)),
+        ],
+        compiler_params=pltpu.CompilerParams(vmem_limit_bytes=VMEM_BYTES),
+        cost_estimate=pl.CostEstimate(flops=10**10, bytes_accessed=2**20, transcendentals=0),
+        name="pack",
+    )(*arrays)
 
 
 def attention_kernel(
@@ -152,33 +216,21 @@
     )(bias, queries, output_gradient, keys, values)
 
 
-def slot_masks(len_ref, adapter_ref, slot_ref, row_count, slots):
-    token = lax.broadcasted_iota(jnp.int32, (1, row_count), 1)
-    adapter = jnp.full((1, row_count), adapter_ref[0, 0], jnp.int32)
-    end = jnp.int32(0)
-    for index in range(len_ref.shape[1] - 1):
-        end = end + len_ref[0, index]
-        adapter = jnp.where(token >= end, adapter_ref[0, index + 1], adapter)
-    return [adapter == slot_ref[slot] for slot in slots]
-
-
-def peer_slots(me, peers, local_slots):
-    return [
-        (me ^ distance) * local_slots + own
-        for distance in range(peers)
-        for own in range(local_slots)
-    ]
-
-
-def select(wide, masks, rank):
+def select(wide, mask_ref, rank):
     total = None
-    for index, mask in enumerate(masks):
-        part = jnp.where(mask, wide[index * rank : (index + 1) * rank], 0.0)
+    for slot in range(mask_ref.shape[0]):
+        part = wide[slot * rank : (slot + 1) * rank] * mask_ref[slot : slot + 1, :]
         total = part if total is None else total + part
     return total
 
 
-def low_kernel(peers, local_slots, len_ref, adapter_ref, slot_ref, me_ref, x_ref, gq_hbm, *refs):
+def spread(low, mask_ref):
+    return jnp.concatenate(
+        [low * mask_ref[slot : slot + 1, :] for slot in range(mask_ref.shape[0])], axis=0
+    ).astype(jnp.bfloat16)
+
+
+def low_kernel(peers, local_slots, mask_ref, x_ref, gq_hbm, *refs):
     factors, (out_ref, sent_ref, gq_ref, sems) = refs[:peers], refs[peers:]
     step = gq_ref.shape[0] // LOW_STEPS
     pieces = [pl.ds(index * step, step) for index in range(LOW_STEPS)]
@@ -190,30 +242,19 @@
         copy.start()
     rank = factors[0].shape[0] // (2 * local_slots)
     share = rank * local_slots
-    row_count = x_ref.shape[0]
-    masks = slot_masks(
-        len_ref, adapter_ref, slot_ref, row_count, peer_slots(me_ref[0], peers, local_slots)
-    )
     down = jnp.concatenate([ref[:share] for ref in factors], axis=0)
-    out_ref[:rank] = select(mxu(down, x_ref[...], NT), masks, rank)
+    out_ref[:rank] = select(mxu(down, x_ref[...], NT), mask_ref, rank)
     total = None
     for piece, copy in zip(pieces, copies):
         up = jnp.concatenate([ref[share:, piece] for ref in factors], axis=0)
         copy.wait()
         part = mxu(up, gq_ref[piece], NN)
         total = part if total is None else total + part
-    out_ref[rank:] = select(total, masks, rank)
+    out_ref[rank:] = select(total, mask_ref, rank)
     sent_ref[...] = out_ref[...].astype(jnp.bfloat16)
 
 
-def spread(low, masks):
-    zero = jnp.zeros_like(low)
-    return jnp.concatenate([jnp.where(mask, low, zero) for mask in masks], axis=0).astype(
-        jnp.bfloat16
-    )
-
-
-def product_kernel(peers, local_slots, parts, len_ref, adapter_ref, slot_ref, me_ref, *refs):
+def product_kernel(peers, local_slots, parts, mask_ref, *refs):
     lows, (x_ref, gq_ref), outs = refs[:parts], refs[parts : parts + 2], refs[parts + 2 :]
     low = lows[0][...]
     for ref in lows[1:]:
@@ -221,14 +262,7 @@
     rank = low.shape[0] // 2
     share = rank * local_slots
     low = low.astype(jnp.bfloat16).astype(jnp.float32)
-    masks = slot_masks(
-        len_ref,
-        adapter_ref,
-        slot_ref,
-        x_ref.shape[0],
-        peer_slots(me_ref[0], peers, local_slots),
-    )
-    wide_in, wide_grad = spread(low[:rank], masks), spread(low[rank:], masks)
+    wide_in, wide_grad = spread(low[:rank], mask_ref), spread(low[rank:], mask_ref)
     down = mxu(wide_grad, x_ref[...], NN) * ADAPTER_SCALE
     up = mxu(wide_in, gq_ref[...], NT) * ADAPTER_SCALE
     for distance, ref in enumerate(outs[:peers]):
@@ -238,26 +272,18 @@
     outs[peers][...] = low[rank:].astype(jnp.bfloat16)
 
 
-def input_kernel(peers, local_slots, len_ref, adapter_ref, slot_ref, me_ref, low_ref, *refs):
+def input_kernel(peers, local_slots, mask_ref, low_ref, *refs):
     factors, out_ref = refs[:peers], refs[peers]
     rank = low_ref.shape[0]
-    masks = slot_masks(
-        len_ref,
-        adapter_ref,
-        slot_ref,
-        low_ref.shape[1],
-        peer_slots(me_ref[0], peers, local_slots),
-    )
-    wide = spread(low_ref[...].astype(jnp.float32), masks)
+    wide = spread(low_ref[...].astype(jnp.float32), mask_ref)
     down = jnp.concatenate([ref[: rank * local_slots] for ref in factors], axis=0)
     out_ref[...] = (mxu(wide, down, TN) * ADAPTER_SCALE).astype(jnp.bfloat16)
 
 
-def call(kernel, scalars, arrays, out_shape, flops, name, in_hbm=(), scratch=()):
+def call(kernel, arrays, out_shape, flops, name, in_hbm=(), scratch=()):
     return pl.pallas_call(
         kernel,
-        in_specs=[pl.BlockSpec(memory_space=pltpu.SMEM)] * len(scalars)
-        + [
+        in_specs=[
             pl.BlockSpec(memory_space=pltpu.HBM if index in in_hbm else pltpu.VMEM)
             for index in range(len(arrays))
         ],
@@ -267,7 +293,7 @@
         compiler_params=pltpu.CompilerParams(vmem_limit_bytes=VMEM_BYTES),
         cost_estimate=pl.CostEstimate(flops=flops, bytes_accessed=4 * 2**20, transcendentals=0),
         name=name,
-    )(*scalars, *arrays)
+    )(*arrays)
 
 
 def swap(array, axis, distance):
@@ -291,31 +317,14 @@
     local_slots, rank, _ = down_weight.shape
     share = local_slots * rank
     peers, parts = lax.axis_size("dp"), lax.axis_size("tensor")
-    me = lax.axis_index("dp").astype(jnp.int32).reshape(1)
-    scalars = (document_length, document_adapter, adapter_in_slot, me)
-    pair_rows = sum(high - low for _, low, high in query_spans(row_count))
-    own, bias = pl.pallas_call(
-        functools.partial(pack_kernel, row_count),
-        in_specs=[pl.BlockSpec(memory_space=pltpu.SMEM)]
-        + [pl.BlockSpec(memory_space=pltpu.HBM)] * 2,
-        out_specs=[pl.BlockSpec(memory_space=pltpu.VMEM)] * 2,
-        out_shape=[
-            jax.ShapeDtypeStruct((2 * share, width), down_weight.dtype),
-            jax.ShapeDtypeStruct((pair_rows, BLOCK), jnp.float32),
-        ],
-        scratch_shapes=[pltpu.SemaphoreType.DMA((2,))],
-        compiler_params=pltpu.CompilerParams(vmem_limit_bytes=VMEM_BYTES),
-        cost_estimate=pl.CostEstimate(flops=10**10, bytes_accessed=2**20, transcendentals=0),
-        name="pack",
-    )(
-        *(
-            pltpu.with_memory_space_constraint(array, pltpu.HBM)
-            for array in (
-                document_length,
-                down_weight.reshape(share, width),
-                up_weight.reshape(share, width),
-            )
-        )
+    own, bias, mask = pack(
+        row_count,
+        peers,
+        document_length,
+        document_adapter,
+        adapter_in_slot,
+        down_weight.reshape(share, width),
+        up_weight.reshape(share, width),
     )
     factors = [own] + [swap(own, "dp", distance) for distance in range(1, peers)]
     query_gradient, key_gradient, value_gradient = attention_backward(
@@ -323,8 +332,8 @@
     )
     low, low_sent = call(
         functools.partial(low_kernel, peers, local_slots),
-        scalars,
         (
+            mask,
             normed_input,
             pltpu.with_memory_space_constraint(query_gradient, pltpu.HBM),
             *factors,
@@ -335,7 +344,7 @@
         ],
         10**9,
         "low",
-        in_hbm=(1,),
+        in_hbm=(2,),
         scratch=[
             pltpu.VMEM((width, row_count), jnp.bfloat16),
             pltpu.SemaphoreType.DMA((LOW_STEPS,)),
@@ -344,8 +353,7 @@
     lows = [low] + [swap(low_sent, "tensor", distance) for distance in range(1, parts)]
     *terms, low_grads = call(
         functools.partial(product_kernel, peers, local_slots, parts),
-        scalars,
-        (*lows, normed_input, query_gradient),
+        (mask, *lows, normed_input, query_gradient),
         [
             jax.ShapeDtypeStruct((2 * share, width), jnp.bfloat16 if distance else jnp.float32)
             for distance in range(peers)
@@ -354,11 +362,10 @@
         10**9,
         "product",
     )
-    received = [swap(terms[distance], "dp", distance) for distance in range(1, peers)]
+    received = [swap(terms[distance], "dp", distance) for distance in reversed(range(1, peers))]
     input_gradient = call(
         functools.partial(input_kernel, peers, local_slots),
-        scalars,
-        (low_grads, *factors),
+        (mask, low_grads, *factors),
         jax.ShapeDtypeStruct((row_count, width), jnp.bfloat16),
         10**9,
         "input_gradient",

time: 42.7 us -> 41 us (0.960)
  Pallas kernels: 18.9 us -> 16.3 us
  waiting for transfers between devices: 9.85 us -> 10.9 us
    pallas_call x4, Pallas kernels: 8.75 us -> 6.14 us  [the longest x3 5.07 us: call(): pl.pallas_call(kernel, in_specs=[pl.BlockSpec(memory_space=pltpu.HBM if i...]
    ppermute x9, waiting for transfers between devices: 9.85 us -> 10.9 us  [swap(): return lax.ppermute(array, axis, [(i, i ^ distance) for i in range(size)])]
where the time goes in v5:
time: 41 us; the launch traced here: 40.9 us
  Pallas kernels  16.3 us (40%)
  starting transfers between devices  12.1 us (30%)
  waiting for transfers between devices  10.9 us (27%)
  local copies, waits for them, and re-layouts  0.74 us (2%)
  between operations  0.73 us (2%)
    ppermute x9, starting transfers between devices, swap(): return lax.ppermute(array, axis, [(i, i ^ distance) for i in range(size)])  12.1 us
    ppermute x9, waiting for transfers between devices, swap(): return lax.ppermute(array, axis, [(i, i ^ distance) for i in range(size)])  10.9 us
    pallas_call x1, Pallas kernels, attention_backward(): pl.pallas_call(attention_kernel, in_specs=[vmem] * 5, out_specs=[pl.Block...  10.2 us
    pallas_call x3, Pallas kernels, call(): pl.pallas_call(kernel, in_specs=[pl.BlockSpec(memory_space=pltpu.HBM if i...  5.07 us
    pallas_call x1, Pallas kernels, pack(): pl.pallas_call(functools.partial(pack_kernel, row_count, peers), in_specs...  1.07 us
  transfers between devices with their start and end apart: 9, of which 5 were waited for; matrix products, arithmetic and copies ran while one was open for 0% of the time, Pallas kernels for 30%

profile of v5, /device:TPU:0, one launch (start us, length us, event | category | flops | bytes accessed | tf_op | source)
XLA Modules:
  0.0 40.9 jit_solution(14939927389135080254)
XLA Ops:
  0.7 1.1 %pack.1 = (bf16[32,2048]{1,0:T(8,128)(2,1)S(1)}, f32[1152,128]{1,0:T(8,128)S(1)}, f32[4,512]{1,0:T(4,128)S(1)}) custom-call(s32[1,8]{1,0:T(1,128)} %len_hbm.1, s32[1,8]{1,0:T(1,128)} %adapter_hbm.1, s32[4]{0:T(128)} %slot_hbm.1, bf16[16,2048]{1,0:T(8,128)(2,1)} %bitcast.6, bf16[16,2048]{1,0:T(8,128)(2,1)} %bitcast.7), custom_call_target="tpu_custom_call" | custom-call | flops 10000000000 | bytes 1048576 | tf_op jit(solution)/shard_map/pack/pallas_call | solution.py:108
  1.8 5.1 %collective-permute-start.2 = (bf16[32,2048]{1,0:T(8,128)(2,1)S(1)}, bf16[32,2048]{1,0:T(8,128)(2,1)S(1)}, u32[]{:S(2)}, u32[]{:S(2)}) collective-permute-start(bf16[32,2048]{1,0:T(8,128)(2,1)S(1)} %get-tuple-element.21.refs_0_), channel_id=1, source_target_pairs={{0,12},{4,8},{8,4},{12,0},{1,13},{5,9},{9,5},{13,1},{2,14},{6,10},... | collective-permute-start | bytes 393224 | tf_op jit(solution)/shard_map/ppermute | solution.py:301
  6.9 0.0 collective-permute-start.1
  6.9 0.6 %collective-permute-start = (bf16[32,2048]{1,0:T(8,128)(2,1)S(1)}, bf16[32,2048]{1,0:T(8,128)(2,1)S(1)}, u32[]{:S(2)}, u32[]{:S(2)}) collective-permute-start(bf16[32,2048]{1,0:T(8,128)(2,1)S(1)} %get-tuple-element.21.refs_0_), channel_id=1, source_target_pairs={{0,4},{4,0},{8,12},{12,8},{1,5},{5,1},{9,13},{13,9},{2,6},{6,2},{1... | collective-permute-start | bytes 393224 | tf_op jit(solution)/shard_map/ppermute | solution.py:301
  7.5 0.0 copy-start
  7.5 10.2 %attention_backward.1 = (bf16[2048,512]{1,0:T(8,128)(2,1)}, bf16[512,256]{1,0:T(8,128)(2,1)}, bf16[512,256]{1,0:T(8,128)(2,1)}) custom-call(f32[1152,128]{1,0:T(8,128)S(1)} %get-tuple-element.19.bias_ref, bf16[512,2048]{1,0:T(8,128)(2,1)S(1)} %copy-done.2, bf16[512,2048]{1,0:T(8,128)(2,1)S(1)} %copy-done.3, bf16[512,256]{1,0:T(8,128)(2,1)S(1)} %copy-done.4, ...), custom_call_target="tpu_custom_call" | custom-call | flops 8000000000 | bytes 8388608 | tf_op jit(solution)/shard_map/attention_backward/pallas_call | solution.py:198
  17.7 0.0 collective-permute-done.2.refs_3_
  17.7 0.2 collective-permute-done.1.refs_2_
  17.9 0.0 collective-permute-done.refs_1_
  18.0 1.9 %low.1 = (f32[32,512]{1,0:T(8,128)S(1)}, bf16[32,512]{1,0:T(8,128)(2,1)S(1)}) custom-call(f32[4,512]{1,0:T(4,128)S(1)} %get-tuple-element.18.mask_ref, bf16[512,2048]{1,0:T(8,128)(2,1)S(1)} %copy-done, bf16[2048,512]{1,0:T(8,128)(2,1)} %get-tuple-element.20.gq_hbm.refs_5_, bf16[32,2048]{1,0:T(8,128)(2,1)S(1)} %get-tuple-element.21.refs_0_, ...), custom_call_target="tpu_custom_call" | custom-call | flops 1000000000 | bytes 4194304 | tf_op jit(solution)/shard_map/low/pallas_call | solution.py:284
  19.9 0.3 collective-permute-start.5
  20.2 1.3 %collective-permute-start.4 = (bf16[32,512]{1,0:T(8,128)(2,1)S(1)}, bf16[32,512]{1,0:T(8,128)(2,1)S(1)}, u32[]{:S(2)}, u32[]{:S(2)}) collective-permute-start(bf16[32,512]{1,0:T(8,128)(2,1)S(1)} %get-tuple-element.23), channel_id=1, source_target_pairs={{0,2},{1,3},{2,0},{3,1},{4,6},{5,7},{6,4},{7,5},{8,10},{9,11},{10,... | collective-permute-start | bytes 98312 | tf_op jit(solution)/shard_map/ppermute | solution.py:301
  21.5 0.3 collective-permute-start.3
  21.8 1.8 %collective-permute-done.5.refs_3_ = bf16[32,512]{1,0:T(8,128)(2,1)S(1)} collective-permute-done((bf16[32,512]{1,0:T(8,128)(2,1)S(1)}, bf16[32,512]{1,0:T(8,128)(2,1)S(1)}, u32[]{:S(2)}, u32[]{:S(2)}) %collective-permute-start.5) | collective-permute-done | bytes 32800 | tf_op jit(solution)/shard_map/ppermute | solution.py:301
  23.6 0.5 %collective-permute-done.4.refs_2_ = bf16[32,512]{1,0:T(8,128)(2,1)S(1)} collective-permute-done((bf16[32,512]{1,0:T(8,128)(2,1)S(1)}, bf16[32,512]{1,0:T(8,128)(2,1)S(1)}, u32[]{:S(2)}, u32[]{:S(2)}) %collective-permute-start.4) | collective-permute-done | bytes 32800 | tf_op jit(solution)/shard_map/ppermute | solution.py:301
  24.1 0.0 collective-permute-done.3.refs_1_
  24.1 1.1 %product.1 = (f32[32,2048]{1,0:T(8,128)S(1)}, bf16[32,2048]{1,0:T(8,128)(2,1)S(1)}, bf16[32,2048]{1,0:T(8,128)(2,1)S(1)}, bf16[32,2048]{1,0:T(8,128)(2,1)S(1)}, bf16[16,512]{1,0:T(8,128)(2,1)S(1)}) custom-call(f32[4,512]{1,0:T(4,128)S(1)} %get-tuple-element.18.mask_ref, f32[32,512]{1,0:T(8,128)S(1)} %get-tuple-element.22.refs_0_, ...), custom_call_target="tpu_custom_call" | custom-call | flops 1000000000 | bytes 4194304 | tf_op jit(solution)/shard_map/product/pallas_call | solution.py:284
  25.2 3.5 %collective-permute-start.6 = (bf16[32,2048]{1,0:T(8,128)(2,1)S(1)}, bf16[32,2048]{1,0:T(8,128)(2,1)S(1)}, u32[]{:S(2)}, u32[]{:S(2)}) collective-permute-start(bf16[32,2048]{1,0:T(8,128)(2,1)S(1)} %get-tuple-element.28), channel_id=1, source_target_pairs={{0,12},{4,8},{8,4},{12,0},{1,13},{5,9},{9,5},{13,1},{2,14},{6,10},... | collective-permute-start | bytes 393224 | tf_op jit(solution)/shard_map/ppermute | solution.py:301
  28.7 1.0 %collective-permute-start.8 = (bf16[32,2048]{1,0:T(8,128)(2,1)S(1)}, bf16[32,2048]{1,0:T(8,128)(2,1)S(1)}, u32[]{:S(2)}, u32[]{:S(2)}) collective-permute-start(bf16[32,2048]{1,0:T(8,128)(2,1)S(1)} %get-tuple-element.30), channel_id=1, source_target_pairs={{0,4},{4,0},{8,12},{12,8},{1,5},{5,1},{9,13},{13,9},{2,6},{6,2},{1... | collective-permute-start | bytes 393224 | tf_op jit(solution)/shard_map/ppermute | solution.py:301
  29.7 2.0 %input_gradient.1 = bf16[512,2048]{1,0:T(8,128)(2,1)} custom-call(f32[4,512]{1,0:T(4,128)S(1)} %get-tuple-element.18.mask_ref, bf16[16,512]{1,0:T(8,128)(2,1)S(1)} %get-tuple-element.24.low_ref, bf16[32,2048]{1,0:T(8,128)(2,1)S(1)} %get-tuple-element.21.refs_0_, bf16[32,2048]{1,0:T(8,128)(2,1)S(1)} %collective-permute-done.refs_1_, ...), custom_call_target="tpu_custom_call" | custom-call | flops 1000000000 | bytes 4194304 | tf_op jit(solution)/shard_map/input_gradient/pallas_call | solution.py:284
  31.7 1.8 %collective-permute-done.6 = bf16[32,2048]{1,0:T(8,128)(2,1)S(1)} collective-permute-done((bf16[32,2048]{1,0:T(8,128)(2,1)S(1)}, bf16[32,2048]{1,0:T(8,128)(2,1)S(1)}, u32[]{:S(2)}, u32[]{:S(2)}) %collective-permute-start.6) | collective-permute-done | bytes 131104 | tf_op jit(solution)/shard_map/ppermute | solution.py:301
  33.5 6.6 %collective-permute-done.7 = bf16[32,2048]{1,0:T(8,128)(2,1)S(1)} collective-permute-done((bf16[32,2048]{1,0:T(8,128)(2,1)S(1)}, bf16[32,2048]{1,0:T(8,128)(2,1)S(1)}, u32[]{:S(2)}, u32[]{:S(2)}) %collective-permute-start.7) | collective-permute-done | bytes 131104 | tf_op jit(solution)/shard_map/ppermute | solution.py:301
  40.1 0.1 convert_add_fusion
  40.1 0.7 %slice_bitcast_fusion = (f32[1,16,2048]{2,1,0:T(8,128)}, f32[1,16,2048]{2,1,0:T(8,128)}) fusion(f32[32,2048]{1,0:T(8,128)S(1)} %convert_add_fusion), kind=kLoop, calls=%fused_computation.1 | loop fusion | bytes 524288 | tf_op jit(solution)/shard_map/reshape | solution.py:377
  (13 shorter events, 0.0 us)
Async XLA Ops:
  0.6 6.9 %copy-start.2 = (bf16[512,2048]{1,0:T(8,128)(2,1)S(1)}, bf16[512,2048]{1,0:T(8,128)(2,1)}, u32[]{:S(2)}) copy-start(bf16[512,2048]{1,0:T(8,128)(2,1)} %q_ref.1) | copy-start | bytes 6291460
  0.6 6.9 %copy-start.3 = (bf16[512,2048]{1,0:T(8,128)(2,1)S(1)}, bf16[512,2048]{1,0:T(8,128)(2,1)}, u32[]{:S(2)}) copy-start(bf16[512,2048]{1,0:T(8,128)(2,1)} %g_ref.1) | copy-start | bytes 6291460
  0.7 6.9 %copy-start.4 = (bf16[512,256]{1,0:T(8,128)(2,1)S(1)}, bf16[512,256]{1,0:T(8,128)(2,1)}, u32[]{:S(2)}) copy-start(bf16[512,256]{1,0:T(8,128)(2,1)} %k_ref.1) | copy-start | bytes 786436
  0.7 6.9 %copy-start.5 = (bf16[512,256]{1,0:T(8,128)(2,1)S(1)}, bf16[512,256]{1,0:T(8,128)(2,1)}, u32[]{:S(2)}) copy-start(bf16[512,256]{1,0:T(8,128)(2,1)} %v_ref.1) | copy-start | bytes 786436
  1.8 16.0 %collective-permute-start.2 = (bf16[32,2048]{1,0:T(8,128)(2,1)S(1)}, bf16[32,2048]{1,0:T(8,128)(2,1)S(1)}, u32[]{:S(2)}, u32[]{:S(2)}) collective-permute-start(bf16[32,2048]{1,0:T(8,128)(2,1)S(1)} %get-tuple-element.21.refs_0_), channel_id=1, source_target_pairs={{0,12},{4,8},{8,4},{12,0},{1,13},{5,9},{9,5},{13,1},{2,14},{6,10},... | collective-permute-start | bytes 393224 | tf_op jit(solution)/shard_map/ppermute | solution.py:301
  6.9 11.1 %collective-permute-start.1 = (bf16[32,2048]{1,0:T(8,128)(2,1)S(1)}, bf16[32,2048]{1,0:T(8,128)(2,1)S(1)}, u32[]{:S(2)}, u32[]{:S(2)}) collective-permute-start(bf16[32,2048]{1,0:T(8,128)(2,1)S(1)} %get-tuple-element.21.refs_0_), channel_id=1, source_target_pairs={{0,8},{4,12},{8,0},{12,4},{1,9},{5,13},{9,1},{13,5},{2,10},{6,14},... | collective-permute-start | bytes 393224 | tf_op jit(solution)/shard_map/ppermute | solution.py:301
  6.9 11.1 %collective-permute-start = (bf16[32,2048]{1,0:T(8,128)(2,1)S(1)}, bf16[32,2048]{1,0:T(8,128)(2,1)S(1)}, u32[]{:S(2)}, u32[]{:S(2)}) collective-permute-start(bf16[32,2048]{1,0:T(8,128)(2,1)S(1)} %get-tuple-element.21.refs_0_), channel_id=1, source_target_pairs={{0,4},{4,0},{8,12},{12,8},{1,5},{5,1},{9,13},{13,9},{2,6},{6,2},{1... | collective-permute-start | bytes 393224 | tf_op jit(solution)/shard_map/ppermute | solution.py:301
  7.5 10.4 %copy-start = (bf16[512,2048]{1,0:T(8,128)(2,1)S(1)}, bf16[512,2048]{1,0:T(8,128)(2,1)}, u32[]{:S(2)}) copy-start(bf16[512,2048]{1,0:T(8,128)(2,1)} %refs_4_.1) | copy-start | bytes 6291460
  17.9 6.2 %copy-start.1 = (bf16[2048,512]{1,0:T(8,128)(2,1)S(1)}, bf16[2048,512]{1,0:T(8,128)(2,1)}, u32[]{:S(2)}) copy-start(bf16[2048,512]{1,0:T(8,128)(2,1)} %get-tuple-element.20.gq_hbm.refs_5_) | copy-start | bytes 6291460
  19.9 3.7 %collective-permute-start.5 = (bf16[32,512]{1,0:T(8,128)(2,1)S(1)}, bf16[32,512]{1,0:T(8,128)(2,1)S(1)}, u32[]{:S(2)}, u32[]{:S(2)}) collective-permute-start(bf16[32,512]{1,0:T(8,128)(2,1)S(1)} %get-tuple-element.23), channel_id=1, source_target_pairs={{0,3},{1,2},{2,1},{3,0},{4,7},{5,6},{6,5},{7,4},{8,11},{9,10},{10,... | collective-permute-start | bytes 98312 | tf_op jit(solution)/shard_map/ppermute | solution.py:301
  20.2 3.9 %collective-permute-start.4 = (bf16[32,512]{1,0:T(8,128)(2,1)S(1)}, bf16[32,512]{1,0:T(8,128)(2,1)S(1)}, u32[]{:S(2)}, u32[]{:S(2)}) collective-permute-start(bf16[32,512]{1,0:T(8,128)(2,1)S(1)} %get-tuple-element.23), channel_id=1, source_target_pairs={{0,2},{1,3},{2,0},{3,1},{4,6},{5,7},{6,4},{7,5},{8,10},{9,11},{10,... | collective-permute-start | bytes 98312 | tf_op jit(solution)/shard_map/ppermute | solution.py:301
  21.5 2.6 %collective-permute-start.3 = (bf16[32,512]{1,0:T(8,128)(2,1)S(1)}, bf16[32,512]{1,0:T(8,128)(2,1)S(1)}, u32[]{:S(2)}, u32[]{:S(2)}) collective-permute-start(bf16[32,512]{1,0:T(8,128)(2,1)S(1)} %get-tuple-element.23), channel_id=1, source_target_pairs={{0,1},{1,0},{2,3},{3,2},{4,5},{5,4},{6,7},{7,6},{8,9},{9,8},{10,11... | collective-permute-start | bytes 98312 | tf_op jit(solution)/shard_map/ppermute | solution.py:301
  25.2 8.3 %collective-permute-start.6 = (bf16[32,2048]{1,0:T(8,128)(2,1)S(1)}, bf16[32,2048]{1,0:T(8,128)(2,1)S(1)}, u32[]{:S(2)}, u32[]{:S(2)}) collective-permute-start(bf16[32,2048]{1,0:T(8,128)(2,1)S(1)} %get-tuple-element.28), channel_id=1, source_target_pairs={{0,12},{4,8},{8,4},{12,0},{1,13},{5,9},{9,5},{13,1},{2,14},{6,10},... | collective-permute-start | bytes 393224 | tf_op jit(solution)/shard_map/ppermute | solution.py:301
  28.7 11.4 %collective-permute-start.7 = (bf16[32,2048]{1,0:T(8,128)(2,1)S(1)}, bf16[32,2048]{1,0:T(8,128)(2,1)S(1)}, u32[]{:S(2)}, u32[]{:S(2)}) collective-permute-start(bf16[32,2048]{1,0:T(8,128)(2,1)S(1)} %get-tuple-element.29), channel_id=1, source_target_pairs={{0,8},{4,12},{8,0},{12,4},{1,9},{5,13},{9,1},{13,5},{2,10},{6,14},... | collective-permute-start | bytes 393224 | tf_op jit(solution)/shard_map/ppermute | solution.py:301
  28.7 11.4 %collective-permute-start.8 = (bf16[32,2048]{1,0:T(8,128)(2,1)S(1)}, bf16[32,2048]{1,0:T(8,128)(2,1)S(1)}, u32[]{:S(2)}, u32[]{:S(2)}) collective-permute-start(bf16[32,2048]{1,0:T(8,128)(2,1)S(1)} %get-tuple-element.30), channel_id=1, source_target_pairs={{0,4},{4,0},{8,12},{12,8},{1,5},{5,1},{9,13},{13,9},{2,6},{6,2},{1... | collective-permute-start | bytes 393224 | tf_op jit(solution)/shard_map/ppermute | solution.py:301

commit v6 on v5

--- a/solution.py
+++ b/solution.py
@@ -14,12 +14,12 @@
 GROUP_SHARE = QUERY_HEAD_COUNT // KEY_VALUE_HEADS
 DOCUMENT_REACH = 256
 BLOCK = 128
+UNIT_HEADS = 2
 
 MASKED = -1e30
 ADAPTER_SCALE = 2.0
 LOG2_E = 1.4426950408889634
 ATTENTION_VMEM = 24 * 1024 * 1024
-LOW_STEPS = 4
 VMEM_BYTES = 16 * 1024 * 1024
 
 NN = (((1,), (0,)), ((), ()))
@@ -130,63 +130,91 @@
     bias_ref, q_ref, g_ref, k_ref, v_ref, gq_hbm, gk_ref, gv_ref, gq_ref, sems
 ):
     row_count = q_ref.shape[0]
+    groups = k_ref.shape[1] // HEAD_SIZE
     scale = 1.0 / math.sqrt(HEAD_SIZE)
     spans = query_spans(row_count)
+
+    units = []
+    for group in range(groups):
+        at = 0
+        for block, (first, low, high) in enumerate(spans):
+            for part in range(0, GROUP_SHARE, UNIT_HEADS):
+                heads = [
+                    slice(h * HEAD_SIZE, (h + 1) * HEAD_SIZE)
+                    for h in range(
+                        group * GROUP_SHARE + part, group * GROUP_SHARE + part + UNIT_HEADS
+                    )
+                ]
+                units.append((group, block, heads, slice(first, first + BLOCK), low, high, at))
+            at += high - low
+
+    columns = [slice(group * HEAD_SIZE, (group + 1) * HEAD_SIZE) for group in range(groups)]
+    key_t = [k_ref[:, column].T for column in columns]
+    grad_key = [[None] * len(spans) for _ in range(groups)]
+    grad_value = [[None] * len(spans) for _ in range(groups)]
     copies = []
-    for group in range(k_ref.shape[1] // HEAD_SIZE):
-        columns = slice(group * HEAD_SIZE, (group + 1) * HEAD_SIZE)
-        heads = [
-            slice(h * HEAD_SIZE, (h + 1) * HEAD_SIZE)
-            for h in range(group * GROUP_SHARE, (group + 1) * GROUP_SHARE)
-        ]
-        key_t = k_ref[:, columns].T
-        grad_key = [None] * len(spans)
-        grad_value = [None] * len(spans)
-        at = 0
-        for first, low, high in spans:
-            width = high - low
-            rows = slice(first, first + BLOCK)
-            query = jnp.concatenate([q_ref[rows, head] for head in heads], axis=0)
-            grad = jnp.concatenate([g_ref[rows, head] for head in heads], axis=0)
-            all_scores = mxu(k_ref[low:high, columns], query, NT)
-            all_grad_weights = mxu(v_ref[low:high, columns], grad, NT)
-            bias = bias_ref[at : at + width, :]
-            at += width
-            rounded, grad_scores = [], []
-            for h in range(GROUP_SHARE):
-                part = slice(h * BLOCK, (h + 1) * BLOCK)
-                scores = all_scores[:, part] * (scale * LOG2_E) + bias
-                grad_weights = all_grad_weights[:, part]
-                largest = jnp.max(scores, axis=0, keepdims=True)
-                numerator = jnp.exp2(scores - largest)
-                weights = numerator * (1.0 / jnp.sum(numerator, axis=0, keepdims=True))
-                rounded.append(weights.astype(jnp.bfloat16))
-                delta = jnp.sum(
-                    rounded[-1].astype(jnp.float32) * grad_weights, axis=0, keepdims=True
-                )
-                grad_scores.append((weights * (grad_weights - delta)).astype(jnp.bfloat16))
-            rounded = jnp.concatenate(rounded, axis=1)
-            grad_scores = jnp.concatenate(grad_scores, axis=1)
-            value_terms = mxu(rounded, grad, NN)
-            key_terms = mxu(grad_scores, query, NN)
-            for index in range(low // BLOCK, high // BLOCK):
-                part = slice(index * BLOCK - low, (index + 1) * BLOCK - low)
-                for total, terms in ((grad_value, value_terms), (grad_key, key_terms)):
-                    total[index] = (
-                        terms[part] if total[index] is None else total[index] + terms[part]
-                    )
-            grad_query = (mxu(key_t[:, low:high], grad_scores, NN) * scale).astype(jnp.bfloat16)
-            for h, head in enumerate(heads):
-                gq_ref[head, rows] = grad_query[:, h * BLOCK : (h + 1) * BLOCK]
-            block = (slice(heads[0].start, heads[-1].stop), rows)
+
+    def products(unit):
+        group, _, heads, rows, low, high, _ = unit
+        query = jnp.concatenate([q_ref[rows, head] for head in heads], axis=0)
+        grad = jnp.concatenate([g_ref[rows, head] for head in heads], axis=0)
+        scores = mxu(k_ref[low:high, columns[group]], query, NT)
+        grad_weights = mxu(v_ref[low:high, columns[group]], grad, NT)
+        return query, grad, scores, grad_weights
+
+    def softmax(unit, query, grad, all_scores, all_grad_weights):
+        low, high, at = unit[4:]
+        bias = bias_ref[at : at + high - low, :]
+        rounded, grad_scores = [], []
+        for h in range(UNIT_HEADS):
+            part = slice(h * BLOCK, (h + 1) * BLOCK)
+            scores = all_scores[:, part] * (scale * LOG2_E) + bias
+            grad_weights = all_grad_weights[:, part]
+            largest = jnp.max(scores, axis=0, keepdims=True)
+            numerator = jnp.exp2(scores - largest)
+            weights = numerator * (1.0 / jnp.sum(numerator, axis=0, keepdims=True))
+            rounded.append(weights.astype(jnp.bfloat16))
+            delta = jnp.sum(rounded[-1].astype(jnp.float32) * grad_weights, axis=0, keepdims=True)
+            grad_scores.append((weights * (grad_weights - delta)).astype(jnp.bfloat16))
+        return query, grad, jnp.concatenate(rounded, axis=1), jnp.concatenate(grad_scores, axis=1)
+
+    def add(total, terms, low, high):
+        for index in range(low // BLOCK, high // BLOCK):
+            part = terms[index * BLOCK - low : (index + 1) * BLOCK - low]
+            total[index] = part if total[index] is None else total[index] + part
+
+    def gradients(unit, query, grad, rounded, grad_scores):
+        group, block, heads, rows, low, high, _ = unit
+        grad_query = (mxu(key_t[group][:, low:high], grad_scores, NN) * scale).astype(jnp.bfloat16)
+        for h, head in enumerate(heads):
+            gq_ref[head, rows] = grad_query[:, h * BLOCK : (h + 1) * BLOCK]
+        add(grad_value[group], mxu(rounded, grad, NN), low, high)
+        add(grad_key[group], mxu(grad_scores, query, NN), low, high)
+        width = GROUP_SHARE * HEAD_SIZE
+        if heads[-1].stop == (group + 1) * width:
+            done = (slice(group * width, (group + 1) * width), rows)
             copies.append(
-                pltpu.make_async_copy(gq_ref.at[block], gq_hbm.at[block], sems.at[len(copies)])
+                pltpu.make_async_copy(gq_ref.at[done], gq_hbm.at[done], sems.at[len(copies)])
             )
             copies[-1].start()
-        for index in range(len(spans)):
-            rows = slice(index * BLOCK, (index + 1) * BLOCK)
-            gk_ref[rows, columns] = (grad_key[index] * scale).astype(jnp.bfloat16)
-            gv_ref[rows, columns] = grad_value[index].astype(jnp.bfloat16)
+            if block == len(spans) - 1:
+                for index in range(len(spans)):
+                    keys = slice(index * BLOCK, (index + 1) * BLOCK)
+                    gk_ref[keys, columns[group]] = (grad_key[group][index] * scale).astype(
+                        jnp.bfloat16
+                    )
+                    gv_ref[keys, columns[group]] = grad_value[group][index].astype(jnp.bfloat16)
+
+    ahead, behind = products(units[0]), None
+    for index, unit in enumerate(units):
+        held = ahead
+        if index + 1 < len(units):
+            ahead = products(units[index + 1])
+        held = softmax(unit, *held)
+        if behind is not None:
+            gradients(units[index - 1], *behind)
+        behind = held
+    gradients(units[-1], *behind)
     for copy in copies:
         copy.wait()
 
@@ -198,14 +226,14 @@
     return pl.pallas_call(
         attention_kernel,
         in_specs=[vmem] * 5,
-        out_specs=[pl.BlockSpec(memory_space=pltpu.HBM), vmem, vmem],
+        out_specs=[pl.BlockSpec(memory_space=pltpu.HBM), vmem, vmem, vmem],
         out_shape=[
             pltpu.HBM(turned, jnp.bfloat16),
             jax.ShapeDtypeStruct(keys.shape, jnp.bfloat16),
             jax.ShapeDtypeStruct(values.shape, jnp.bfloat16),
+            jax.ShapeDtypeStruct(turned, jnp.bfloat16),
         ],
         scratch_shapes=[
-            pltpu.VMEM(turned, jnp.bfloat16),
             pltpu.SemaphoreType.DMA((chunks,)),
         ],
         compiler_params=pltpu.CompilerParams(vmem_limit_bytes=ATTENTION_VMEM),
@@ -230,26 +258,14 @@
     ).astype(jnp.bfloat16)
 
 
-def low_kernel(peers, local_slots, mask_ref, x_ref, gq_hbm, *refs):
-    factors, (out_ref, sent_ref, gq_ref, sems) = refs[:peers], refs[peers:]
-    step = gq_ref.shape[0] // LOW_STEPS
-    pieces = [pl.ds(index * step, step) for index in range(LOW_STEPS)]
-    copies = [
-        pltpu.make_async_copy(gq_hbm.at[piece], gq_ref.at[piece], sems.at[index])
-        for index, piece in enumerate(pieces)
-    ]
-    for copy in copies:
-        copy.start()
+def low_kernel(peers, local_slots, mask_ref, x_ref, gq_ref, *refs):
+    factors, (out_ref, sent_ref) = refs[:peers], refs[peers:]
     rank = factors[0].shape[0] // (2 * local_slots)
     share = rank * local_slots
     down = jnp.concatenate([ref[:share] for ref in factors], axis=0)
     out_ref[:rank] = select(mxu(down, x_ref[...], NT), mask_ref, rank)
-    total = None
-    for piece, copy in zip(pieces, copies):
-        up = jnp.concatenate([ref[share:, piece] for ref in factors], axis=0)
-        copy.wait()
-        part = mxu(up, gq_ref[piece], NN)
-        total = part if total is None else total + part
+    up = jnp.concatenate([ref[share:] for ref in factors], axis=0)
+    total = mxu(up, gq_ref[...], NN)
     out_ref[rank:] = select(total, mask_ref, rank)
     sent_ref[...] = out_ref[...].astype(jnp.bfloat16)
 
@@ -280,16 +296,12 @@
     out_ref[...] = (mxu(wide, down, TN) * ADAPTER_SCALE).astype(jnp.bfloat16)
 
 
-def call(kernel, arrays, out_shape, flops, name, in_hbm=(), scratch=()):
+def call(kernel, arrays, out_shape, flops, name):
     return pl.pallas_call(
         kernel,
-        in_specs=[
-            pl.BlockSpec(memory_space=pltpu.HBM if index in in_hbm else pltpu.VMEM)
-            for index in range(len(arrays))
-        ],
+        in_specs=[pl.BlockSpec(memory_space=pltpu.VMEM)] * len(arrays),
         out_specs=jax.tree.map(lambda _: pl.BlockSpec(memory_space=pltpu.VMEM), out_shape),
         out_shape=out_shape,
-        scratch_shapes=scratch,
         compiler_params=pltpu.CompilerParams(vmem_limit_bytes=VMEM_BYTES),
         cost_estimate=pl.CostEstimate(flops=flops, bytes_accessed=4 * 2**20, transcendentals=0),
         name=name,
@@ -327,7 +339,7 @@
         up_weight.reshape(share, width),
     )
     factors = [own] + [swap(own, "dp", distance) for distance in range(1, peers)]
-    query_gradient, key_gradient, value_gradient = attention_backward(
+    query_gradient, key_gradient, value_gradient, near = attention_backward(
         bias, rotated_queries, output_gradient, rotated_keys, value_rows
     )
     low, low_sent = call(
@@ -335,7 +347,7 @@
         (
             mask,
             normed_input,
-            pltpu.with_memory_space_constraint(query_gradient, pltpu.HBM),
+            near,
             *factors,
         ),
         [
@@ -344,11 +356,6 @@
         ],
         10**9,
         "low",
-        in_hbm=(2,),
-        scratch=[
-            pltpu.VMEM((width, row_count), jnp.bfloat16),
-            pltpu.SemaphoreType.DMA((LOW_STEPS,)),
-        ],
     )
     lows = [low] + [swap(low_sent, "tensor", distance) for distance in range(1, parts)]
     *terms, low_grads = call(

time: 41 us -> 40.9 us (level)
  Pallas kernels: 16.3 us -> 14.5 us
  waiting for transfers between devices: 10.9 us -> 12.5 us
    ppermute x9, waiting for transfers between devices: 10.9 us -> 12.5 us  [swap(): return lax.ppermute(array, axis, [(i, i ^ distance) for i in range(size)])]
    pallas_call x1, Pallas kernels: 10.2 us -> 9.15 us  [attention_backward(): pl.pallas_call(attention_kernel, in_specs=[vmem] * 5, out_specs=[pl.Block...]
    pallas_call x3, Pallas kernels: 5.07 us -> 4.28 us  [call(): pl.pallas_call(kernel, in_specs=[pl.BlockSpec(memory_space=pltpu.VMEM)] *...]
  transfers between devices with their start and end apart: 9 -> 9, of which waited for: 5 -> 5; matrix products, arithmetic and copies ran while one was open for 0% -> 0% of each run, Pallas kernels for 30% -> 28%
where the time goes in v6:
time: 40.9 us; the launch traced here: 40.7 us
  Pallas kernels  14.5 us (35%)
  waiting for transfers between devices  12.5 us (31%)
  starting transfers between devices  12.1 us (30%)
  between operations  0.75 us (2%)
  local copies, waits for them, and re-layouts  0.74 us (2%)
    ppermute x9, waiting for transfers between devices, swap(): return lax.ppermute(array, axis, [(i, i ^ distance) for i in range(size)])  12.5 us
    ppermute x9, starting transfers between devices, swap(): return lax.ppermute(array, axis, [(i, i ^ distance) for i in range(size)])  12.1 us
    pallas_call x1, Pallas kernels, attention_backward(): pl.pallas_call(attention_kernel, in_specs=[vmem] * 5, out_specs=[pl.Block...  9.15 us
    pallas_call x3, Pallas kernels, call(): pl.pallas_call(kernel, in_specs=[pl.BlockSpec(memory_space=pltpu.VMEM)] *...  4.28 us
    pallas_call x1, Pallas kernels, pack(): pl.pallas_call(functools.partial(pack_kernel, row_count, peers), in_specs...  1.07 us
  transfers between devices with their start and end apart: 9, of which 5 were waited for; matrix products, arithmetic and copies ran while one was open for 0% of the time, Pallas kernels for 28%

profile of v6, /device:TPU:0, one launch (start us, length us, event | category | flops | bytes accessed | tf_op | source)
XLA Modules:
  0.0 40.7 jit_solution(10582447925878429594)
XLA Ops:
  0.7 1.1 %pack.1 = (bf16[32,2048]{1,0:T(8,128)(2,1)S(1)}, f32[1152,128]{1,0:T(8,128)S(1)}, f32[4,512]{1,0:T(4,128)S(1)}) custom-call(s32[1,8]{1,0:T(1,128)} %len_hbm.1, s32[1,8]{1,0:T(1,128)} %adapter_hbm.1, s32[4]{0:T(128)} %slot_hbm.1, bf16[16,2048]{1,0:T(8,128)(2,1)} %bitcast.6, bf16[16,2048]{1,0:T(8,128)(2,1)} %bitcast.7), custom_call_target="tpu_custom_call" | custom-call | flops 10000000000 | bytes 1048576 | tf_op jit(solution)/shard_map/pack/pallas_call | solution.py:108
  1.8 3.1 %collective-permute-start = (bf16[32,2048]{1,0:T(8,128)(2,1)S(1)}, bf16[32,2048]{1,0:T(8,128)(2,1)S(1)}, u32[]{:S(2)}, u32[]{:S(2)}) collective-permute-start(bf16[32,2048]{1,0:T(8,128)(2,1)S(1)} %get-tuple-element.22.refs_0_), channel_id=1, source_target_pairs={{0,4},{4,0},{8,12},{12,8},{1,5},{5,1},{9,13},{13,9},{2,6},{6,2},{1... | collective-permute-start | bytes 393224 | tf_op jit(solution)/shard_map/ppermute | solution.py:313
  4.8 2.6 %collective-permute-start.1 = (bf16[32,2048]{1,0:T(8,128)(2,1)S(1)}, bf16[32,2048]{1,0:T(8,128)(2,1)S(1)}, u32[]{:S(2)}, u32[]{:S(2)}) collective-permute-start(bf16[32,2048]{1,0:T(8,128)(2,1)S(1)} %get-tuple-element.22.refs_0_), channel_id=1, source_target_pairs={{0,8},{4,12},{8,0},{12,4},{1,9},{5,13},{9,1},{13,5},{2,10},{6,14},... | collective-permute-start | bytes 393224 | tf_op jit(solution)/shard_map/ppermute | solution.py:313
  7.5 0.0 copy-start
  7.5 9.2 %attention_backward.1 = (bf16[2048,512]{1,0:T(8,128)(2,1)}, bf16[512,256]{1,0:T(8,128)(2,1)}, bf16[512,256]{1,0:T(8,128)(2,1)}, bf16[2048,512]{1,0:T(8,128)(2,1)S(1)}) custom-call(f32[1152,128]{1,0:T(8,128)S(1)} %get-tuple-element.20.bias_ref, bf16[512,2048]{1,0:T(8,128)(2,1)S(1)} %copy-done.2, bf16[512,2048]{1,0:T(8,128)(2,1)S(1)} %copy-done.3, ...), custom_call_target="tpu_custom_call" | custom-call | flops 8000000000 | bytes 8388608 | tf_op jit(solution)/shard_map/attention_backward/pallas_call | solution.py:226
  16.6 0.0 collective-permute-done.refs_1_
  16.6 1.1 %collective-permute-done.1.refs_2_ = bf16[32,2048]{1,0:T(8,128)(2,1)S(1)} collective-permute-done((bf16[32,2048]{1,0:T(8,128)(2,1)S(1)}, bf16[32,2048]{1,0:T(8,128)(2,1)S(1)}, u32[]{:S(2)}, u32[]{:S(2)}) %collective-permute-start.1) | collective-permute-done | bytes 131104 | tf_op jit(solution)/shard_map/ppermute | solution.py:313
  17.8 0.0 collective-permute-done.2.refs_3_
  17.8 1.1 %low.1 = (f32[32,512]{1,0:T(8,128)S(1)}, bf16[32,512]{1,0:T(8,128)(2,1)S(1)}) custom-call(f32[4,512]{1,0:T(4,128)S(1)} %get-tuple-element.19.mask_ref, bf16[512,2048]{1,0:T(8,128)(2,1)S(1)} %copy-done, bf16[2048,512]{1,0:T(8,128)(2,1)S(1)} %get-tuple-element.21.gq_ref, bf16[32,2048]{1,0:T(8,128)(2,1)S(1)} %get-tuple-element.22.refs_0_, ...), custom_call_target="tpu_custom_call" | custom-call | flops 1000000000 | bytes 4194304 | tf_op jit(solution)/shard_map/low/pallas_call | solution.py:300
  18.9 0.1 collective-permute-start.3
  19.0 1.6 %collective-permute-start.4 = (bf16[32,512]{1,0:T(8,128)(2,1)S(1)}, bf16[32,512]{1,0:T(8,128)(2,1)S(1)}, u32[]{:S(2)}, u32[]{:S(2)}) collective-permute-start(bf16[32,512]{1,0:T(8,128)(2,1)S(1)} %get-tuple-element.24), channel_id=1, source_target_pairs={{0,2},{1,3},{2,0},{3,1},{4,6},{5,7},{6,4},{7,5},{8,10},{9,11},{10,... | collective-permute-start | bytes 98312 | tf_op jit(solution)/shard_map/ppermute | solution.py:313
  20.5 0.3 collective-permute-start.5
  20.8 0.0 collective-permute-done.3.refs_1_
  20.8 2.1 %collective-permute-done.4.refs_2_ = bf16[32,512]{1,0:T(8,128)(2,1)S(1)} collective-permute-done((bf16[32,512]{1,0:T(8,128)(2,1)S(1)}, bf16[32,512]{1,0:T(8,128)(2,1)S(1)}, u32[]{:S(2)}, u32[]{:S(2)}) %collective-permute-start.4) | collective-permute-done | bytes 32800 | tf_op jit(solution)/shard_map/ppermute | solution.py:313
  23.0 0.9 %collective-permute-done.5.refs_3_ = bf16[32,512]{1,0:T(8,128)(2,1)S(1)} collective-permute-done((bf16[32,512]{1,0:T(8,128)(2,1)S(1)}, bf16[32,512]{1,0:T(8,128)(2,1)S(1)}, u32[]{:S(2)}, u32[]{:S(2)}) %collective-permute-start.5) | collective-permute-done | bytes 32800 | tf_op jit(solution)/shard_map/ppermute | solution.py:313
  23.9 1.1 %product.1 = (f32[32,2048]{1,0:T(8,128)S(1)}, bf16[32,2048]{1,0:T(8,128)(2,1)S(1)}, bf16[32,2048]{1,0:T(8,128)(2,1)S(1)}, bf16[32,2048]{1,0:T(8,128)(2,1)S(1)}, bf16[16,512]{1,0:T(8,128)(2,1)S(1)}) custom-call(f32[4,512]{1,0:T(4,128)S(1)} %get-tuple-element.19.mask_ref, f32[32,512]{1,0:T(8,128)S(1)} %get-tuple-element.23.refs_0_, ...), custom_call_target="tpu_custom_call" | custom-call | flops 1000000000 | bytes 4194304 | tf_op jit(solution)/shard_map/product/pallas_call | solution.py:300
  25.0 2.0 %collective-permute-start.8 = (bf16[32,2048]{1,0:T(8,128)(2,1)S(1)}, bf16[32,2048]{1,0:T(8,128)(2,1)S(1)}, u32[]{:S(2)}, u32[]{:S(2)}) collective-permute-start(bf16[32,2048]{1,0:T(8,128)(2,1)S(1)} %get-tuple-element.32), channel_id=1, source_target_pairs={{0,4},{4,0},{8,12},{12,8},{1,5},{5,1},{9,13},{13,9},{2,6},{6,2},{1... | collective-permute-start | bytes 393224 | tf_op jit(solution)/shard_map/ppermute | solution.py:313
  27.0 1.3 %collective-permute-start.7 = (bf16[32,2048]{1,0:T(8,128)(2,1)S(1)}, bf16[32,2048]{1,0:T(8,128)(2,1)S(1)}, u32[]{:S(2)}, u32[]{:S(2)}) collective-permute-start(bf16[32,2048]{1,0:T(8,128)(2,1)S(1)} %get-tuple-element.31), channel_id=1, source_target_pairs={{0,8},{4,12},{8,0},{12,4},{1,9},{5,13},{9,1},{13,5},{2,10},{6,14},... | collective-permute-start | bytes 393224 | tf_op jit(solution)/shard_map/ppermute | solution.py:313
  28.3 1.2 %collective-permute-start.6 = (bf16[32,2048]{1,0:T(8,128)(2,1)S(1)}, bf16[32,2048]{1,0:T(8,128)(2,1)S(1)}, u32[]{:S(2)}, u32[]{:S(2)}) collective-permute-start(bf16[32,2048]{1,0:T(8,128)(2,1)S(1)} %get-tuple-element.30), channel_id=1, source_target_pairs={{0,12},{4,8},{8,4},{12,0},{1,13},{5,9},{9,5},{13,1},{2,14},{6,10},... | collective-permute-start | bytes 393224 | tf_op jit(solution)/shard_map/ppermute | solution.py:313
  29.5 2.0 %input_gradient.1 = bf16[512,2048]{1,0:T(8,128)(2,1)} custom-call(f32[4,512]{1,0:T(4,128)S(1)} %get-tuple-element.19.mask_ref, bf16[16,512]{1,0:T(8,128)(2,1)S(1)} %get-tuple-element.26.low_ref, bf16[32,2048]{1,0:T(8,128)(2,1)S(1)} %get-tuple-element.22.refs_0_, bf16[32,2048]{1,0:T(8,128)(2,1)S(1)} %collective-permute-done.refs_1_, ...), custom_call_target="tpu_custom_call" | custom-call | flops 1000000000 | bytes 4194304 | tf_op jit(solution)/shard_map/input_gradient/pallas_call | solution.py:300
  31.5 1.2 %collective-permute-done.8 = bf16[32,2048]{1,0:T(8,128)(2,1)S(1)} collective-permute-done((bf16[32,2048]{1,0:T(8,128)(2,1)S(1)}, bf16[32,2048]{1,0:T(8,128)(2,1)S(1)}, u32[]{:S(2)}, u32[]{:S(2)}) %collective-permute-start.8) | collective-permute-done | bytes 131104 | tf_op jit(solution)/shard_map/ppermute | solution.py:313
  32.8 7.2 %collective-permute-done.7 = bf16[32,2048]{1,0:T(8,128)(2,1)S(1)} collective-permute-done((bf16[32,2048]{1,0:T(8,128)(2,1)S(1)}, bf16[32,2048]{1,0:T(8,128)(2,1)S(1)}, u32[]{:S(2)}, u32[]{:S(2)}) %collective-permute-start.7) | collective-permute-done | bytes 131104 | tf_op jit(solution)/shard_map/ppermute | solution.py:313
  39.9 0.1 convert_add_fusion
  40.0 0.7 %slice_bitcast_fusion = (f32[1,16,2048]{2,1,0:T(8,128)}, f32[1,16,2048]{2,1,0:T(8,128)}) fusion(f32[32,2048]{1,0:T(8,128)S(1)} %convert_add_fusion), kind=kLoop, calls=%fused_computation.1 | loop fusion | bytes 524288 | tf_op jit(solution)/shard_map/reshape | solution.py:384
  (13 shorter events, 0.0 us)
Async XLA Ops:
  0.6 6.8 %copy-start.2 = (bf16[512,2048]{1,0:T(8,128)(2,1)S(1)}, bf16[512,2048]{1,0:T(8,128)(2,1)}, u32[]{:S(2)}) copy-start(bf16[512,2048]{1,0:T(8,128)(2,1)} %q_ref.1) | copy-start | bytes 6291460
  0.6 6.8 %copy-start.3 = (bf16[512,2048]{1,0:T(8,128)(2,1)S(1)}, bf16[512,2048]{1,0:T(8,128)(2,1)}, u32[]{:S(2)}) copy-start(bf16[512,2048]{1,0:T(8,128)(2,1)} %g_ref.1) | copy-start | bytes 6291460
  0.7 6.8 %copy-start.4 = (bf16[512,256]{1,0:T(8,128)(2,1)S(1)}, bf16[512,256]{1,0:T(8,128)(2,1)}, u32[]{:S(2)}) copy-start(bf16[512,256]{1,0:T(8,128)(2,1)} %k_ref.1) | copy-start | bytes 786436
  0.7 6.8 %copy-start.5 = (bf16[512,256]{1,0:T(8,128)(2,1)S(1)}, bf16[512,256]{1,0:T(8,128)(2,1)}, u32[]{:S(2)}) copy-start(bf16[512,256]{1,0:T(8,128)(2,1)} %v_ref.1) | copy-start | bytes 786436
  1.8 14.9 %collective-permute-start = (bf16[32,2048]{1,0:T(8,128)(2,1)S(1)}, bf16[32,2048]{1,0:T(8,128)(2,1)S(1)}, u32[]{:S(2)}, u32[]{:S(2)}) collective-permute-start(bf16[32,2048]{1,0:T(8,128)(2,1)S(1)} %get-tuple-element.22.refs_0_), channel_id=1, source_target_pairs={{0,4},{4,0},{8,12},{12,8},{1,5},{5,1},{9,13},{13,9},{2,6},{6,2},{1... | collective-permute-start | bytes 393224 | tf_op jit(solution)/shard_map/ppermute | solution.py:313
  4.8 12.9 %collective-permute-start.1 = (bf16[32,2048]{1,0:T(8,128)(2,1)S(1)}, bf16[32,2048]{1,0:T(8,128)(2,1)S(1)}, u32[]{:S(2)}, u32[]{:S(2)}) collective-permute-start(bf16[32,2048]{1,0:T(8,128)(2,1)S(1)} %get-tuple-element.22.refs_0_), channel_id=1, source_target_pairs={{0,8},{4,12},{8,0},{12,4},{1,9},{5,13},{9,1},{13,5},{2,10},{6,14},... | collective-permute-start | bytes 393224 | tf_op jit(solution)/shard_map/ppermute | solution.py:313
  7.4 10.3 %collective-permute-start.2 = (bf16[32,2048]{1,0:T(8,128)(2,1)S(1)}, bf16[32,2048]{1,0:T(8,128)(2,1)S(1)}, u32[]{:S(2)}, u32[]{:S(2)}) collective-permute-start(bf16[32,2048]{1,0:T(8,128)(2,1)S(1)} %get-tuple-element.22.refs_0_), channel_id=1, source_target_pairs={{0,12},{4,8},{8,4},{12,0},{1,13},{5,9},{9,5},{13,1},{2,14},{6,10},... | collective-permute-start | bytes 393224 | tf_op jit(solution)/shard_map/ppermute | solution.py:313
  7.5 10.3 %copy-start = (bf16[512,2048]{1,0:T(8,128)(2,1)S(1)}, bf16[512,2048]{1,0:T(8,128)(2,1)}, u32[]{:S(2)}) copy-start(bf16[512,2048]{1,0:T(8,128)(2,1)} %refs_4_.1) | copy-start | bytes 6291460
  17.8 6.1 %copy-start.1 = (bf16[2048,512]{1,0:T(8,128)(2,1)S(1)}, bf16[2048,512]{1,0:T(8,128)(2,1)}, u32[]{:S(2)}) copy-start(bf16[2048,512]{1,0:T(8,128)(2,1)} %get-tuple-element.25.refs_5_) | copy-start | bytes 6291460
  18.9 1.9 %collective-permute-start.3 = (bf16[32,512]{1,0:T(8,128)(2,1)S(1)}, bf16[32,512]{1,0:T(8,128)(2,1)S(1)}, u32[]{:S(2)}, u32[]{:S(2)}) collective-permute-start(bf16[32,512]{1,0:T(8,128)(2,1)S(1)} %get-tuple-element.24), channel_id=1, source_target_pairs={{0,1},{1,0},{2,3},{3,2},{4,5},{5,4},{6,7},{7,6},{8,9},{9,8},{10,11... | collective-permute-start | bytes 98312 | tf_op jit(solution)/shard_map/ppermute | solution.py:313
  19.0 4.0 %collective-permute-start.4 = (bf16[32,512]{1,0:T(8,128)(2,1)S(1)}, bf16[32,512]{1,0:T(8,128)(2,1)S(1)}, u32[]{:S(2)}, u32[]{:S(2)}) collective-permute-start(bf16[32,512]{1,0:T(8,128)(2,1)S(1)} %get-tuple-element.24), channel_id=1, source_target_pairs={{0,2},{1,3},{2,0},{3,1},{4,6},{5,7},{6,4},{7,5},{8,10},{9,11},{10,... | collective-permute-start | bytes 98312 | tf_op jit(solution)/shard_map/ppermute | solution.py:313
  20.5 3.3 %collective-permute-start.5 = (bf16[32,512]{1,0:T(8,128)(2,1)S(1)}, bf16[32,512]{1,0:T(8,128)(2,1)S(1)}, u32[]{:S(2)}, u32[]{:S(2)}) collective-permute-start(bf16[32,512]{1,0:T(8,128)(2,1)S(1)} %get-tuple-element.24), channel_id=1, source_target_pairs={{0,3},{1,2},{2,1},{3,0},{4,7},{5,6},{6,5},{7,4},{8,11},{9,10},{10,... | collective-permute-start | bytes 98312 | tf_op jit(solution)/shard_map/ppermute | solution.py:313
  25.0 7.8 %collective-permute-start.8 = (bf16[32,2048]{1,0:T(8,128)(2,1)S(1)}, bf16[32,2048]{1,0:T(8,128)(2,1)S(1)}, u32[]{:S(2)}, u32[]{:S(2)}) collective-permute-start(bf16[32,2048]{1,0:T(8,128)(2,1)S(1)} %get-tuple-element.32), channel_id=1, source_target_pairs={{0,4},{4,0},{8,12},{12,8},{1,5},{5,1},{9,13},{13,9},{2,6},{6,2},{1... | collective-permute-start | bytes 393224 | tf_op jit(solution)/shard_map/ppermute | solution.py:313
  27.0 12.9 %collective-permute-start.7 = (bf16[32,2048]{1,0:T(8,128)(2,1)S(1)}, bf16[32,2048]{1,0:T(8,128)(2,1)S(1)}, u32[]{:S(2)}, u32[]{:S(2)}) collective-permute-start(bf16[32,2048]{1,0:T(8,128)(2,1)S(1)} %get-tuple-element.31), channel_id=1, source_target_pairs={{0,8},{4,12},{8,0},{12,4},{1,9},{5,13},{9,1},{13,5},{2,10},{6,14},... | collective-permute-start | bytes 393224 | tf_op jit(solution)/shard_map/ppermute | solution.py:313
  28.3 11.6 %collective-permute-start.6 = (bf16[32,2048]{1,0:T(8,128)(2,1)S(1)}, bf16[32,2048]{1,0:T(8,128)(2,1)S(1)}, u32[]{:S(2)}, u32[]{:S(2)}) collective-permute-start(bf16[32,2048]{1,0:T(8,128)(2,1)S(1)} %get-tuple-element.30), channel_id=1, source_target_pairs={{0,12},{4,8},{8,4},{12,0},{1,13},{5,9},{9,5},{13,1},{2,14},{6,10},... | collective-permute-start | bytes 393224 | tf_op jit(solution)/shard_map/ppermute | solution.py:313

commit v7 on v6

--- a/solution.py
+++ b/solution.py
@@ -36,6 +36,10 @@
         (at, max(0, (at - (DOCUMENT_REACH - 1)) // BLOCK * BLOCK), at + BLOCK)
         for at in range(0, row_count, BLOCK)
     ]
+
+
+def distances(size):
+    return [0, *range(size - 1, 0, -1)]
 
 
 def pack_kernel(
@@ -82,9 +86,9 @@
         adapter = jnp.where(token >= end, adapter_ref[0, index + 1], adapter)
         begin = jnp.where(token >= end, end, begin)
     me = lax.axis_index("dp")
-    for distance in range(peers):
+    for place, distance in enumerate(distances(peers)):
         for own in range(local_slots):
-            row = distance * local_slots + own
+            row = place * local_slots + own
             held = slot_ref[(me ^ distance) * local_slots + own]
             mask_ref[row : row + 1, :] = jnp.where(adapter == held, 1.0, 0.0)
     at = 0
@@ -281,8 +285,8 @@
     wide_in, wide_grad = spread(low[:rank], mask_ref), spread(low[rank:], mask_ref)
     down = mxu(wide_grad, x_ref[...], NN) * ADAPTER_SCALE
     up = mxu(wide_in, gq_ref[...], NT) * ADAPTER_SCALE
-    for distance, ref in enumerate(outs[:peers]):
-        rows = slice(distance * share, (distance + 1) * share)
+    for place, ref in enumerate(outs[:peers]):
+        rows = slice(place * share, (place + 1) * share)
         ref[:share] = down[rows].astype(ref.dtype)
         ref[share:] = up[rows].astype(ref.dtype)
     outs[peers][...] = low[rank:].astype(jnp.bfloat16)
@@ -338,7 +342,7 @@
         down_weight.reshape(share, width),
         up_weight.reshape(share, width),
     )
-    factors = [own] + [swap(own, "dp", distance) for distance in range(1, peers)]
+    factors = [own] + [swap(own, "dp", distance) for distance in distances(peers)[1:]]
     query_gradient, key_gradient, value_gradient, near = attention_backward(
         bias, rotated_queries, output_gradient, rotated_keys, value_rows
     )
@@ -357,19 +361,21 @@
         10**9,
         "low",
     )
-    lows = [low] + [swap(low_sent, "tensor", distance) for distance in range(1, parts)]
+    lows = [low] + [swap(low_sent, "tensor", distance) for distance in distances(parts)[1:]]
     *terms, low_grads = call(
         functools.partial(product_kernel, peers, local_slots, parts),
         (mask, *lows, normed_input, query_gradient),
         [
-            jax.ShapeDtypeStruct((2 * share, width), jnp.bfloat16 if distance else jnp.float32)
-            for distance in range(peers)
+            jax.ShapeDtypeStruct((2 * share, width), jnp.bfloat16 if place else jnp.float32)
+            for place in range(peers)
         ]
         + [jax.ShapeDtypeStruct((rank, row_count), jnp.bfloat16)],
         10**9,
         "product",
     )
-    received = [swap(terms[distance], "dp", distance) for distance in reversed(range(1, peers))]
+    received = [
+        swap(part, "dp", distance) for distance, part in zip(distances(peers)[1:], terms[1:])
+    ]
     input_gradient = call(
         functools.partial(input_kernel, peers, local_slots),
         (mask, low_grads, *factors),
@@ -378,7 +384,7 @@
         "input_gradient",
     )
     total = terms[0]
-    for part in received:
+    for part in received[::-1]:
         total = total + part.astype(jnp.float32)
     down_gradient = total[:share].reshape(local_slots, rank, width)
     up_gradient = total[share:].reshape(local_slots, rank, width)

time: 40.9 us -> 39.2 us (0.958)
  waiting for transfers between devices: 12.5 us -> 10.9 us
    ppermute x9, waiting for transfers between devices: 12.5 us -> 10.9 us  [swap(): return lax.ppermute(array, axis, [(i, i ^ distance) for i in range(size)])]
  transfers between devices with their start and end apart: 9 -> 9, of which waited for: 5 -> 5; matrix products, arithmetic and copies ran while one was open for 0% -> 0% of each run, Pallas kernels for 28% -> 29%
where the time goes in v7:
time: 39.2 us; the launch traced here: 39.1 us
  Pallas kernels  14.5 us (37%)
  starting transfers between devices  12.1 us (31%)
  waiting for transfers between devices  10.9 us (28%)
  local copies, waits for them, and re-layouts  0.74 us (2%)
  between operations  0.73 us (2%)
    ppermute x9, starting transfers between devices, swap(): return lax.ppermute(array, axis, [(i, i ^ distance) for i in range(size)])  12.1 us
    ppermute x9, waiting for transfers between devices, swap(): return lax.ppermute(array, axis, [(i, i ^ distance) for i in range(size)])  10.9 us
    pallas_call x1, Pallas kernels, attention_backward(): pl.pallas_call(attention_kernel, in_specs=[vmem] * 5, out_specs=[pl.Block...  9.15 us
    pallas_call x3, Pallas kernels, call(): pl.pallas_call(kernel, in_specs=[pl.BlockSpec(memory_space=pltpu.VMEM)] *...  4.28 us
    pallas_call x1, Pallas kernels, pack(): pl.pallas_call(functools.partial(pack_kernel, row_count, peers), in_specs...  1.07 us
  transfers between devices with their start and end apart: 9, of which 5 were waited for; matrix products, arithmetic and copies ran while one was open for 0% of the time, Pallas kernels for 29%

profile of v7, /device:TPU:0, one launch (start us, length us, event | category | flops | bytes accessed | tf_op | source)
XLA Modules:
  0.0 39.1 jit_solution(16052290309520712462)
XLA Ops:
  0.7 1.1 %pack.1 = (bf16[32,2048]{1,0:T(8,128)(2,1)S(1)}, f32[1152,128]{1,0:T(8,128)S(1)}, f32[4,512]{1,0:T(4,128)S(1)}) custom-call(s32[1,8]{1,0:T(1,128)} %len_hbm.1, s32[1,8]{1,0:T(1,128)} %adapter_hbm.1, s32[4]{0:T(128)} %slot_hbm.1, bf16[16,2048]{1,0:T(8,128)(2,1)} %bitcast.6, bf16[16,2048]{1,0:T(8,128)(2,1)} %bitcast.7), custom_call_target="tpu_custom_call" | custom-call | flops 10000000000 | bytes 1048576 | tf_op jit(solution)/shard_map/pack/pallas_call | solution.py:112
  1.8 5.1 %collective-permute-start = (bf16[32,2048]{1,0:T(8,128)(2,1)S(1)}, bf16[32,2048]{1,0:T(8,128)(2,1)S(1)}, u32[]{:S(2)}, u32[]{:S(2)}) collective-permute-start(bf16[32,2048]{1,0:T(8,128)(2,1)S(1)} %get-tuple-element.22.refs_0_), channel_id=1, source_target_pairs={{0,12},{4,8},{8,4},{12,0},{1,13},{5,9},{9,5},{13,1},{2,14},{6,10},... | collective-permute-start | bytes 393224 | tf_op jit(solution)/shard_map/ppermute | solution.py:317
  6.9 0.0 collective-permute-start.1
  6.9 0.6 %collective-permute-start.2 = (bf16[32,2048]{1,0:T(8,128)(2,1)S(1)}, bf16[32,2048]{1,0:T(8,128)(2,1)S(1)}, u32[]{:S(2)}, u32[]{:S(2)}) collective-permute-start(bf16[32,2048]{1,0:T(8,128)(2,1)S(1)} %get-tuple-element.22.refs_0_), channel_id=1, source_target_pairs={{0,4},{4,0},{8,12},{12,8},{1,5},{5,1},{9,13},{13,9},{2,6},{6,2},{1... | collective-permute-start | bytes 393224 | tf_op jit(solution)/shard_map/ppermute | solution.py:317
  7.5 0.0 copy-start
  7.5 9.2 %attention_backward.1 = (bf16[2048,512]{1,0:T(8,128)(2,1)}, bf16[512,256]{1,0:T(8,128)(2,1)}, bf16[512,256]{1,0:T(8,128)(2,1)}, bf16[2048,512]{1,0:T(8,128)(2,1)S(1)}) custom-call(f32[1152,128]{1,0:T(8,128)S(1)} %get-tuple-element.20.bias_ref, bf16[512,2048]{1,0:T(8,128)(2,1)S(1)} %copy-done.2, bf16[512,2048]{1,0:T(8,128)(2,1)S(1)} %copy-done.3, ...), custom_call_target="tpu_custom_call" | custom-call | flops 8000000000 | bytes 8388608 | tf_op jit(solution)/shard_map/attention_backward/pallas_call | solution.py:230
  16.7 0.0 collective-permute-done.refs_1_
  16.7 1.2 %collective-permute-done.1.refs_2_ = bf16[32,2048]{1,0:T(8,128)(2,1)S(1)} collective-permute-done((bf16[32,2048]{1,0:T(8,128)(2,1)S(1)}, bf16[32,2048]{1,0:T(8,128)(2,1)S(1)}, u32[]{:S(2)}, u32[]{:S(2)}) %collective-permute-start.1) | collective-permute-done | bytes 131104 | tf_op jit(solution)/shard_map/ppermute | solution.py:317
  17.9 0.0 collective-permute-done.2.refs_3_
  18.0 1.1 %low.1 = (f32[32,512]{1,0:T(8,128)S(1)}, bf16[32,512]{1,0:T(8,128)(2,1)S(1)}) custom-call(f32[4,512]{1,0:T(4,128)S(1)} %get-tuple-element.19.mask_ref, bf16[512,2048]{1,0:T(8,128)(2,1)S(1)} %copy-done, bf16[2048,512]{1,0:T(8,128)(2,1)S(1)} %get-tuple-element.21.gq_ref, bf16[32,2048]{1,0:T(8,128)(2,1)S(1)} %get-tuple-element.22.refs_0_, ...), custom_call_target="tpu_custom_call" | custom-call | flops 1000000000 | bytes 4194304 | tf_op jit(solution)/shard_map/low/pallas_call | solution.py:304
  19.1 0.3 collective-permute-start.3
  19.4 1.3 %collective-permute-start.4 = (bf16[32,512]{1,0:T(8,128)(2,1)S(1)}, bf16[32,512]{1,0:T(8,128)(2,1)S(1)}, u32[]{:S(2)}, u32[]{:S(2)}) collective-permute-start(bf16[32,512]{1,0:T(8,128)(2,1)S(1)} %get-tuple-element.24), channel_id=1, source_target_pairs={{0,2},{1,3},{2,0},{3,1},{4,6},{5,7},{6,4},{7,5},{8,10},{9,11},{10,... | collective-permute-start | bytes 98312 | tf_op jit(solution)/shard_map/ppermute | solution.py:317
  20.7 0.3 collective-permute-start.5
  21.0 1.8 %collective-permute-done.3.refs_1_ = bf16[32,512]{1,0:T(8,128)(2,1)S(1)} collective-permute-done((bf16[32,512]{1,0:T(8,128)(2,1)S(1)}, bf16[32,512]{1,0:T(8,128)(2,1)S(1)}, u32[]{:S(2)}, u32[]{:S(2)}) %collective-permute-start.3) | collective-permute-done | bytes 32800 | tf_op jit(solution)/shard_map/ppermute | solution.py:317
  22.8 0.5 %collective-permute-done.4.refs_2_ = bf16[32,512]{1,0:T(8,128)(2,1)S(1)} collective-permute-done((bf16[32,512]{1,0:T(8,128)(2,1)S(1)}, bf16[32,512]{1,0:T(8,128)(2,1)S(1)}, u32[]{:S(2)}, u32[]{:S(2)}) %collective-permute-start.4) | collective-permute-done | bytes 32800 | tf_op jit(solution)/shard_map/ppermute | solution.py:317
  23.3 0.0 collective-permute-done.5.refs_3_
  23.3 1.1 %product.1 = (f32[32,2048]{1,0:T(8,128)S(1)}, bf16[32,2048]{1,0:T(8,128)(2,1)S(1)}, bf16[32,2048]{1,0:T(8,128)(2,1)S(1)}, bf16[32,2048]{1,0:T(8,128)(2,1)S(1)}, bf16[16,512]{1,0:T(8,128)(2,1)S(1)}) custom-call(f32[4,512]{1,0:T(4,128)S(1)} %get-tuple-element.19.mask_ref, f32[32,512]{1,0:T(8,128)S(1)} %get-tuple-element.23.refs_0_, ...), custom_call_target="tpu_custom_call" | custom-call | flops 1000000000 | bytes 4194304 | tf_op jit(solution)/shard_map/product/pallas_call | solution.py:304
  24.4 2.5 %collective-permute-start.8 = (bf16[32,2048]{1,0:T(8,128)(2,1)S(1)}, bf16[32,2048]{1,0:T(8,128)(2,1)S(1)}, u32[]{:S(2)}, u32[]{:S(2)}) collective-permute-start(bf16[32,2048]{1,0:T(8,128)(2,1)S(1)} %get-tuple-element.32), channel_id=1, source_target_pairs={{0,12},{4,8},{8,4},{12,0},{1,13},{5,9},{9,5},{13,1},{2,14},{6,10},... | collective-permute-start | bytes 393224 | tf_op jit(solution)/shard_map/ppermute | solution.py:317
  26.9 2.0 %collective-permute-start.6 = (bf16[32,2048]{1,0:T(8,128)(2,1)S(1)}, bf16[32,2048]{1,0:T(8,128)(2,1)S(1)}, u32[]{:S(2)}, u32[]{:S(2)}) collective-permute-start(bf16[32,2048]{1,0:T(8,128)(2,1)S(1)} %get-tuple-element.30), channel_id=1, source_target_pairs={{0,4},{4,0},{8,12},{12,8},{1,5},{5,1},{9,13},{13,9},{2,6},{6,2},{1... | collective-permute-start | bytes 393224 | tf_op jit(solution)/shard_map/ppermute | solution.py:317
  28.9 2.0 %input_gradient.1 = bf16[512,2048]{1,0:T(8,128)(2,1)} custom-call(f32[4,512]{1,0:T(4,128)S(1)} %get-tuple-element.19.mask_ref, bf16[16,512]{1,0:T(8,128)(2,1)S(1)} %get-tuple-element.26.low_ref, bf16[32,2048]{1,0:T(8,128)(2,1)S(1)} %get-tuple-element.22.refs_0_, bf16[32,2048]{1,0:T(8,128)(2,1)S(1)} %collective-permute-done.refs_1_, ...), custom_call_target="tpu_custom_call" | custom-call | flops 1000000000 | bytes 4194304 | tf_op jit(solution)/shard_map/input_gradient/pallas_call | solution.py:304
  30.9 1.8 %collective-permute-done.8 = bf16[32,2048]{1,0:T(8,128)(2,1)S(1)} collective-permute-done((bf16[32,2048]{1,0:T(8,128)(2,1)S(1)}, bf16[32,2048]{1,0:T(8,128)(2,1)S(1)}, u32[]{:S(2)}, u32[]{:S(2)}) %collective-permute-start.8) | collective-permute-done | bytes 131104 | tf_op jit(solution)/shard_map/ppermute | solution.py:317
  32.7 5.5 %collective-permute-done.7 = bf16[32,2048]{1,0:T(8,128)(2,1)S(1)} collective-permute-done((bf16[32,2048]{1,0:T(8,128)(2,1)S(1)}, bf16[32,2048]{1,0:T(8,128)(2,1)S(1)}, u32[]{:S(2)}, u32[]{:S(2)}) %collective-permute-start.7) | collective-permute-done | bytes 131104 | tf_op jit(solution)/shard_map/ppermute | solution.py:317
  38.3 0.1 convert_add_fusion
  38.3 0.7 %slice_bitcast_fusion = (f32[1,16,2048]{2,1,0:T(8,128)}, f32[1,16,2048]{2,1,0:T(8,128)}) fusion(f32[32,2048]{1,0:T(8,128)S(1)} %convert_add_fusion), kind=kLoop, calls=%fused_computation.1 | loop fusion | bytes 524288 | tf_op jit(solution)/shard_map/reshape | solution.py:390
  (13 shorter events, 0.0 us)
Async XLA Ops:
  0.6 6.9 %copy-start.2 = (bf16[512,2048]{1,0:T(8,128)(2,1)S(1)}, bf16[512,2048]{1,0:T(8,128)(2,1)}, u32[]{:S(2)}) copy-start(bf16[512,2048]{1,0:T(8,128)(2,1)} %q_ref.1) | copy-start | bytes 6291460
  0.6 6.9 %copy-start.3 = (bf16[512,2048]{1,0:T(8,128)(2,1)S(1)}, bf16[512,2048]{1,0:T(8,128)(2,1)}, u32[]{:S(2)}) copy-start(bf16[512,2048]{1,0:T(8,128)(2,1)} %g_ref.1) | copy-start | bytes 6291460
  0.7 6.9 %copy-start.4 = (bf16[512,256]{1,0:T(8,128)(2,1)S(1)}, bf16[512,256]{1,0:T(8,128)(2,1)}, u32[]{:S(2)}) copy-start(bf16[512,256]{1,0:T(8,128)(2,1)} %k_ref.1) | copy-start | bytes 786436
  0.7 6.9 %copy-start.5 = (bf16[512,256]{1,0:T(8,128)(2,1)S(1)}, bf16[512,256]{1,0:T(8,128)(2,1)}, u32[]{:S(2)}) copy-start(bf16[512,256]{1,0:T(8,128)(2,1)} %v_ref.1) | copy-start | bytes 786436
  1.8 14.9 %collective-permute-start = (bf16[32,2048]{1,0:T(8,128)(2,1)S(1)}, bf16[32,2048]{1,0:T(8,128)(2,1)S(1)}, u32[]{:S(2)}, u32[]{:S(2)}) collective-permute-start(bf16[32,2048]{1,0:T(8,128)(2,1)S(1)} %get-tuple-element.22.refs_0_), channel_id=1, source_target_pairs={{0,12},{4,8},{8,4},{12,0},{1,13},{5,9},{9,5},{13,1},{2,14},{6,10},... | collective-permute-start | bytes 393224 | tf_op jit(solution)/shard_map/ppermute | solution.py:317
  6.9 11.1 %collective-permute-start.1 = (bf16[32,2048]{1,0:T(8,128)(2,1)S(1)}, bf16[32,2048]{1,0:T(8,128)(2,1)S(1)}, u32[]{:S(2)}, u32[]{:S(2)}) collective-permute-start(bf16[32,2048]{1,0:T(8,128)(2,1)S(1)} %get-tuple-element.22.refs_0_), channel_id=1, source_target_pairs={{0,8},{4,12},{8,0},{12,4},{1,9},{5,13},{9,1},{13,5},{2,10},{6,14},... | collective-permute-start | bytes 393224 | tf_op jit(solution)/shard_map/ppermute | solution.py:317
  6.9 11.1 %collective-permute-start.2 = (bf16[32,2048]{1,0:T(8,128)(2,1)S(1)}, bf16[32,2048]{1,0:T(8,128)(2,1)S(1)}, u32[]{:S(2)}, u32[]{:S(2)}) collective-permute-start(bf16[32,2048]{1,0:T(8,128)(2,1)S(1)} %get-tuple-element.22.refs_0_), channel_id=1, source_target_pairs={{0,4},{4,0},{8,12},{12,8},{1,5},{5,1},{9,13},{13,9},{2,6},{6,2},{1... | collective-permute-start | bytes 393224 | tf_op jit(solution)/shard_map/ppermute | solution.py:317
  7.5 10.4 %copy-start = (bf16[512,2048]{1,0:T(8,128)(2,1)S(1)}, bf16[512,2048]{1,0:T(8,128)(2,1)}, u32[]{:S(2)}) copy-start(bf16[512,2048]{1,0:T(8,128)(2,1)} %refs_4_.1) | copy-start | bytes 6291460
  17.9 5.4 %copy-start.1 = (bf16[2048,512]{1,0:T(8,128)(2,1)S(1)}, bf16[2048,512]{1,0:T(8,128)(2,1)}, u32[]{:S(2)}) copy-start(bf16[2048,512]{1,0:T(8,128)(2,1)} %get-tuple-element.25.refs_5_) | copy-start | bytes 6291460
  19.1 3.7 %collective-permute-start.3 = (bf16[32,512]{1,0:T(8,128)(2,1)S(1)}, bf16[32,512]{1,0:T(8,128)(2,1)S(1)}, u32[]{:S(2)}, u32[]{:S(2)}) collective-permute-start(bf16[32,512]{1,0:T(8,128)(2,1)S(1)} %get-tuple-element.24), channel_id=1, source_target_pairs={{0,3},{1,2},{2,1},{3,0},{4,7},{5,6},{6,5},{7,4},{8,11},{9,10},{10,... | collective-permute-start | bytes 98312 | tf_op jit(solution)/shard_map/ppermute | solution.py:317
  19.4 3.9 %collective-permute-start.4 = (bf16[32,512]{1,0:T(8,128)(2,1)S(1)}, bf16[32,512]{1,0:T(8,128)(2,1)S(1)}, u32[]{:S(2)}, u32[]{:S(2)}) collective-permute-start(bf16[32,512]{1,0:T(8,128)(2,1)S(1)} %get-tuple-element.24), channel_id=1, source_target_pairs={{0,2},{1,3},{2,0},{3,1},{4,6},{5,7},{6,4},{7,5},{8,10},{9,11},{10,... | collective-permute-start | bytes 98312 | tf_op jit(solution)/shard_map/ppermute | solution.py:317
  20.7 2.6 %collective-permute-start.5 = (bf16[32,512]{1,0:T(8,128)(2,1)S(1)}, bf16[32,512]{1,0:T(8,128)(2,1)S(1)}, u32[]{:S(2)}, u32[]{:S(2)}) collective-permute-start(bf16[32,512]{1,0:T(8,128)(2,1)S(1)} %get-tuple-element.24), channel_id=1, source_target_pairs={{0,1},{1,0},{2,3},{3,2},{4,5},{5,4},{6,7},{7,6},{8,9},{9,8},{10,11... | collective-permute-start | bytes 98312 | tf_op jit(solution)/shard_map/ppermute | solution.py:317
  24.4 8.3 %collective-permute-start.8 = (bf16[32,2048]{1,0:T(8,128)(2,1)S(1)}, bf16[32,2048]{1,0:T(8,128)(2,1)S(1)}, u32[]{:S(2)}, u32[]{:S(2)}) collective-permute-start(bf16[32,2048]{1,0:T(8,128)(2,1)S(1)} %get-tuple-element.32), channel_id=1, source_target_pairs={{0,12},{4,8},{8,4},{12,0},{1,13},{5,9},{9,5},{13,1},{2,14},{6,10},... | collective-permute-start | bytes 393224 | tf_op jit(solution)/shard_map/ppermute | solution.py:317
  26.9 11.3 %collective-permute-start.7 = (bf16[32,2048]{1,0:T(8,128)(2,1)S(1)}, bf16[32,2048]{1,0:T(8,128)(2,1)S(1)}, u32[]{:S(2)}, u32[]{:S(2)}) collective-permute-start(bf16[32,2048]{1,0:T(8,128)(2,1)S(1)} %get-tuple-element.31), channel_id=1, source_target_pairs={{0,8},{4,12},{8,0},{12,4},{1,9},{5,13},{9,1},{13,5},{2,10},{6,14},... | collective-permute-start | bytes 393224 | tf_op jit(solution)/shard_map/ppermute | solution.py:317
  26.9 11.3 %collective-permute-start.6 = (bf16[32,2048]{1,0:T(8,128)(2,1)S(1)}, bf16[32,2048]{1,0:T(8,128)(2,1)S(1)}, u32[]{:S(2)}, u32[]{:S(2)}) collective-permute-start(bf16[32,2048]{1,0:T(8,128)(2,1)S(1)} %get-tuple-element.30), channel_id=1, source_target_pairs={{0,4},{4,0},{8,12},{12,8},{1,5},{5,1},{9,13},{13,9},{2,6},{6,2},{1... | collective-permute-start | bytes 393224 | tf_op jit(solution)/shard_map/ppermute | solution.py:317

commit v8 on v7

--- a/solution.py
+++ b/solution.py
@@ -274,6 +274,10 @@
     sent_ref[...] = out_ref[...].astype(jnp.bfloat16)
 
 
+def relayed(peers):
+    return [distance for distance in distances(peers)[1:] if distance % 2 and distance > 1]
+
+
 def product_kernel(peers, local_slots, parts, mask_ref, *refs):
     lows, (x_ref, gq_ref), outs = refs[:parts], refs[parts : parts + 2], refs[parts + 2 :]
     low = lows[0][...]
@@ -283,13 +287,23 @@
     share = rank * local_slots
     low = low.astype(jnp.bfloat16).astype(jnp.float32)
     wide_in, wide_grad = spread(low[:rank], mask_ref), spread(low[rank:], mask_ref)
+    up = mxu(wide_in, gq_ref[...], NT) * ADAPTER_SCALE
     down = mxu(wide_grad, x_ref[...], NN) * ADAPTER_SCALE
-    up = mxu(wide_in, gq_ref[...], NT) * ADAPTER_SCALE
-    for place, ref in enumerate(outs[:peers]):
-        rows = slice(place * share, (place + 1) * share)
-        ref[:share] = down[rows].astype(ref.dtype)
-        ref[share:] = up[rows].astype(ref.dtype)
-    outs[peers][...] = low[rank:].astype(jnp.bfloat16)
+    place = {distance: index for index, distance in enumerate(distances(peers))}
+    rows = {
+        distance: slice(index * share, (index + 1) * share) for distance, index in place.items()
+    }
+    own_ref, near_ref, low_ref, relay_ref, kept_ref, *far_refs = outs
+    own_ref[:share], own_ref[share:] = down[rows[0]], up[rows[0]]
+    near_ref[:share] = down[rows[1]].astype(jnp.bfloat16)
+    near_ref[share:] = up[rows[1]].astype(jnp.bfloat16)
+    low_ref[...] = low[rank:].astype(jnp.bfloat16)
+    for index, distance in enumerate(relayed(peers)):
+        part = slice(index * share, (index + 1) * share)
+        relay_ref[part] = up[rows[distance]].astype(jnp.bfloat16)
+        kept_ref[part] = up[rows[distance ^ 1]]
+    for distance, ref in zip(distances(peers)[1:-1], far_refs):
+        ref[...] = down[rows[distance]].astype(jnp.bfloat16)
 
 
 def input_kernel(peers, local_slots, mask_ref, low_ref, *refs):
@@ -362,19 +376,30 @@
         "low",
     )
     lows = [low] + [swap(low_sent, "tensor", distance) for distance in distances(parts)[1:]]
-    *terms, low_grads = call(
+    relays = relayed(peers)
+    far = distances(peers)[1:-1]
+    own_terms, near_terms, low_grads, relay, kept, *far_terms = call(
         functools.partial(product_kernel, peers, local_slots, parts),
         (mask, *lows, normed_input, query_gradient),
         [
-            jax.ShapeDtypeStruct((2 * share, width), jnp.bfloat16 if place else jnp.float32)
-            for place in range(peers)
+            jax.ShapeDtypeStruct((2 * share, width), jnp.float32),
+            jax.ShapeDtypeStruct((2 * share, width), jnp.bfloat16),
+            jax.ShapeDtypeStruct((rank, row_count), jnp.bfloat16),
+            jax.ShapeDtypeStruct((len(relays) * share, width), jnp.bfloat16),
+            jax.ShapeDtypeStruct((len(relays) * share, width), jnp.float32),
         ]
-        + [jax.ShapeDtypeStruct((rank, row_count), jnp.bfloat16)],
+        + [jax.ShapeDtypeStruct((share, width), jnp.bfloat16)] * len(far),
         10**9,
         "product",
     )
-    received = [
-        swap(part, "dp", distance) for distance, part in zip(distances(peers)[1:], terms[1:])
+    relay = swap(relay, "dp", 1)
+    far_terms = [swap(part, "dp", distance) for distance, part in zip(far, far_terms)]
+    relay, near_terms = lax.optimization_barrier((relay, near_terms))
+    near_terms = swap(near_terms, "dp", 1)
+    paired = (kept + relay.astype(jnp.float32)).astype(jnp.bfloat16)
+    paired = [
+        swap(paired[index * share : (index + 1) * share], "dp", distance ^ 1)
+        for index, distance in enumerate(relays)
     ]
     input_gradient = call(
         functools.partial(input_kernel, peers, local_slots),
@@ -383,11 +408,14 @@
         10**9,
         "input_gradient",
     )
-    total = terms[0]
-    for part in received[::-1]:
-        total = total + part.astype(jnp.float32)
-    down_gradient = total[:share].reshape(local_slots, rank, width)
-    up_gradient = total[share:].reshape(local_slots, rank, width)
+    down_gradient = own_terms[:share] + near_terms[:share].astype(jnp.float32)
+    up_gradient = own_terms[share:] + near_terms[share:].astype(jnp.float32)
+    for part in far_terms[::-1]:
+        down_gradient = down_gradient + part.astype(jnp.float32)
+    for part in paired:
+        up_gradient = up_gradient + part.astype(jnp.float32)
+    down_gradient = down_gradient.reshape(local_slots, rank, width)
+    up_gradient = up_gradient.reshape(local_slots, rank, width)
     return (input_gradient, key_gradient, value_gradient, down_gradient, up_gradient)
 
 

time: 39.2 us -> 37.9 us (0.967)
  waiting for transfers between devices: 10.9 us -> 7.39 us
  starting transfers between devices: 12.1 us -> 14.3 us
  other arithmetic: 0.07 us -> 0.78 us
  local copies, waits for them, and re-layouts: 0.74 us -> 0.03 us
    ppermute x9 -> x11, waiting for transfers between devices: 10.9 us -> 7.39 us  [swap(): return lax.ppermute(array, axis, [(i, i ^ distance) for i in range(size)])]
    ppermute x9 -> x11, starting transfers between devices: 12.1 us -> 14.3 us  [swap(): return lax.ppermute(array, axis, [(i, i ^ distance) for i in range(size)])]
    reshape x0 -> x1, other arithmetic: none -> 0.76 us  [local(): up_gradient = up_gradient.reshape(local_slots, rank, width)]
    reshape x1 -> x0, local copies, waits for them, and re-layouts: 0.72 us -> none  [local(): up_gradient = total[share:].reshape(local_slots, rank, width)]
  transfers between devices with their start and end apart: 9 -> 11, of which waited for: 5 -> 6; matrix products, arithmetic and copies ran while one was open for 0% -> 0% of each run, Pallas kernels for 29% -> 30%
where the time goes in v8:
time: 37.9 us; the launch traced here: 37.8 us
  Pallas kernels  14.5 us (38%)
  starting transfers between devices  14.3 us (38%)
  waiting for transfers between devices  7.39 us (19%)
  other arithmetic  0.78 us (2%)
  between operations  0.72 us (2%)
    ppermute x11, starting transfers between devices, swap(): return lax.ppermute(array, axis, [(i, i ^ distance) for i in range(size)])  14.3 us
    pallas_call x1, Pallas kernels, attention_backward(): pl.pallas_call(attention_kernel, in_specs=[vmem] * 5, out_specs=[pl.Block...  9.16 us
    ppermute x11, waiting for transfers between devices, swap(): return lax.ppermute(array, axis, [(i, i ^ distance) for i in range(size)])  7.39 us
    pallas_call x3, Pallas kernels, call(): pl.pallas_call(kernel, in_specs=[pl.BlockSpec(memory_space=pltpu.VMEM)] *...  4.28 us
    pallas_call x1, Pallas kernels, pack(): pl.pallas_call(functools.partial(pack_kernel, row_count, peers), in_specs...  1.07 us
  transfers between devices with their start and end apart: 11, of which 6 were waited for; matrix products, arithmetic and copies ran while one was open for 0% of the time, Pallas kernels for 30%

profile of v8, /device:TPU:0, one launch (start us, length us, event | category | flops | bytes accessed | tf_op | source)
XLA Modules:
  0.0 37.8 jit_solution(1643111036832284928)
XLA Ops:
  0.7 1.1 %pack.1 = (bf16[32,2048]{1,0:T(8,128)(2,1)S(1)}, f32[1152,128]{1,0:T(8,128)S(1)}, f32[4,512]{1,0:T(4,128)S(1)}) custom-call(s32[1,8]{1,0:T(1,128)} %len_hbm.1, s32[1,8]{1,0:T(1,128)} %adapter_hbm.1, s32[4]{0:T(128)} %slot_hbm.1, bf16[16,2048]{1,0:T(8,128)(2,1)} %bitcast.6, bf16[16,2048]{1,0:T(8,128)(2,1)} %bitcast.7), custom_call_target="tpu_custom_call" | custom-call | flops 10000000000 | bytes 1048576 | tf_op jit(solution)/shard_map/pack/pallas_call | solution.py:112
  1.8 5.1 %collective-permute-start = (bf16[32,2048]{1,0:T(8,128)(2,1)S(1)}, bf16[32,2048]{1,0:T(8,128)(2,1)S(1)}, u32[]{:S(2)}, u32[]{:S(2)}) collective-permute-start(bf16[32,2048]{1,0:T(8,128)(2,1)S(1)} %get-tuple-element.26.refs_0_), channel_id=1, source_target_pairs={{0,12},{4,8},{8,4},{12,0},{1,13},{5,9},{9,5},{13,1},{2,14},{6,10},... | collective-permute-start | bytes 393224 | tf_op jit(solution)/shard_map/ppermute | solution.py:331
  6.9 0.6 %collective-permute-start.2 = (bf16[32,2048]{1,0:T(8,128)(2,1)S(1)}, bf16[32,2048]{1,0:T(8,128)(2,1)S(1)}, u32[]{:S(2)}, u32[]{:S(2)}) collective-permute-start(bf16[32,2048]{1,0:T(8,128)(2,1)S(1)} %get-tuple-element.26.refs_0_), channel_id=1, source_target_pairs={{0,4},{4,0},{8,12},{12,8},{1,5},{5,1},{9,13},{13,9},{2,6},{6,2},{1... | collective-permute-start | bytes 393224 | tf_op jit(solution)/shard_map/ppermute | solution.py:331
  7.5 0.0 copy-start
  7.5 9.2 %attention_backward.1 = (bf16[2048,512]{1,0:T(8,128)(2,1)}, bf16[512,256]{1,0:T(8,128)(2,1)}, bf16[512,256]{1,0:T(8,128)(2,1)}, bf16[2048,512]{1,0:T(8,128)(2,1)S(1)}) custom-call(f32[1152,128]{1,0:T(8,128)S(1)} %get-tuple-element.24.bias_ref, bf16[512,2048]{1,0:T(8,128)(2,1)S(1)} %copy-done.2, bf16[512,2048]{1,0:T(8,128)(2,1)S(1)} %copy-done.3, ...), custom_call_target="tpu_custom_call" | custom-call | flops 8000000000 | bytes 8388608 | tf_op jit(solution)/shard_map/attention_backward/pallas_call | solution.py:230
  16.7 0.0 collective-permute-done.refs_1_
  16.7 1.2 %collective-permute-done.1.refs_2_ = bf16[32,2048]{1,0:T(8,128)(2,1)S(1)} collective-permute-done((bf16[32,2048]{1,0:T(8,128)(2,1)S(1)}, bf16[32,2048]{1,0:T(8,128)(2,1)S(1)}, u32[]{:S(2)}, u32[]{:S(2)}) %collective-permute-start.1) | collective-permute-done | bytes 131104 | tf_op jit(solution)/shard_map/ppermute | solution.py:331
  18.0 1.1 %low.1 = (f32[32,512]{1,0:T(8,128)S(1)}, bf16[32,512]{1,0:T(8,128)(2,1)S(1)}) custom-call(f32[4,512]{1,0:T(4,128)S(1)} %get-tuple-element.23.mask_ref, bf16[512,2048]{1,0:T(8,128)(2,1)S(1)} %copy-done, bf16[2048,512]{1,0:T(8,128)(2,1)S(1)} %get-tuple-element.25.gq_ref, bf16[32,2048]{1,0:T(8,128)(2,1)S(1)} %get-tuple-element.26.refs_0_, ...), custom_call_target="tpu_custom_call" | custom-call | flops 1000000000 | bytes 4194304 | tf_op jit(solution)/shard_map/low/pallas_call | solution.py:318
  19.1 0.3 collective-permute-start.3
  19.4 1.3 %collective-permute-start.4 = (bf16[32,512]{1,0:T(8,128)(2,1)S(1)}, bf16[32,512]{1,0:T(8,128)(2,1)S(1)}, u32[]{:S(2)}, u32[]{:S(2)}) collective-permute-start(bf16[32,512]{1,0:T(8,128)(2,1)S(1)} %get-tuple-element.28), channel_id=1, source_target_pairs={{0,2},{1,3},{2,0},{3,1},{4,6},{5,7},{6,4},{7,5},{8,10},{9,11},{10,... | collective-permute-start | bytes 98312 | tf_op jit(solution)/shard_map/ppermute | solution.py:331
  20.7 0.3 collective-permute-start.5
  21.0 1.8 %collective-permute-done.3.refs_1_ = bf16[32,512]{1,0:T(8,128)(2,1)S(1)} collective-permute-done((bf16[32,512]{1,0:T(8,128)(2,1)S(1)}, bf16[32,512]{1,0:T(8,128)(2,1)S(1)}, u32[]{:S(2)}, u32[]{:S(2)}) %collective-permute-start.3) | collective-permute-done | bytes 32800 | tf_op jit(solution)/shard_map/ppermute | solution.py:331
  22.8 0.5 %collective-permute-done.4.refs_2_ = bf16[32,512]{1,0:T(8,128)(2,1)S(1)} collective-permute-done((bf16[32,512]{1,0:T(8,128)(2,1)S(1)}, bf16[32,512]{1,0:T(8,128)(2,1)S(1)}, u32[]{:S(2)}, u32[]{:S(2)}) %collective-permute-start.4) | collective-permute-done | bytes 32800 | tf_op jit(solution)/shard_map/ppermute | solution.py:331
  23.3 1.1 %product.1 = (f32[32,2048]{1,0:T(8,128)S(1)}, bf16[32,2048]{1,0:T(8,128)(2,1)S(1)}, bf16[16,512]{1,0:T(8,128)(2,1)S(1)}, bf16[16,2048]{1,0:T(8,128)(2,1)S(1)}, f...) custom-call(f32[4,512]{1,0:T(4,128)S(1)} %get-tuple-element.23.mask_ref, ...), custom_call_target="tpu_custom_call" | custom-call | flops 1000000000 | bytes 4194304 | tf_op jit(solution)/shard_map/product/pallas_call | solution.py:318
  24.4 0.5 %collective-permute-start.6 = (bf16[16,2048]{1,0:T(8,128)(2,1)S(1)}, bf16[16,2048]{1,0:T(8,128)(2,1)S(1)}, u32[]{:S(2)}, u32[]{:S(2)}) collective-permute-start(bf16[16,2048]{1,0:T(8,128)(2,1)S(1)} %get-tuple-element.34), channel_id=1, source_target_pairs={{0,4},{4,0},{8,12},{12,8},{1,5},{5,1},{9,13},{13,9},{2,6},{6,2},{1... | collective-permute-start | bytes 196616 | tf_op jit(solution)/shard_map/ppermute | solution.py:331
  24.9 2.4 %collective-permute-start.9 = (bf16[16,2048]{1,0:T(8,128)(2,1)S(1)}, bf16[16,2048]{1,0:T(8,128)(2,1)S(1)}, u32[]{:S(2)}, u32[]{:S(2)}) collective-permute-start(bf16[16,2048]{1,0:T(8,128)(2,1)S(1)} %get-tuple-element.38), channel_id=1, source_target_pairs={{0,12},{4,8},{8,4},{12,0},{1,13},{5,9},{9,5},{13,1},{2,14},{6,10},... | collective-permute-start | bytes 196616 | tf_op jit(solution)/shard_map/ppermute | solution.py:331
  27.3 0.7 %collective-permute-start.8 = (bf16[16,2048]{1,0:T(8,128)(2,1)S(1)}, bf16[16,2048]{1,0:T(8,128)(2,1)S(1)}, u32[]{:S(2)}, u32[]{:S(2)}) collective-permute-start(bf16[16,2048]{1,0:T(8,128)(2,1)S(1)} %get-tuple-element.37), channel_id=1, source_target_pairs={{0,8},{4,12},{8,0},{12,4},{1,9},{5,13},{9,1},{13,5},{2,10},{6,14},... | collective-permute-start | bytes 196616 | tf_op jit(solution)/shard_map/ppermute | solution.py:331
  28.0 0.8 %collective-permute-done.6 = bf16[16,2048]{1,0:T(8,128)(2,1)S(1)} collective-permute-done((bf16[16,2048]{1,0:T(8,128)(2,1)S(1)}, bf16[16,2048]{1,0:T(8,128)(2,1)S(1)}, u32[]{:S(2)}, u32[]{:S(2)}) %collective-permute-start.6) | collective-permute-done | bytes 65568 | tf_op jit(solution)/shard_map/ppermute | solution.py:331
  28.7 0.5 %collective-permute-start.7 = (bf16[32,2048]{1,0:T(8,128)(2,1)S(1)}, bf16[32,2048]{1,0:T(8,128)(2,1)S(1)}, u32[]{:S(2)}, u32[]{:S(2)}) collective-permute-start(bf16[32,2048]{1,0:T(8,128)(2,1)S(1)} %get-tuple-element.36), channel_id=1, source_target_pairs={{0,4},{4,0},{8,12},{12,8},{1,5},{5,1},{9,13},{13,9},{2,6},{6,2},{1... | collective-permute-start | bytes 393224 | tf_op jit(solution)/shard_map/ppermute | solution.py:331
  29.3 2.6 %collective-permute-start.10 = (bf16[16,2048]{1,0:T(8,128)(2,1)S(1)}, bf16[16,2048]{1,0:T(8,128)(2,1)S(1)}, u32[]{:S(2)}, u32[]{:S(2)}) collective-permute-start(bf16[16,2048]{1,0:T(8,128)(2,1)S(1)} %add_convert_fusion), channel_id=1, source_target_pairs={{0,8},{4,12},{8,0},{12,4},{1,9},{5,13},{9,1},{13,5},{2,10},{6,14},... | collective-permute-start | bytes 196616 | tf_op jit(solution)/shard_map/ppermute | solution.py:331
  31.9 2.0 %input_gradient.1 = bf16[512,2048]{1,0:T(8,128)(2,1)} custom-call(f32[4,512]{1,0:T(4,128)S(1)} %get-tuple-element.23.mask_ref, bf16[16,512]{1,0:T(8,128)(2,1)S(1)} %get-tuple-element.30.low_ref, bf16[32,2048]{1,0:T(8,128)(2,1)S(1)} %get-tuple-element.26.refs_0_, bf16[32,2048]{1,0:T(8,128)(2,1)S(1)} %collective-permute-done.refs_1_, ...), custom_call_target="tpu_custom_call" | custom-call | flops 1000000000 | bytes 4194304 | tf_op jit(solution)/shard_map/input_gradient/pallas_call | solution.py:318
  33.9 1.2 %collective-permute-done.8 = bf16[16,2048]{1,0:T(8,128)(2,1)S(1)} collective-permute-done((bf16[16,2048]{1,0:T(8,128)(2,1)S(1)}, bf16[16,2048]{1,0:T(8,128)(2,1)S(1)}, u32[]{:S(2)}, u32[]{:S(2)}) %collective-permute-start.8) | collective-permute-done | bytes 65568 | tf_op jit(solution)/shard_map/ppermute | solution.py:331
  35.1 1.9 %collective-permute-done.10 = bf16[16,2048]{1,0:T(8,128)(2,1)S(1)} collective-permute-done((bf16[16,2048]{1,0:T(8,128)(2,1)S(1)}, bf16[16,2048]{1,0:T(8,128)(2,1)S(1)}, u32[]{:S(2)}, u32[]{:S(2)}) %collective-permute-start.10) | collective-permute-done | bytes 65568 | tf_op jit(solution)/shard_map/ppermute | solution.py:331
  37.0 0.8 %add_bitcast_fusion = (f32[1,16,2048]{2,1,0:T(8,128)}, f32[1,16,2048]{2,1,0:T(8,128)}) fusion(bf16[16,2048]{1,0:T(8,128)(2,1)S(1)} %collective-permute-done.10, f32[32,2048]{1,0:T(8,128)S(1)} %get-tuple-element.33, bf16[32,2048]{1,0:T(8,128)(2,1)S(1)} %collective-permute-done.7, bf16[16,2048]{1,0:T(8,128)(2,1)S(1)} %collective-permute-done.9, ...), kind=kLoop, calls=%fused_computation | loop fusion | flops 327680 | bytes 851968 | tf_op jit(solution)/shard_map/reshape | solution.py:418
  (17 shorter events, 0.1 us)
Async XLA Ops:
  0.6 6.9 %copy-start.2 = (bf16[512,2048]{1,0:T(8,128)(2,1)S(1)}, bf16[512,2048]{1,0:T(8,128)(2,1)}, u32[]{:S(2)}) copy-start(bf16[512,2048]{1,0:T(8,128)(2,1)} %q_ref.1) | copy-start | bytes 6291460
  0.6 6.9 %copy-start.3 = (bf16[512,2048]{1,0:T(8,128)(2,1)S(1)}, bf16[512,2048]{1,0:T(8,128)(2,1)}, u32[]{:S(2)}) copy-start(bf16[512,2048]{1,0:T(8,128)(2,1)} %g_ref.1) | copy-start | bytes 6291460
  0.7 6.9 %copy-start.4 = (bf16[512,256]{1,0:T(8,128)(2,1)S(1)}, bf16[512,256]{1,0:T(8,128)(2,1)}, u32[]{:S(2)}) copy-start(bf16[512,256]{1,0:T(8,128)(2,1)} %k_ref.1) | copy-start | bytes 786436
  0.7 6.9 %copy-start.5 = (bf16[512,256]{1,0:T(8,128)(2,1)S(1)}, bf16[512,256]{1,0:T(8,128)(2,1)}, u32[]{:S(2)}) copy-start(bf16[512,256]{1,0:T(8,128)(2,1)} %v_ref.1) | copy-start | bytes 786436
  1.8 15.0 %collective-permute-start = (bf16[32,2048]{1,0:T(8,128)(2,1)S(1)}, bf16[32,2048]{1,0:T(8,128)(2,1)S(1)}, u32[]{:S(2)}, u32[]{:S(2)}) collective-permute-start(bf16[32,2048]{1,0:T(8,128)(2,1)S(1)} %get-tuple-element.26.refs_0_), channel_id=1, source_target_pairs={{0,12},{4,8},{8,4},{12,0},{1,13},{5,9},{9,5},{13,1},{2,14},{6,10},... | collective-permute-start | bytes 393224 | tf_op jit(solution)/shard_map/ppermute | solution.py:331
  6.9 11.1 %collective-permute-start.1 = (bf16[32,2048]{1,0:T(8,128)(2,1)S(1)}, bf16[32,2048]{1,0:T(8,128)(2,1)S(1)}, u32[]{:S(2)}, u32[]{:S(2)}) collective-permute-start(bf16[32,2048]{1,0:T(8,128)(2,1)S(1)} %get-tuple-element.26.refs_0_), channel_id=1, source_target_pairs={{0,8},{4,12},{8,0},{12,4},{1,9},{5,13},{9,1},{13,5},{2,10},{6,14},... | collective-permute-start | bytes 393224 | tf_op jit(solution)/shard_map/ppermute | solution.py:331
  6.9 11.1 %collective-permute-start.2 = (bf16[32,2048]{1,0:T(8,128)(2,1)S(1)}, bf16[32,2048]{1,0:T(8,128)(2,1)S(1)}, u32[]{:S(2)}, u32[]{:S(2)}) collective-permute-start(bf16[32,2048]{1,0:T(8,128)(2,1)S(1)} %get-tuple-element.26.refs_0_), channel_id=1, source_target_pairs={{0,4},{4,0},{8,12},{12,8},{1,5},{5,1},{9,13},{13,9},{2,6},{6,2},{1... | collective-permute-start | bytes 393224 | tf_op jit(solution)/shard_map/ppermute | solution.py:331
  7.5 10.4 %copy-start = (bf16[512,2048]{1,0:T(8,128)(2,1)S(1)}, bf16[512,2048]{1,0:T(8,128)(2,1)}, u32[]{:S(2)}) copy-start(bf16[512,2048]{1,0:T(8,128)(2,1)} %refs_4_.1) | copy-start | bytes 6291460
  17.9 5.4 %copy-start.1 = (bf16[2048,512]{1,0:T(8,128)(2,1)S(1)}, bf16[2048,512]{1,0:T(8,128)(2,1)}, u32[]{:S(2)}) copy-start(bf16[2048,512]{1,0:T(8,128)(2,1)} %get-tuple-element.29.refs_5_) | copy-start | bytes 6291460
  19.1 3.7 %collective-permute-start.3 = (bf16[32,512]{1,0:T(8,128)(2,1)S(1)}, bf16[32,512]{1,0:T(8,128)(2,1)S(1)}, u32[]{:S(2)}, u32[]{:S(2)}) collective-permute-start(bf16[32,512]{1,0:T(8,128)(2,1)S(1)} %get-tuple-element.28), channel_id=1, source_target_pairs={{0,3},{1,2},{2,1},{3,0},{4,7},{5,6},{6,5},{7,4},{8,11},{9,10},{10,... | collective-permute-start | bytes 98312 | tf_op jit(solution)/shard_map/ppermute | solution.py:331
  19.4 3.9 %collective-permute-start.4 = (bf16[32,512]{1,0:T(8,128)(2,1)S(1)}, bf16[32,512]{1,0:T(8,128)(2,1)S(1)}, u32[]{:S(2)}, u32[]{:S(2)}) collective-permute-start(bf16[32,512]{1,0:T(8,128)(2,1)S(1)} %get-tuple-element.28), channel_id=1, source_target_pairs={{0,2},{1,3},{2,0},{3,1},{4,6},{5,7},{6,4},{7,5},{8,10},{9,11},{10,... | collective-permute-start | bytes 98312 | tf_op jit(solution)/shard_map/ppermute | solution.py:331
  20.7 2.6 %collective-permute-start.5 = (bf16[32,512]{1,0:T(8,128)(2,1)S(1)}, bf16[32,512]{1,0:T(8,128)(2,1)S(1)}, u32[]{:S(2)}, u32[]{:S(2)}) collective-permute-start(bf16[32,512]{1,0:T(8,128)(2,1)S(1)} %get-tuple-element.28), channel_id=1, source_target_pairs={{0,1},{1,0},{2,3},{3,2},{4,5},{5,4},{6,7},{7,6},{8,9},{9,8},{10,11... | collective-permute-start | bytes 98312 | tf_op jit(solution)/shard_map/ppermute | solution.py:331
  24.4 4.3 %collective-permute-start.6 = (bf16[16,2048]{1,0:T(8,128)(2,1)S(1)}, bf16[16,2048]{1,0:T(8,128)(2,1)S(1)}, u32[]{:S(2)}, u32[]{:S(2)}) collective-permute-start(bf16[16,2048]{1,0:T(8,128)(2,1)S(1)} %get-tuple-element.34), channel_id=1, source_target_pairs={{0,4},{4,0},{8,12},{12,8},{1,5},{5,1},{9,13},{13,9},{2,6},{6,2},{1... | collective-permute-start | bytes 196616 | tf_op jit(solution)/shard_map/ppermute | solution.py:331
  24.9 9.1 %collective-permute-start.9 = (bf16[16,2048]{1,0:T(8,128)(2,1)S(1)}, bf16[16,2048]{1,0:T(8,128)(2,1)S(1)}, u32[]{:S(2)}, u32[]{:S(2)}) collective-permute-start(bf16[16,2048]{1,0:T(8,128)(2,1)S(1)} %get-tuple-element.38), channel_id=1, source_target_pairs={{0,12},{4,8},{8,4},{12,0},{1,13},{5,9},{9,5},{13,1},{2,14},{6,10},... | collective-permute-start | bytes 196616 | tf_op jit(solution)/shard_map/ppermute | solution.py:331
  27.3 7.8 %collective-permute-start.8 = (bf16[16,2048]{1,0:T(8,128)(2,1)S(1)}, bf16[16,2048]{1,0:T(8,128)(2,1)S(1)}, u32[]{:S(2)}, u32[]{:S(2)}) collective-permute-start(bf16[16,2048]{1,0:T(8,128)(2,1)S(1)} %get-tuple-element.37), channel_id=1, source_target_pairs={{0,8},{4,12},{8,0},{12,4},{1,9},{5,13},{9,1},{13,5},{2,10},{6,14},... | collective-permute-start | bytes 196616 | tf_op jit(solution)/shard_map/ppermute | solution.py:331
  28.7 8.3 %collective-permute-start.7 = (bf16[32,2048]{1,0:T(8,128)(2,1)S(1)}, bf16[32,2048]{1,0:T(8,128)(2,1)S(1)}, u32[]{:S(2)}, u32[]{:S(2)}) collective-permute-start(bf16[32,2048]{1,0:T(8,128)(2,1)S(1)} %get-tuple-element.36), channel_id=1, source_target_pairs={{0,4},{4,0},{8,12},{12,8},{1,5},{5,1},{9,13},{13,9},{2,6},{6,2},{1... | collective-permute-start | bytes 393224 | tf_op jit(solution)/shard_map/ppermute | solution.py:331
  29.3 7.7 %collective-permute-start.10 = (bf16[16,2048]{1,0:T(8,128)(2,1)S(1)}, bf16[16,2048]{1,0:T(8,128)(2,1)S(1)}, u32[]{:S(2)}, u32[]{:S(2)}) collective-permute-start(bf16[16,2048]{1,0:T(8,128)(2,1)S(1)} %add_convert_fusion), channel_id=1, source_target_pairs={{0,8},{4,12},{8,0},{12,4},{1,9},{5,13},{9,1},{13,5},{2,10},{6,14},... | collective-permute-start | bytes 196616 | tf_op jit(solution)/shard_map/ppermute | solution.py:331

commit v9 on v8

--- a/solution.py
+++ b/solution.py
@@ -394,7 +394,6 @@
     )
     relay = swap(relay, "dp", 1)
     far_terms = [swap(part, "dp", distance) for distance, part in zip(far, far_terms)]
-    relay, near_terms = lax.optimization_barrier((relay, near_terms))
     near_terms = swap(near_terms, "dp", 1)
     paired = (kept + relay.astype(jnp.float32)).astype(jnp.bfloat16)
     paired = [
@@ -408,12 +407,13 @@
         10**9,
         "input_gradient",
     )
-    down_gradient = own_terms[:share] + near_terms[:share].astype(jnp.float32)
-    up_gradient = own_terms[share:] + near_terms[share:].astype(jnp.float32)
+    down_gradient, up_gradient = own_terms[:share], own_terms[share:]
     for part in far_terms[::-1]:
         down_gradient = down_gradient + part.astype(jnp.float32)
     for part in paired:
         up_gradient = up_gradient + part.astype(jnp.float32)
+    down_gradient = down_gradient + near_terms[:share].astype(jnp.float32)
+    up_gradient = up_gradient + near_terms[share:].astype(jnp.float32)
     down_gradient = down_gradient.reshape(local_slots, rank, width)
     up_gradient = up_gradient.reshape(local_slots, rank, width)
     return (input_gradient, key_gradient, value_gradient, down_gradient, up_gradient)

time: 37.9 us -> 39.6 us (1.045)
  waiting for transfers between devices: 7.39 us -> 8.71 us
  starting transfers between devices: 14.3 us -> 14.7 us
    ppermute x11, waiting for transfers between devices: 7.39 us -> 8.71 us  [swap(): return lax.ppermute(array, axis, [(i, i ^ distance) for i in range(size)])]
  transfers between devices with their start and end apart: 11 -> 11, of which waited for: 6 -> 7; matrix products, arithmetic and copies ran while one was open for 0% -> 0% of each run, Pallas kernels for 30% -> 28%
where the time goes in v9:
time: 39.6 us; the launch traced here: 39.5 us
  starting transfers between devices  14.7 us (37%)
  Pallas kernels  14.5 us (37%)
  waiting for transfers between devices  8.71 us (22%)
  other arithmetic  0.78 us (2%)
  between operations  0.72 us (2%)
    ppermute x11, starting transfers between devices, swap(): return lax.ppermute(array, axis, [(i, i ^ distance) for i in range(size)])  14.7 us
    pallas_call x1, Pallas kernels, attention_backward(): pl.pallas_call(attention_kernel, in_specs=[vmem] * 5, out_specs=[pl.Block...  9.16 us
    ppermute x11, waiting for transfers between devices, swap(): return lax.ppermute(array, axis, [(i, i ^ distance) for i in range(size)])  8.71 us
    pallas_call x3, Pallas kernels, call(): pl.pallas_call(kernel, in_specs=[pl.BlockSpec(memory_space=pltpu.VMEM)] *...  4.28 us
    pallas_call x1, Pallas kernels, pack(): pl.pallas_call(functools.partial(pack_kernel, row_count, peers), in_specs...  1.07 us
  transfers between devices with their start and end apart: 11, of which 7 were waited for; matrix products, arithmetic and copies ran while one was open for 0% of the time, Pallas kernels for 28%

profile of v9, /device:TPU:0, one launch (start us, length us, event | category | flops | bytes accessed | tf_op | source)
XLA Modules:
  0.0 39.5 jit_solution(2292960345848753171)
XLA Ops:
  0.7 1.1 %pack.1 = (bf16[32,2048]{1,0:T(8,128)(2,1)S(1)}, f32[1152,128]{1,0:T(8,128)S(1)}, f32[4,512]{1,0:T(4,128)S(1)}) custom-call(s32[1,8]{1,0:T(1,128)} %len_hbm.1, s32[1,8]{1,0:T(1,128)} %adapter_hbm.1, s32[4]{0:T(128)} %slot_hbm.1, bf16[16,2048]{1,0:T(8,128)(2,1)} %bitcast.6, bf16[16,2048]{1,0:T(8,128)(2,1)} %bitcast.7), custom_call_target="tpu_custom_call" | custom-call | flops 10000000000 | bytes 1048576 | tf_op jit(solution)/shard_map/pack/pallas_call | solution.py:112
  1.8 5.1 %collective-permute-start = (bf16[32,2048]{1,0:T(8,128)(2,1)S(1)}, bf16[32,2048]{1,0:T(8,128)(2,1)S(1)}, u32[]{:S(2)}, u32[]{:S(2)}) collective-permute-start(bf16[32,2048]{1,0:T(8,128)(2,1)S(1)} %get-tuple-element.24.refs_0_), channel_id=1, source_target_pairs={{0,12},{4,8},{8,4},{12,0},{1,13},{5,9},{9,5},{13,1},{2,14},{6,10},... | collective-permute-start | bytes 393224 | tf_op jit(solution)/shard_map/ppermute | solution.py:331
  6.9 0.6 %collective-permute-start.2 = (bf16[32,2048]{1,0:T(8,128)(2,1)S(1)}, bf16[32,2048]{1,0:T(8,128)(2,1)S(1)}, u32[]{:S(2)}, u32[]{:S(2)}) collective-permute-start(bf16[32,2048]{1,0:T(8,128)(2,1)S(1)} %get-tuple-element.24.refs_0_), channel_id=1, source_target_pairs={{0,4},{4,0},{8,12},{12,8},{1,5},{5,1},{9,13},{13,9},{2,6},{6,2},{1... | collective-permute-start | bytes 393224 | tf_op jit(solution)/shard_map/ppermute | solution.py:331
  7.5 0.0 copy-start
  7.5 9.2 %attention_backward.1 = (bf16[2048,512]{1,0:T(8,128)(2,1)}, bf16[512,256]{1,0:T(8,128)(2,1)}, bf16[512,256]{1,0:T(8,128)(2,1)}, bf16[2048,512]{1,0:T(8,128)(2,1)S(1)}) custom-call(f32[1152,128]{1,0:T(8,128)S(1)} %get-tuple-element.22.bias_ref, bf16[512,2048]{1,0:T(8,128)(2,1)S(1)} %copy-done.2, bf16[512,2048]{1,0:T(8,128)(2,1)S(1)} %copy-done.3, ...), custom_call_target="tpu_custom_call" | custom-call | flops 8000000000 | bytes 8388608 | tf_op jit(solution)/shard_map/attention_backward/pallas_call | solution.py:230
  16.7 1.2 %collective-permute-done.1.refs_2_ = bf16[32,2048]{1,0:T(8,128)(2,1)S(1)} collective-permute-done((bf16[32,2048]{1,0:T(8,128)(2,1)S(1)}, bf16[32,2048]{1,0:T(8,128)(2,1)S(1)}, u32[]{:S(2)}, u32[]{:S(2)}) %collective-permute-start.1) | collective-permute-done | bytes 131104 | tf_op jit(solution)/shard_map/ppermute | solution.py:331
  18.0 1.1 %low.1 = (f32[32,512]{1,0:T(8,128)S(1)}, bf16[32,512]{1,0:T(8,128)(2,1)S(1)}) custom-call(f32[4,512]{1,0:T(4,128)S(1)} %get-tuple-element.21.mask_ref, bf16[512,2048]{1,0:T(8,128)(2,1)S(1)} %copy-done, bf16[2048,512]{1,0:T(8,128)(2,1)S(1)} %get-tuple-element.23.gq_ref, bf16[32,2048]{1,0:T(8,128)(2,1)S(1)} %get-tuple-element.24.refs_0_, ...), custom_call_target="tpu_custom_call" | custom-call | flops 1000000000 | bytes 4194304 | tf_op jit(solution)/shard_map/low/pallas_call | solution.py:318
  19.1 0.3 collective-permute-start.3
  19.4 1.3 %collective-permute-start.4 = (bf16[32,512]{1,0:T(8,128)(2,1)S(1)}, bf16[32,512]{1,0:T(8,128)(2,1)S(1)}, u32[]{:S(2)}, u32[]{:S(2)}) collective-permute-start(bf16[32,512]{1,0:T(8,128)(2,1)S(1)} %get-tuple-element.26), channel_id=1, source_target_pairs={{0,2},{1,3},{2,0},{3,1},{4,6},{5,7},{6,4},{7,5},{8,10},{9,11},{10,... | collective-permute-start | bytes 98312 | tf_op jit(solution)/shard_map/ppermute | solution.py:331
  20.7 0.3 collective-permute-start.5
  21.0 1.8 %collective-permute-done.3.refs_1_ = bf16[32,512]{1,0:T(8,128)(2,1)S(1)} collective-permute-done((bf16[32,512]{1,0:T(8,128)(2,1)S(1)}, bf16[32,512]{1,0:T(8,128)(2,1)S(1)}, u32[]{:S(2)}, u32[]{:S(2)}) %collective-permute-start.3) | collective-permute-done | bytes 32800 | tf_op jit(solution)/shard_map/ppermute | solution.py:331
  22.8 0.5 %collective-permute-done.4.refs_2_ = bf16[32,512]{1,0:T(8,128)(2,1)S(1)} collective-permute-done((bf16[32,512]{1,0:T(8,128)(2,1)S(1)}, bf16[32,512]{1,0:T(8,128)(2,1)S(1)}, u32[]{:S(2)}, u32[]{:S(2)}) %collective-permute-start.4) | collective-permute-done | bytes 32800 | tf_op jit(solution)/shard_map/ppermute | solution.py:331
  23.3 0.0 collective-permute-done.5.refs_3_
  23.3 1.1 %product.1 = (f32[32,2048]{1,0:T(8,128)S(1)}, bf16[32,2048]{1,0:T(8,128)(2,1)S(1)}, bf16[16,512]{1,0:T(8,128)(2,1)S(1)}, bf16[16,2048]{1,0:T(8,128)(2,1)S(1)}, f...) custom-call(f32[4,512]{1,0:T(4,128)S(1)} %get-tuple-element.21.mask_ref, ...), custom_call_target="tpu_custom_call" | custom-call | flops 1000000000 | bytes 4194304 | tf_op jit(solution)/shard_map/product/pallas_call | solution.py:318
  24.4 0.5 %collective-permute-start.9 = (bf16[16,2048]{1,0:T(8,128)(2,1)S(1)}, bf16[16,2048]{1,0:T(8,128)(2,1)S(1)}, u32[]{:S(2)}, u32[]{:S(2)}) collective-permute-start(bf16[16,2048]{1,0:T(8,128)(2,1)S(1)} %get-tuple-element.36), channel_id=1, source_target_pairs={{0,4},{4,0},{8,12},{12,8},{1,5},{5,1},{9,13},{13,9},{2,6},{6,2},{1... | collective-permute-start | bytes 196616 | tf_op jit(solution)/shard_map/ppermute | solution.py:331
  24.9 1.6 %collective-permute-start.8 = (bf16[32,2048]{1,0:T(8,128)(2,1)S(1)}, bf16[32,2048]{1,0:T(8,128)(2,1)S(1)}, u32[]{:S(2)}, u32[]{:S(2)}) collective-permute-start(bf16[32,2048]{1,0:T(8,128)(2,1)S(1)} %get-tuple-element.34), channel_id=1, source_target_pairs={{0,4},{4,0},{8,12},{12,8},{1,5},{5,1},{9,13},{13,9},{2,6},{6,2},{1... | collective-permute-start | bytes 393224 | tf_op jit(solution)/shard_map/ppermute | solution.py:331
  26.5 2.4 %collective-permute-start.7 = (bf16[16,2048]{1,0:T(8,128)(2,1)S(1)}, bf16[16,2048]{1,0:T(8,128)(2,1)S(1)}, u32[]{:S(2)}, u32[]{:S(2)}) collective-permute-start(bf16[16,2048]{1,0:T(8,128)(2,1)S(1)} %get-tuple-element.33), channel_id=1, source_target_pairs={{0,12},{4,8},{8,4},{12,0},{1,13},{5,9},{9,5},{13,1},{2,14},{6,10},... | collective-permute-start | bytes 196616 | tf_op jit(solution)/shard_map/ppermute | solution.py:331
  28.9 0.5 %collective-permute-done.9 = bf16[16,2048]{1,0:T(8,128)(2,1)S(1)} collective-permute-done((bf16[16,2048]{1,0:T(8,128)(2,1)S(1)}, bf16[16,2048]{1,0:T(8,128)(2,1)S(1)}, u32[]{:S(2)}, u32[]{:S(2)}) %collective-permute-start.9) | collective-permute-done | bytes 65568 | tf_op jit(solution)/shard_map/ppermute | solution.py:331
  29.4 2.5 %collective-permute-start.10 = (bf16[16,2048]{1,0:T(8,128)(2,1)S(1)}, bf16[16,2048]{1,0:T(8,128)(2,1)S(1)}, u32[]{:S(2)}, u32[]{:S(2)}) collective-permute-start(bf16[16,2048]{1,0:T(8,128)(2,1)S(1)} %add_convert_fusion), channel_id=1, source_target_pairs={{0,8},{4,12},{8,0},{12,4},{1,9},{5,13},{9,1},{13,5},{2,10},{6,14},... | collective-permute-start | bytes 196616 | tf_op jit(solution)/shard_map/ppermute | solution.py:331
  32.0 2.0 %input_gradient.1 = bf16[512,2048]{1,0:T(8,128)(2,1)} custom-call(f32[4,512]{1,0:T(4,128)S(1)} %get-tuple-element.21.mask_ref, bf16[16,512]{1,0:T(8,128)(2,1)S(1)} %get-tuple-element.28.low_ref, bf16[32,2048]{1,0:T(8,128)(2,1)S(1)} %get-tuple-element.24.refs_0_, bf16[32,2048]{1,0:T(8,128)(2,1)S(1)} %collective-permute-done.refs_1_, ...), custom_call_target="tpu_custom_call" | custom-call | flops 1000000000 | bytes 4194304 | tf_op jit(solution)/shard_map/input_gradient/pallas_call | solution.py:318
  34.0 0.8 %collective-permute-done.7 = bf16[16,2048]{1,0:T(8,128)(2,1)S(1)} collective-permute-done((bf16[16,2048]{1,0:T(8,128)(2,1)S(1)}, bf16[16,2048]{1,0:T(8,128)(2,1)S(1)}, u32[]{:S(2)}, u32[]{:S(2)}) %collective-permute-start.7) | collective-permute-done | bytes 65568 | tf_op jit(solution)/shard_map/ppermute | solution.py:331
  34.8 3.2 %collective-permute-done.6 = bf16[16,2048]{1,0:T(8,128)(2,1)S(1)} collective-permute-done((bf16[16,2048]{1,0:T(8,128)(2,1)S(1)}, bf16[16,2048]{1,0:T(8,128)(2,1)S(1)}, u32[]{:S(2)}, u32[]{:S(2)}) %collective-permute-start.6) | collective-permute-done | bytes 65568 | tf_op jit(solution)/shard_map/ppermute | solution.py:331
  38.0 0.7 %collective-permute-done.10 = bf16[16,2048]{1,0:T(8,128)(2,1)S(1)} collective-permute-done((bf16[16,2048]{1,0:T(8,128)(2,1)S(1)}, bf16[16,2048]{1,0:T(8,128)(2,1)S(1)}, u32[]{:S(2)}, u32[]{:S(2)}) %collective-permute-start.10) | collective-permute-done | bytes 65568 | tf_op jit(solution)/shard_map/ppermute | solution.py:331
  38.7 0.8 %add_bitcast_fusion = (f32[1,16,2048]{2,1,0:T(8,128)}, f32[1,16,2048]{2,1,0:T(8,128)}) fusion(bf16[16,2048]{1,0:T(8,128)(2,1)S(1)} %collective-permute-done.10, f32[32,2048]{1,0:T(8,128)S(1)} %get-tuple-element.31, bf16[32,2048]{1,0:T(8,128)(2,1)S(1)} %collective-permute-done.8, bf16[16,2048]{1,0:T(8,128)(2,1)S(1)} %collective-permute-done.7, ...), kind=kLoop, calls=%fused_computation | loop fusion | flops 327680 | bytes 851968 | tf_op jit(solution)/shard_map/reshape | solution.py:418
  (17 shorter events, 0.1 us)
Async XLA Ops:
  0.6 6.9 %copy-start.2 = (bf16[512,2048]{1,0:T(8,128)(2,1)S(1)}, bf16[512,2048]{1,0:T(8,128)(2,1)}, u32[]{:S(2)}) copy-start(bf16[512,2048]{1,0:T(8,128)(2,1)} %q_ref.1) | copy-start | bytes 6291460
  0.6 6.9 %copy-start.3 = (bf16[512,2048]{1,0:T(8,128)(2,1)S(1)}, bf16[512,2048]{1,0:T(8,128)(2,1)}, u32[]{:S(2)}) copy-start(bf16[512,2048]{1,0:T(8,128)(2,1)} %g_ref.1) | copy-start | bytes 6291460
  0.7 6.9 %copy-start.4 = (bf16[512,256]{1,0:T(8,128)(2,1)S(1)}, bf16[512,256]{1,0:T(8,128)(2,1)}, u32[]{:S(2)}) copy-start(bf16[512,256]{1,0:T(8,128)(2,1)} %k_ref.1) | copy-start | bytes 786436
  0.7 6.9 %copy-start.5 = (bf16[512,256]{1,0:T(8,128)(2,1)S(1)}, bf16[512,256]{1,0:T(8,128)(2,1)}, u32[]{:S(2)}) copy-start(bf16[512,256]{1,0:T(8,128)(2,1)} %v_ref.1) | copy-start | bytes 786436
  1.8 15.0 %collective-permute-start = (bf16[32,2048]{1,0:T(8,128)(2,1)S(1)}, bf16[32,2048]{1,0:T(8,128)(2,1)S(1)}, u32[]{:S(2)}, u32[]{:S(2)}) collective-permute-start(bf16[32,2048]{1,0:T(8,128)(2,1)S(1)} %get-tuple-element.24.refs_0_), channel_id=1, source_target_pairs={{0,12},{4,8},{8,4},{12,0},{1,13},{5,9},{9,5},{13,1},{2,14},{6,10},... | collective-permute-start | bytes 393224 | tf_op jit(solution)/shard_map/ppermute | solution.py:331
  6.9 11.1 %collective-permute-start.1 = (bf16[32,2048]{1,0:T(8,128)(2,1)S(1)}, bf16[32,2048]{1,0:T(8,128)(2,1)S(1)}, u32[]{:S(2)}, u32[]{:S(2)}) collective-permute-start(bf16[32,2048]{1,0:T(8,128)(2,1)S(1)} %get-tuple-element.24.refs_0_), channel_id=1, source_target_pairs={{0,8},{4,12},{8,0},{12,4},{1,9},{5,13},{9,1},{13,5},{2,10},{6,14},... | collective-permute-start | bytes 393224 | tf_op jit(solution)/shard_map/ppermute | solution.py:331
  6.9 11.1 %collective-permute-start.2 = (bf16[32,2048]{1,0:T(8,128)(2,1)S(1)}, bf16[32,2048]{1,0:T(8,128)(2,1)S(1)}, u32[]{:S(2)}, u32[]{:S(2)}) collective-permute-start(bf16[32,2048]{1,0:T(8,128)(2,1)S(1)} %get-tuple-element.24.refs_0_), channel_id=1, source_target_pairs={{0,4},{4,0},{8,12},{12,8},{1,5},{5,1},{9,13},{13,9},{2,6},{6,2},{1... | collective-permute-start | bytes 393224 | tf_op jit(solution)/shard_map/ppermute | solution.py:331
  7.5 10.4 %copy-start = (bf16[512,2048]{1,0:T(8,128)(2,1)S(1)}, bf16[512,2048]{1,0:T(8,128)(2,1)}, u32[]{:S(2)}) copy-start(bf16[512,2048]{1,0:T(8,128)(2,1)} %refs_4_.1) | copy-start | bytes 6291460
  17.9 5.4 %copy-start.1 = (bf16[2048,512]{1,0:T(8,128)(2,1)S(1)}, bf16[2048,512]{1,0:T(8,128)(2,1)}, u32[]{:S(2)}) copy-start(bf16[2048,512]{1,0:T(8,128)(2,1)} %get-tuple-element.27.refs_5_) | copy-start | bytes 6291460
  19.1 3.7 %collective-permute-start.3 = (bf16[32,512]{1,0:T(8,128)(2,1)S(1)}, bf16[32,512]{1,0:T(8,128)(2,1)S(1)}, u32[]{:S(2)}, u32[]{:S(2)}) collective-permute-start(bf16[32,512]{1,0:T(8,128)(2,1)S(1)} %get-tuple-element.26), channel_id=1, source_target_pairs={{0,3},{1,2},{2,1},{3,0},{4,7},{5,6},{6,5},{7,4},{8,11},{9,10},{10,... | collective-permute-start | bytes 98312 | tf_op jit(solution)/shard_map/ppermute | solution.py:331
  19.4 3.9 %collective-permute-start.4 = (bf16[32,512]{1,0:T(8,128)(2,1)S(1)}, bf16[32,512]{1,0:T(8,128)(2,1)S(1)}, u32[]{:S(2)}, u32[]{:S(2)}) collective-permute-start(bf16[32,512]{1,0:T(8,128)(2,1)S(1)} %get-tuple-element.26), channel_id=1, source_target_pairs={{0,2},{1,3},{2,0},{3,1},{4,6},{5,7},{6,4},{7,5},{8,10},{9,11},{10,... | collective-permute-start | bytes 98312 | tf_op jit(solution)/shard_map/ppermute | solution.py:331
  20.7 2.6 %collective-permute-start.5 = (bf16[32,512]{1,0:T(8,128)(2,1)S(1)}, bf16[32,512]{1,0:T(8,128)(2,1)S(1)}, u32[]{:S(2)}, u32[]{:S(2)}) collective-permute-start(bf16[32,512]{1,0:T(8,128)(2,1)S(1)} %get-tuple-element.26), channel_id=1, source_target_pairs={{0,1},{1,0},{2,3},{3,2},{4,5},{5,4},{6,7},{7,6},{8,9},{9,8},{10,11... | collective-permute-start | bytes 98312 | tf_op jit(solution)/shard_map/ppermute | solution.py:331
  24.4 5.0 %collective-permute-start.9 = (bf16[16,2048]{1,0:T(8,128)(2,1)S(1)}, bf16[16,2048]{1,0:T(8,128)(2,1)S(1)}, u32[]{:S(2)}, u32[]{:S(2)}) collective-permute-start(bf16[16,2048]{1,0:T(8,128)(2,1)S(1)} %get-tuple-element.36), channel_id=1, source_target_pairs={{0,4},{4,0},{8,12},{12,8},{1,5},{5,1},{9,13},{13,9},{2,6},{6,2},{1... | collective-permute-start | bytes 196616 | tf_op jit(solution)/shard_map/ppermute | solution.py:331
  24.9 13.1 %collective-permute-start.8 = (bf16[32,2048]{1,0:T(8,128)(2,1)S(1)}, bf16[32,2048]{1,0:T(8,128)(2,1)S(1)}, u32[]{:S(2)}, u32[]{:S(2)}) collective-permute-start(bf16[32,2048]{1,0:T(8,128)(2,1)S(1)} %get-tuple-element.34), channel_id=1, source_target_pairs={{0,4},{4,0},{8,12},{12,8},{1,5},{5,1},{9,13},{13,9},{2,6},{6,2},{1... | collective-permute-start | bytes 393224 | tf_op jit(solution)/shard_map/ppermute | solution.py:331
  26.5 8.3 %collective-permute-start.7 = (bf16[16,2048]{1,0:T(8,128)(2,1)S(1)}, bf16[16,2048]{1,0:T(8,128)(2,1)S(1)}, u32[]{:S(2)}, u32[]{:S(2)}) collective-permute-start(bf16[16,2048]{1,0:T(8,128)(2,1)S(1)} %get-tuple-element.33), channel_id=1, source_target_pairs={{0,12},{4,8},{8,4},{12,0},{1,13},{5,9},{9,5},{13,1},{2,14},{6,10},... | collective-permute-start | bytes 196616 | tf_op jit(solution)/shard_map/ppermute | solution.py:331
  28.9 9.1 %collective-permute-start.6 = (bf16[16,2048]{1,0:T(8,128)(2,1)S(1)}, bf16[16,2048]{1,0:T(8,128)(2,1)S(1)}, u32[]{:S(2)}, u32[]{:S(2)}) collective-permute-start(bf16[16,2048]{1,0:T(8,128)(2,1)S(1)} %get-tuple-element.32), channel_id=1, source_target_pairs={{0,8},{4,12},{8,0},{12,4},{1,9},{5,13},{9,1},{13,5},{2,10},{6,14},... | collective-permute-start | bytes 196616 | tf_op jit(solution)/shard_map/ppermute | solution.py:331
  29.4 9.3 %collective-permute-start.10 = (bf16[16,2048]{1,0:T(8,128)(2,1)S(1)}, bf16[16,2048]{1,0:T(8,128)(2,1)S(1)}, u32[]{:S(2)}, u32[]{:S(2)}) collective-permute-start(bf16[16,2048]{1,0:T(8,128)(2,1)S(1)} %add_convert_fusion), channel_id=1, source_target_pairs={{0,8},{4,12},{8,0},{12,4},{1,9},{5,13},{9,1},{13,5},{2,10},{6,14},... | collective-permute-start | bytes 196616 | tf_op jit(solution)/shard_map/ppermute | solution.py:331

commit v10 on v9

--- a/solution.py
+++ b/solution.py
@@ -293,10 +293,10 @@
     rows = {
         distance: slice(index * share, (index + 1) * share) for distance, index in place.items()
     }
-    own_ref, near_ref, low_ref, relay_ref, kept_ref, *far_refs = outs
+    own_ref, near_down_ref, near_up_ref, low_ref, relay_ref, kept_ref, *far_refs = outs
     own_ref[:share], own_ref[share:] = down[rows[0]], up[rows[0]]
-    near_ref[:share] = down[rows[1]].astype(jnp.bfloat16)
-    near_ref[share:] = up[rows[1]].astype(jnp.bfloat16)
+    near_down_ref[...] = down[rows[1]].astype(jnp.bfloat16)
+    near_up_ref[...] = up[rows[1]].astype(jnp.bfloat16)
     low_ref[...] = low[rank:].astype(jnp.bfloat16)
     for index, distance in enumerate(relayed(peers)):
         part = slice(index * share, (index + 1) * share)
@@ -378,12 +378,13 @@
     lows = [low] + [swap(low_sent, "tensor", distance) for distance in distances(parts)[1:]]
     relays = relayed(peers)
     far = distances(peers)[1:-1]
-    own_terms, near_terms, low_grads, relay, kept, *far_terms = call(
+    own_terms, near_down, near_up, low_grads, relay, kept, *far_terms = call(
         functools.partial(product_kernel, peers, local_slots, parts),
         (mask, *lows, normed_input, query_gradient),
         [
             jax.ShapeDtypeStruct((2 * share, width), jnp.float32),
-            jax.ShapeDtypeStruct((2 * share, width), jnp.bfloat16),
+            jax.ShapeDtypeStruct((share, width), jnp.bfloat16),
+            jax.ShapeDtypeStruct((share, width), jnp.bfloat16),
             jax.ShapeDtypeStruct((rank, row_count), jnp.bfloat16),
             jax.ShapeDtypeStruct((len(relays) * share, width), jnp.bfloat16),
             jax.ShapeDtypeStruct((len(relays) * share, width), jnp.float32),
@@ -394,7 +395,8 @@
     )
     relay = swap(relay, "dp", 1)
     far_terms = [swap(part, "dp", distance) for distance, part in zip(far, far_terms)]
-    near_terms = swap(near_terms, "dp", 1)
+    relay, near_down, near_up = lax.optimization_barrier((relay, near_down, near_up))
+    near_down, near_up = swap(near_down, "dp", 1), swap(near_up, "dp", 1)
     paired = (kept + relay.astype(jnp.float32)).astype(jnp.bfloat16)
     paired = [
         swap(paired[index * share : (index + 1) * share], "dp", distance ^ 1)
@@ -407,13 +409,12 @@
         10**9,
         "input_gradient",
     )
-    down_gradient, up_gradient = own_terms[:share], own_terms[share:]
+    down_gradient = own_terms[:share] + near_down.astype(jnp.float32)
+    up_gradient = own_terms[share:] + near_up.astype(jnp.float32)
     for part in far_terms[::-1]:
         down_gradient = down_gradient + part.astype(jnp.float32)
     for part in paired:
         up_gradient = up_gradient + part.astype(jnp.float32)
-    down_gradient = down_gradient + near_terms[:share].astype(jnp.float32)
-    up_gradient = up_gradient + near_terms[share:].astype(jnp.float32)
     down_gradient = down_gradient.reshape(local_slots, rank, width)
     up_gradient = up_gradient.reshape(local_slots, rank, width)
     return (input_gradient, key_gradient, value_gradient, down_gradient, up_gradient)

time: 39.6 us -> 39.1 us (0.987)
  waiting for transfers between devices: 8.71 us -> 7.86 us
  starting transfers between devices: 14.7 us -> 15.1 us
    ppermute x11 -> x12, waiting for transfers between devices: 8.71 us -> 7.86 us  [swap(): return lax.ppermute(array, axis, [(i, i ^ distance) for i in range(size)])]
    ppermute x11 -> x12, starting transfers between devices: 14.7 us -> 15.1 us  [swap(): return lax.ppermute(array, axis, [(i, i ^ distance) for i in range(size)])]
  transfers between devices with their start and end apart: 11 -> 12, of which waited for: 7 -> 8; matrix products, arithmetic and copies ran while one was open for 0% -> 0% of each run, Pallas kernels for 28% -> 29%
where the time goes in v10:
time: 39.1 us; the launch traced here: 39 us
  starting transfers between devices  15.1 us (39%)
  Pallas kernels  14.5 us (37%)
  waiting for transfers between devices  7.86 us (20%)
  other arithmetic  0.77 us (2%)
  between operations  0.72 us (2%)
    ppermute x12, starting transfers between devices, swap(): return lax.ppermute(array, axis, [(i, i ^ distance) for i in range(size)])  15.1 us
    pallas_call x1, Pallas kernels, attention_backward(): pl.pallas_call(attention_kernel, in_specs=[vmem] * 5, out_specs=[pl.Block...  9.16 us
    ppermute x12, waiting for transfers between devices, swap(): return lax.ppermute(array, axis, [(i, i ^ distance) for i in range(size)])  7.86 us
    pallas_call x3, Pallas kernels, call(): pl.pallas_call(kernel, in_specs=[pl.BlockSpec(memory_space=pltpu.VMEM)] *...  4.28 us
    pallas_call x1, Pallas kernels, pack(): pl.pallas_call(functools.partial(pack_kernel, row_count, peers), in_specs...  1.07 us
  transfers between devices with their start and end apart: 12, of which 8 were waited for; matrix products, arithmetic and copies ran while one was open for 0% of the time, Pallas kernels for 29%

profile of v10, /device:TPU:0, one launch (start us, length us, event | category | flops | bytes accessed | tf_op | source)
XLA Modules:
  0.0 39.0 jit_solution(17961481164278696126)
XLA Ops:
  0.7 1.1 %pack.1 = (bf16[32,2048]{1,0:T(8,128)(2,1)S(1)}, f32[1152,128]{1,0:T(8,128)S(1)}, f32[4,512]{1,0:T(4,128)S(1)}) custom-call(s32[1,8]{1,0:T(1,128)} %len_hbm.1, s32[1,8]{1,0:T(1,128)} %adapter_hbm.1, s32[4]{0:T(128)} %slot_hbm.1, bf16[16,2048]{1,0:T(8,128)(2,1)} %bitcast.6, bf16[16,2048]{1,0:T(8,128)(2,1)} %bitcast.7), custom_call_target="tpu_custom_call" | custom-call | flops 10000000000 | bytes 1048576 | tf_op jit(solution)/shard_map/pack/pallas_call | solution.py:112
  1.8 5.1 %collective-permute-start = (bf16[32,2048]{1,0:T(8,128)(2,1)S(1)}, bf16[32,2048]{1,0:T(8,128)(2,1)S(1)}, u32[]{:S(2)}, u32[]{:S(2)}) collective-permute-start(bf16[32,2048]{1,0:T(8,128)(2,1)S(1)} %get-tuple-element.28.refs_0_), channel_id=1, source_target_pairs={{0,12},{4,8},{8,4},{12,0},{1,13},{5,9},{9,5},{13,1},{2,14},{6,10},... | collective-permute-start | bytes 393224 | tf_op jit(solution)/shard_map/ppermute | solution.py:331
  6.9 0.6 %collective-permute-start.2 = (bf16[32,2048]{1,0:T(8,128)(2,1)S(1)}, bf16[32,2048]{1,0:T(8,128)(2,1)S(1)}, u32[]{:S(2)}, u32[]{:S(2)}) collective-permute-start(bf16[32,2048]{1,0:T(8,128)(2,1)S(1)} %get-tuple-element.28.refs_0_), channel_id=1, source_target_pairs={{0,4},{4,0},{8,12},{12,8},{1,5},{5,1},{9,13},{13,9},{2,6},{6,2},{1... | collective-permute-start | bytes 393224 | tf_op jit(solution)/shard_map/ppermute | solution.py:331
  7.5 9.2 %attention_backward.1 = (bf16[2048,512]{1,0:T(8,128)(2,1)}, bf16[512,256]{1,0:T(8,128)(2,1)}, bf16[512,256]{1,0:T(8,128)(2,1)}, bf16[2048,512]{1,0:T(8,128)(2,1)S(1)}) custom-call(f32[1152,128]{1,0:T(8,128)S(1)} %get-tuple-element.26.bias_ref, bf16[512,2048]{1,0:T(8,128)(2,1)S(1)} %copy-done.2, bf16[512,2048]{1,0:T(8,128)(2,1)S(1)} %copy-done.3, ...), custom_call_target="tpu_custom_call" | custom-call | flops 8000000000 | bytes 8388608 | tf_op jit(solution)/shard_map/attention_backward/pallas_call | solution.py:230
  16.7 1.2 %collective-permute-done.1.refs_2_ = bf16[32,2048]{1,0:T(8,128)(2,1)S(1)} collective-permute-done((bf16[32,2048]{1,0:T(8,128)(2,1)S(1)}, bf16[32,2048]{1,0:T(8,128)(2,1)S(1)}, u32[]{:S(2)}, u32[]{:S(2)}) %collective-permute-start.1) | collective-permute-done | bytes 131104 | tf_op jit(solution)/shard_map/ppermute | solution.py:331
  18.0 1.1 %low.1 = (f32[32,512]{1,0:T(8,128)S(1)}, bf16[32,512]{1,0:T(8,128)(2,1)S(1)}) custom-call(f32[4,512]{1,0:T(4,128)S(1)} %get-tuple-element.25.mask_ref, bf16[512,2048]{1,0:T(8,128)(2,1)S(1)} %copy-done, bf16[2048,512]{1,0:T(8,128)(2,1)S(1)} %get-tuple-element.27.gq_ref, bf16[32,2048]{1,0:T(8,128)(2,1)S(1)} %get-tuple-element.28.refs_0_, ...), custom_call_target="tpu_custom_call" | custom-call | flops 1000000000 | bytes 4194304 | tf_op jit(solution)/shard_map/low/pallas_call | solution.py:318
  19.1 0.3 collective-permute-start.3
  19.4 1.3 %collective-permute-start.4 = (bf16[32,512]{1,0:T(8,128)(2,1)S(1)}, bf16[32,512]{1,0:T(8,128)(2,1)S(1)}, u32[]{:S(2)}, u32[]{:S(2)}) collective-permute-start(bf16[32,512]{1,0:T(8,128)(2,1)S(1)} %get-tuple-element.30), channel_id=1, source_target_pairs={{0,2},{1,3},{2,0},{3,1},{4,6},{5,7},{6,4},{7,5},{8,10},{9,11},{10,... | collective-permute-start | bytes 98312 | tf_op jit(solution)/shard_map/ppermute | solution.py:331
  21.0 1.8 %collective-permute-done.3.refs_1_ = bf16[32,512]{1,0:T(8,128)(2,1)S(1)} collective-permute-done((bf16[32,512]{1,0:T(8,128)(2,1)S(1)}, bf16[32,512]{1,0:T(8,128)(2,1)S(1)}, u32[]{:S(2)}, u32[]{:S(2)}) %collective-permute-start.3) | collective-permute-done | bytes 32800 | tf_op jit(solution)/shard_map/ppermute | solution.py:331
  22.8 0.5 %collective-permute-done.4.refs_2_ = bf16[32,512]{1,0:T(8,128)(2,1)S(1)} collective-permute-done((bf16[32,512]{1,0:T(8,128)(2,1)S(1)}, bf16[32,512]{1,0:T(8,128)(2,1)S(1)}, u32[]{:S(2)}, u32[]{:S(2)}) %collective-permute-start.4) | collective-permute-done | bytes 32800 | tf_op jit(solution)/shard_map/ppermute | solution.py:331
  23.3 1.1 %product.1 = (f32[32,2048]{1,0:T(8,128)S(1)}, bf16[16,2048]{1,0:T(8,128)(2,1)S(1)}, bf16[16,2048]{1,0:T(8,128)(2,1)S(1)}, bf16[16,512]{1,0:T(8,128)(2,1)S(1)}, b...) custom-call(f32[4,512]{1,0:T(4,128)S(1)} %get-tuple-element.25.mask_, ...), custom_call_target="tpu_custom_call" | custom-call | flops 1000000000 | bytes 4194304 | tf_op jit(solution)/shard_map/product/pallas_call | solution.py:318
  24.4 0.5 %collective-permute-start.6 = (bf16[16,2048]{1,0:T(8,128)(2,1)S(1)}, bf16[16,2048]{1,0:T(8,128)(2,1)S(1)}, u32[]{:S(2)}, u32[]{:S(2)}) collective-permute-start(bf16[16,2048]{1,0:T(8,128)(2,1)S(1)} %get-tuple-element.36), channel_id=1, source_target_pairs={{0,4},{4,0},{8,12},{12,8},{1,5},{5,1},{9,13},{13,9},{2,6},{6,2},{1... | collective-permute-start | bytes 196616 | tf_op jit(solution)/shard_map/ppermute | solution.py:331
  24.9 2.4 %collective-permute-start.9 = (bf16[16,2048]{1,0:T(8,128)(2,1)S(1)}, bf16[16,2048]{1,0:T(8,128)(2,1)S(1)}, u32[]{:S(2)}, u32[]{:S(2)}) collective-permute-start(bf16[16,2048]{1,0:T(8,128)(2,1)S(1)} %get-tuple-element.41), channel_id=1, source_target_pairs={{0,12},{4,8},{8,4},{12,0},{1,13},{5,9},{9,5},{13,1},{2,14},{6,10},... | collective-permute-start | bytes 196616 | tf_op jit(solution)/shard_map/ppermute | solution.py:331
  27.3 0.7 %collective-permute-start.8 = (bf16[16,2048]{1,0:T(8,128)(2,1)S(1)}, bf16[16,2048]{1,0:T(8,128)(2,1)S(1)}, u32[]{:S(2)}, u32[]{:S(2)}) collective-permute-start(bf16[16,2048]{1,0:T(8,128)(2,1)S(1)} %get-tuple-element.40), channel_id=1, source_target_pairs={{0,8},{4,12},{8,0},{12,4},{1,9},{5,13},{9,1},{13,5},{2,10},{6,14},... | collective-permute-start | bytes 196616 | tf_op jit(solution)/shard_map/ppermute | solution.py:331
  28.0 0.8 %collective-permute-done.6 = bf16[16,2048]{1,0:T(8,128)(2,1)S(1)} collective-permute-done((bf16[16,2048]{1,0:T(8,128)(2,1)S(1)}, bf16[16,2048]{1,0:T(8,128)(2,1)S(1)}, u32[]{:S(2)}, u32[]{:S(2)}) %collective-permute-start.6) | collective-permute-done | bytes 65568 | tf_op jit(solution)/shard_map/ppermute | solution.py:331
  28.8 1.8 %collective-permute-start.11 = (bf16[16,2048]{1,0:T(8,128)(2,1)S(1)}, bf16[16,2048]{1,0:T(8,128)(2,1)S(1)}, u32[]{:S(2)}, u32[]{:S(2)}) collective-permute-start(bf16[16,2048]{1,0:T(8,128)(2,1)S(1)} %add_convert_fusion), channel_id=1, source_target_pairs={{0,8},{4,12},{8,0},{12,4},{1,9},{5,13},{9,1},{13,5},{2,10},{6,14},... | collective-permute-start | bytes 196616 | tf_op jit(solution)/shard_map/ppermute | solution.py:331
  30.6 1.3 %collective-permute-start.10 = (bf16[16,2048]{1,0:T(8,128)(2,1)S(1)}, bf16[16,2048]{1,0:T(8,128)(2,1)S(1)}, u32[]{:S(2)}, u32[]{:S(2)}) collective-permute-start(bf16[16,2048]{1,0:T(8,128)(2,1)S(1)} %get-tuple-element.42), channel_id=1, source_target_pairs={{0,4},{4,0},{8,12},{12,8},{1,5},{5,1},{9,13},{13,9},{2,6},{6,2},{1... | collective-permute-start | bytes 196616 | tf_op jit(solution)/shard_map/ppermute | solution.py:331
  31.9 0.7 %collective-permute-start.7 = (bf16[16,2048]{1,0:T(8,128)(2,1)S(1)}, bf16[16,2048]{1,0:T(8,128)(2,1)S(1)}, u32[]{:S(2)}, u32[]{:S(2)}) collective-permute-start(bf16[16,2048]{1,0:T(8,128)(2,1)S(1)} %get-tuple-element.39), channel_id=1, source_target_pairs={{0,4},{4,0},{8,12},{12,8},{1,5},{5,1},{9,13},{13,9},{2,6},{6,2},{1... | collective-permute-start | bytes 196616 | tf_op jit(solution)/shard_map/ppermute | solution.py:331
  32.6 2.0 %input_gradient.1 = bf16[512,2048]{1,0:T(8,128)(2,1)} custom-call(f32[4,512]{1,0:T(4,128)S(1)} %get-tuple-element.25.mask_ref, bf16[16,512]{1,0:T(8,128)(2,1)S(1)} %get-tuple-element.32.low_ref, bf16[32,2048]{1,0:T(8,128)(2,1)S(1)} %get-tuple-element.28.refs_0_, bf16[32,2048]{1,0:T(8,128)(2,1)S(1)} %collective-permute-done.refs_1_, ...), custom_call_target="tpu_custom_call" | custom-call | flops 1000000000 | bytes 4194304 | tf_op jit(solution)/shard_map/input_gradient/pallas_call | solution.py:318
  34.7 1.4 %collective-permute-done.8 = bf16[16,2048]{1,0:T(8,128)(2,1)S(1)} collective-permute-done((bf16[16,2048]{1,0:T(8,128)(2,1)S(1)}, bf16[16,2048]{1,0:T(8,128)(2,1)S(1)}, u32[]{:S(2)}, u32[]{:S(2)}) %collective-permute-start.8) | collective-permute-done | bytes 65568 | tf_op jit(solution)/shard_map/ppermute | solution.py:331
  36.1 1.0 %collective-permute-done.11 = bf16[16,2048]{1,0:T(8,128)(2,1)S(1)} collective-permute-done((bf16[16,2048]{1,0:T(8,128)(2,1)S(1)}, bf16[16,2048]{1,0:T(8,128)(2,1)S(1)}, u32[]{:S(2)}, u32[]{:S(2)}) %collective-permute-start.11) | collective-permute-done | bytes 65568 | tf_op jit(solution)/shard_map/ppermute | solution.py:331
  37.1 0.4 %collective-permute-done.10 = bf16[16,2048]{1,0:T(8,128)(2,1)S(1)} collective-permute-done((bf16[16,2048]{1,0:T(8,128)(2,1)S(1)}, bf16[16,2048]{1,0:T(8,128)(2,1)S(1)}, u32[]{:S(2)}, u32[]{:S(2)}) %collective-permute-start.10) | collective-permute-done | bytes 65568 | tf_op jit(solution)/shard_map/ppermute | solution.py:331
  37.5 0.7 %collective-permute-done.7 = bf16[16,2048]{1,0:T(8,128)(2,1)S(1)} collective-permute-done((bf16[16,2048]{1,0:T(8,128)(2,1)S(1)}, bf16[16,2048]{1,0:T(8,128)(2,1)S(1)}, u32[]{:S(2)}, u32[]{:S(2)}) %collective-permute-start.7) | collective-permute-done | bytes 65568 | tf_op jit(solution)/shard_map/ppermute | solution.py:331
  38.2 0.8 %add_bitcast_fusion = (f32[1,16,2048]{2,1,0:T(8,128)}, f32[1,16,2048]{2,1,0:T(8,128)}) fusion(bf16[16,2048]{1,0:T(8,128)(2,1)S(1)} %collective-permute-done.11, bf16[16,2048]{1,0:T(8,128)(2,1)S(1)} %collective-permute-done.10, f32[32,2048]{1,0:T(8,128)S(1)} %get-tuple-element.35, bf16[16,2048]{1,0:T(8,128)(2,1)S(1)} %collective-permute-done.9, ...), kind=kLoop, calls=%fused_computation | loop fusion | flops 327680 | bytes 851968 | tf_op jit(solution)/shard_map/reshape | solution.py:419
  (19 shorter events, 0.3 us)
Async XLA Ops:
  0.6 6.9 %copy-start.2 = (bf16[512,2048]{1,0:T(8,128)(2,1)S(1)}, bf16[512,2048]{1,0:T(8,128)(2,1)}, u32[]{:S(2)}) copy-start(bf16[512,2048]{1,0:T(8,128)(2,1)} %q_ref.1) | copy-start | bytes 6291460
  0.6 6.9 %copy-start.3 = (bf16[512,2048]{1,0:T(8,128)(2,1)S(1)}, bf16[512,2048]{1,0:T(8,128)(2,1)}, u32[]{:S(2)}) copy-start(bf16[512,2048]{1,0:T(8,128)(2,1)} %g_ref.1) | copy-start | bytes 6291460
  0.7 6.9 %copy-start.4 = (bf16[512,256]{1,0:T(8,128)(2,1)S(1)}, bf16[512,256]{1,0:T(8,128)(2,1)}, u32[]{:S(2)}) copy-start(bf16[512,256]{1,0:T(8,128)(2,1)} %k_ref.1) | copy-start | bytes 786436
  0.7 6.9 %copy-start.5 = (bf16[512,256]{1,0:T(8,128)(2,1)S(1)}, bf16[512,256]{1,0:T(8,128)(2,1)}, u32[]{:S(2)}) copy-start(bf16[512,256]{1,0:T(8,128)(2,1)} %v_ref.1) | copy-start | bytes 786436
  1.8 15.0 %collective-permute-start = (bf16[32,2048]{1,0:T(8,128)(2,1)S(1)}, bf16[32,2048]{1,0:T(8,128)(2,1)S(1)}, u32[]{:S(2)}, u32[]{:S(2)}) collective-permute-start(bf16[32,2048]{1,0:T(8,128)(2,1)S(1)} %get-tuple-element.28.refs_0_), channel_id=1, source_target_pairs={{0,12},{4,8},{8,4},{12,0},{1,13},{5,9},{9,5},{13,1},{2,14},{6,10},... | collective-permute-start | bytes 393224 | tf_op jit(solution)/shard_map/ppermute | solution.py:331
  6.9 11.1 %collective-permute-start.1 = (bf16[32,2048]{1,0:T(8,128)(2,1)S(1)}, bf16[32,2048]{1,0:T(8,128)(2,1)S(1)}, u32[]{:S(2)}, u32[]{:S(2)}) collective-permute-start(bf16[32,2048]{1,0:T(8,128)(2,1)S(1)} %get-tuple-element.28.refs_0_), channel_id=1, source_target_pairs={{0,8},{4,12},{8,0},{12,4},{1,9},{5,13},{9,1},{13,5},{2,10},{6,14},... | collective-permute-start | bytes 393224 | tf_op jit(solution)/shard_map/ppermute | solution.py:331
  6.9 11.1 %collective-permute-start.2 = (bf16[32,2048]{1,0:T(8,128)(2,1)S(1)}, bf16[32,2048]{1,0:T(8,128)(2,1)S(1)}, u32[]{:S(2)}, u32[]{:S(2)}) collective-permute-start(bf16[32,2048]{1,0:T(8,128)(2,1)S(1)} %get-tuple-element.28.refs_0_), channel_id=1, source_target_pairs={{0,4},{4,0},{8,12},{12,8},{1,5},{5,1},{9,13},{13,9},{2,6},{6,2},{1... | collective-permute-start | bytes 393224 | tf_op jit(solution)/shard_map/ppermute | solution.py:331
  7.5 10.4 %copy-start = (bf16[512,2048]{1,0:T(8,128)(2,1)S(1)}, bf16[512,2048]{1,0:T(8,128)(2,1)}, u32[]{:S(2)}) copy-start(bf16[512,2048]{1,0:T(8,128)(2,1)} %refs_4_.1) | copy-start | bytes 6291460
  17.9 5.4 %copy-start.1 = (bf16[2048,512]{1,0:T(8,128)(2,1)S(1)}, bf16[2048,512]{1,0:T(8,128)(2,1)}, u32[]{:S(2)}) copy-start(bf16[2048,512]{1,0:T(8,128)(2,1)} %get-tuple-element.31.refs_5_) | copy-start | bytes 6291460
  19.1 3.7 %collective-permute-start.3 = (bf16[32,512]{1,0:T(8,128)(2,1)S(1)}, bf16[32,512]{1,0:T(8,128)(2,1)S(1)}, u32[]{:S(2)}, u32[]{:S(2)}) collective-permute-start(bf16[32,512]{1,0:T(8,128)(2,1)S(1)} %get-tuple-element.30), channel_id=1, source_target_pairs={{0,3},{1,2},{2,1},{3,0},{4,7},{5,6},{6,5},{7,4},{8,11},{9,10},{10,... | collective-permute-start | bytes 98312 | tf_op jit(solution)/shard_map/ppermute | solution.py:331
  19.4 3.9 %collective-permute-start.4 = (bf16[32,512]{1,0:T(8,128)(2,1)S(1)}, bf16[32,512]{1,0:T(8,128)(2,1)S(1)}, u32[]{:S(2)}, u32[]{:S(2)}) collective-permute-start(bf16[32,512]{1,0:T(8,128)(2,1)S(1)} %get-tuple-element.30), channel_id=1, source_target_pairs={{0,2},{1,3},{2,0},{3,1},{4,6},{5,7},{6,4},{7,5},{8,10},{9,11},{10,... | collective-permute-start | bytes 98312 | tf_op jit(solution)/shard_map/ppermute | solution.py:331
  20.7 2.6 %collective-permute-start.5 = (bf16[32,512]{1,0:T(8,128)(2,1)S(1)}, bf16[32,512]{1,0:T(8,128)(2,1)S(1)}, u32[]{:S(2)}, u32[]{:S(2)}) collective-permute-start(bf16[32,512]{1,0:T(8,128)(2,1)S(1)} %get-tuple-element.30), channel_id=1, source_target_pairs={{0,1},{1,0},{2,3},{3,2},{4,5},{5,4},{6,7},{7,6},{8,9},{9,8},{10,11... | collective-permute-start | bytes 98312 | tf_op jit(solution)/shard_map/ppermute | solution.py:331
  24.4 4.3 %collective-permute-start.6 = (bf16[16,2048]{1,0:T(8,128)(2,1)S(1)}, bf16[16,2048]{1,0:T(8,128)(2,1)S(1)}, u32[]{:S(2)}, u32[]{:S(2)}) collective-permute-start(bf16[16,2048]{1,0:T(8,128)(2,1)S(1)} %get-tuple-element.36), channel_id=1, source_target_pairs={{0,4},{4,0},{8,12},{12,8},{1,5},{5,1},{9,13},{13,9},{2,6},{6,2},{1... | collective-permute-start | bytes 196616 | tf_op jit(solution)/shard_map/ppermute | solution.py:331
  24.9 9.8 %collective-permute-start.9 = (bf16[16,2048]{1,0:T(8,128)(2,1)S(1)}, bf16[16,2048]{1,0:T(8,128)(2,1)S(1)}, u32[]{:S(2)}, u32[]{:S(2)}) collective-permute-start(bf16[16,2048]{1,0:T(8,128)(2,1)S(1)} %get-tuple-element.41), channel_id=1, source_target_pairs={{0,12},{4,8},{8,4},{12,0},{1,13},{5,9},{9,5},{13,1},{2,14},{6,10},... | collective-permute-start | bytes 196616 | tf_op jit(solution)/shard_map/ppermute | solution.py:331
  27.3 8.8 %collective-permute-start.8 = (bf16[16,2048]{1,0:T(8,128)(2,1)S(1)}, bf16[16,2048]{1,0:T(8,128)(2,1)S(1)}, u32[]{:S(2)}, u32[]{:S(2)}) collective-permute-start(bf16[16,2048]{1,0:T(8,128)(2,1)S(1)} %get-tuple-element.40), channel_id=1, source_target_pairs={{0,8},{4,12},{8,0},{12,4},{1,9},{5,13},{9,1},{13,5},{2,10},{6,14},... | collective-permute-start | bytes 196616 | tf_op jit(solution)/shard_map/ppermute | solution.py:331
  28.8 8.3 %collective-permute-start.11 = (bf16[16,2048]{1,0:T(8,128)(2,1)S(1)}, bf16[16,2048]{1,0:T(8,128)(2,1)S(1)}, u32[]{:S(2)}, u32[]{:S(2)}) collective-permute-start(bf16[16,2048]{1,0:T(8,128)(2,1)S(1)} %add_convert_fusion), channel_id=1, source_target_pairs={{0,8},{4,12},{8,0},{12,4},{1,9},{5,13},{9,1},{13,5},{2,10},{6,14},... | collective-permute-start | bytes 196616 | tf_op jit(solution)/shard_map/ppermute | solution.py:331
  30.6 6.9 %collective-permute-start.10 = (bf16[16,2048]{1,0:T(8,128)(2,1)S(1)}, bf16[16,2048]{1,0:T(8,128)(2,1)S(1)}, u32[]{:S(2)}, u32[]{:S(2)}) collective-permute-start(bf16[16,2048]{1,0:T(8,128)(2,1)S(1)} %get-tuple-element.42), channel_id=1, source_target_pairs={{0,4},{4,0},{8,12},{12,8},{1,5},{5,1},{9,13},{13,9},{2,6},{6,2},{1... | collective-permute-start | bytes 196616 | tf_op jit(solution)/shard_map/ppermute | solution.py:331
  31.9 6.3 %collective-permute-start.7 = (bf16[16,2048]{1,0:T(8,128)(2,1)S(1)}, bf16[16,2048]{1,0:T(8,128)(2,1)S(1)}, u32[]{:S(2)}, u32[]{:S(2)}) collective-permute-start(bf16[16,2048]{1,0:T(8,128)(2,1)S(1)} %get-tuple-element.39), channel_id=1, source_target_pairs={{0,4},{4,0},{8,12},{12,8},{1,5},{5,1},{9,13},{13,9},{2,6},{6,2},{1... | collective-permute-start | bytes 196616 | tf_op jit(solution)/shard_map/ppermute | solution.py:331

commit v11 on v8

--- a/solution.py
+++ b/solution.py
@@ -394,7 +394,7 @@
     )
     relay = swap(relay, "dp", 1)
     far_terms = [swap(part, "dp", distance) for distance, part in zip(far, far_terms)]
-    relay, near_terms = lax.optimization_barrier((relay, near_terms))
+    far_terms[0], near_terms = lax.optimization_barrier((far_terms[0], near_terms))
     near_terms = swap(near_terms, "dp", 1)
     paired = (kept + relay.astype(jnp.float32)).astype(jnp.bfloat16)
     paired = [

time: 37.9 us -> 39.8 us (1.050)
  waiting for transfers between devices: 7.39 us -> 10.8 us
  starting transfers between devices: 14.3 us -> 12.8 us
    ppermute x11, waiting for transfers between devices: 7.39 us -> 10.8 us  [swap(): return lax.ppermute(array, axis, [(i, i ^ distance) for i in range(size)])]
    ppermute x11, starting transfers between devices: 14.3 us -> 12.8 us  [swap(): return lax.ppermute(array, axis, [(i, i ^ distance) for i in range(size)])]
  transfers between devices with their start and end apart: 11 -> 11, of which waited for: 6 -> 6; matrix products, arithmetic and copies ran while one was open for 0% -> 0% of each run, Pallas kernels for 30% -> 28%
where the time goes in v11:
time: 39.8 us; the launch traced here: 39.7 us
  Pallas kernels  14.5 us (36%)
  starting transfers between devices  12.8 us (32%)
  waiting for transfers between devices  10.8 us (27%)
  other arithmetic  0.78 us (2%)
  between operations  0.72 us (2%)
    ppermute x11, starting transfers between devices, swap(): return lax.ppermute(array, axis, [(i, i ^ distance) for i in range(size)])  12.8 us
    ppermute x11, waiting for transfers between devices, swap(): return lax.ppermute(array, axis, [(i, i ^ distance) for i in range(size)])  10.8 us
    pallas_call x1, Pallas kernels, attention_backward(): pl.pallas_call(attention_kernel, in_specs=[vmem] * 5, out_specs=[pl.Block...  9.16 us
    pallas_call x3, Pallas kernels, call(): pl.pallas_call(kernel, in_specs=[pl.BlockSpec(memory_space=pltpu.VMEM)] *...  4.28 us
    pallas_call x1, Pallas kernels, pack(): pl.pallas_call(functools.partial(pack_kernel, row_count, peers), in_specs...  1.07 us
  transfers between devices with their start and end apart: 11, of which 6 were waited for; matrix products, arithmetic and copies ran while one was open for 0% of the time, Pallas kernels for 28%

profile of v11, /device:TPU:0, one launch (start us, length us, event | category | flops | bytes accessed | tf_op | source)
XLA Modules:
  0.0 39.7 jit_solution(17756221545557606016)
XLA Ops:
  0.7 1.1 %pack.1 = (bf16[32,2048]{1,0:T(8,128)(2,1)S(1)}, f32[1152,128]{1,0:T(8,128)S(1)}, f32[4,512]{1,0:T(4,128)S(1)}) custom-call(s32[1,8]{1,0:T(1,128)} %len_hbm.1, s32[1,8]{1,0:T(1,128)} %adapter_hbm.1, s32[4]{0:T(128)} %slot_hbm.1, bf16[16,2048]{1,0:T(8,128)(2,1)} %bitcast.6, bf16[16,2048]{1,0:T(8,128)(2,1)} %bitcast.7), custom_call_target="tpu_custom_call" | custom-call | flops 10000000000 | bytes 1048576 | tf_op jit(solution)/shard_map/pack/pallas_call | solution.py:112
  1.8 5.1 %collective-permute-start = (bf16[32,2048]{1,0:T(8,128)(2,1)S(1)}, bf16[32,2048]{1,0:T(8,128)(2,1)S(1)}, u32[]{:S(2)}, u32[]{:S(2)}) collective-permute-start(bf16[32,2048]{1,0:T(8,128)(2,1)S(1)} %get-tuple-element.26.refs_0_), channel_id=1, source_target_pairs={{0,12},{4,8},{8,4},{12,0},{1,13},{5,9},{9,5},{13,1},{2,14},{6,10},... | collective-permute-start | bytes 393224 | tf_op jit(solution)/shard_map/ppermute | solution.py:331
  6.9 0.0 collective-permute-start.1
  6.9 0.6 %collective-permute-start.2 = (bf16[32,2048]{1,0:T(8,128)(2,1)S(1)}, bf16[32,2048]{1,0:T(8,128)(2,1)S(1)}, u32[]{:S(2)}, u32[]{:S(2)}) collective-permute-start(bf16[32,2048]{1,0:T(8,128)(2,1)S(1)} %get-tuple-element.26.refs_0_), channel_id=1, source_target_pairs={{0,4},{4,0},{8,12},{12,8},{1,5},{5,1},{9,13},{13,9},{2,6},{6,2},{1... | collective-permute-start | bytes 393224 | tf_op jit(solution)/shard_map/ppermute | solution.py:331
  7.5 0.0 copy-start
  7.5 9.2 %attention_backward.1 = (bf16[2048,512]{1,0:T(8,128)(2,1)}, bf16[512,256]{1,0:T(8,128)(2,1)}, bf16[512,256]{1,0:T(8,128)(2,1)}, bf16[2048,512]{1,0:T(8,128)(2,1)S(1)}) custom-call(f32[1152,128]{1,0:T(8,128)S(1)} %get-tuple-element.24.bias_ref, bf16[512,2048]{1,0:T(8,128)(2,1)S(1)} %copy-done.2, bf16[512,2048]{1,0:T(8,128)(2,1)S(1)} %copy-done.3, ...), custom_call_target="tpu_custom_call" | custom-call | flops 8000000000 | bytes 8388608 | tf_op jit(solution)/shard_map/attention_backward/pallas_call | solution.py:230
  16.7 1.2 %collective-permute-done.1.refs_2_ = bf16[32,2048]{1,0:T(8,128)(2,1)S(1)} collective-permute-done((bf16[32,2048]{1,0:T(8,128)(2,1)S(1)}, bf16[32,2048]{1,0:T(8,128)(2,1)S(1)}, u32[]{:S(2)}, u32[]{:S(2)}) %collective-permute-start.1) | collective-permute-done | bytes 131104 | tf_op jit(solution)/shard_map/ppermute | solution.py:331
  18.0 1.1 %low.1 = (f32[32,512]{1,0:T(8,128)S(1)}, bf16[32,512]{1,0:T(8,128)(2,1)S(1)}) custom-call(f32[4,512]{1,0:T(4,128)S(1)} %get-tuple-element.23.mask_ref, bf16[512,2048]{1,0:T(8,128)(2,1)S(1)} %copy-done, bf16[2048,512]{1,0:T(8,128)(2,1)S(1)} %get-tuple-element.25.gq_ref, bf16[32,2048]{1,0:T(8,128)(2,1)S(1)} %get-tuple-element.26.refs_0_, ...), custom_call_target="tpu_custom_call" | custom-call | flops 1000000000 | bytes 4194304 | tf_op jit(solution)/shard_map/low/pallas_call | solution.py:318
  19.1 0.3 collective-permute-start.3
  19.4 1.3 %collective-permute-start.4 = (bf16[32,512]{1,0:T(8,128)(2,1)S(1)}, bf16[32,512]{1,0:T(8,128)(2,1)S(1)}, u32[]{:S(2)}, u32[]{:S(2)}) collective-permute-start(bf16[32,512]{1,0:T(8,128)(2,1)S(1)} %get-tuple-element.28), channel_id=1, source_target_pairs={{0,2},{1,3},{2,0},{3,1},{4,6},{5,7},{6,4},{7,5},{8,10},{9,11},{10,... | collective-permute-start | bytes 98312 | tf_op jit(solution)/shard_map/ppermute | solution.py:331
  20.7 0.3 collective-permute-start.5
  21.0 1.8 %collective-permute-done.3.refs_1_ = bf16[32,512]{1,0:T(8,128)(2,1)S(1)} collective-permute-done((bf16[32,512]{1,0:T(8,128)(2,1)S(1)}, bf16[32,512]{1,0:T(8,128)(2,1)S(1)}, u32[]{:S(2)}, u32[]{:S(2)}) %collective-permute-start.3) | collective-permute-done | bytes 32800 | tf_op jit(solution)/shard_map/ppermute | solution.py:331
  22.8 0.5 %collective-permute-done.4.refs_2_ = bf16[32,512]{1,0:T(8,128)(2,1)S(1)} collective-permute-done((bf16[32,512]{1,0:T(8,128)(2,1)S(1)}, bf16[32,512]{1,0:T(8,128)(2,1)S(1)}, u32[]{:S(2)}, u32[]{:S(2)}) %collective-permute-start.4) | collective-permute-done | bytes 32800 | tf_op jit(solution)/shard_map/ppermute | solution.py:331
  23.3 0.0 collective-permute-done.5.refs_3_
  23.3 1.1 %product.1 = (f32[32,2048]{1,0:T(8,128)S(1)}, bf16[32,2048]{1,0:T(8,128)(2,1)S(1)}, bf16[16,512]{1,0:T(8,128)(2,1)S(1)}, bf16[16,2048]{1,0:T(8,128)(2,1)S(1)}, f...) custom-call(f32[4,512]{1,0:T(4,128)S(1)} %get-tuple-element.23.mask_ref, ...), custom_call_target="tpu_custom_call" | custom-call | flops 1000000000 | bytes 4194304 | tf_op jit(solution)/shard_map/product/pallas_call | solution.py:318
  24.4 2.5 %collective-permute-start.6 = (bf16[16,2048]{1,0:T(8,128)(2,1)S(1)}, bf16[16,2048]{1,0:T(8,128)(2,1)S(1)}, u32[]{:S(2)}, u32[]{:S(2)}) collective-permute-start(bf16[16,2048]{1,0:T(8,128)(2,1)S(1)} %get-tuple-element.34), channel_id=1, source_target_pairs={{0,12},{4,8},{8,4},{12,0},{1,13},{5,9},{9,5},{13,1},{2,14},{6,10},... | collective-permute-start | bytes 196616 | tf_op jit(solution)/shard_map/ppermute | solution.py:331
  26.9 2.0 %collective-permute-start.8 = (bf16[16,2048]{1,0:T(8,128)(2,1)S(1)}, bf16[16,2048]{1,0:T(8,128)(2,1)S(1)}, u32[]{:S(2)}, u32[]{:S(2)}) collective-permute-start(bf16[16,2048]{1,0:T(8,128)(2,1)S(1)} %get-tuple-element.37), channel_id=1, source_target_pairs={{0,8},{4,12},{8,0},{12,4},{1,9},{5,13},{9,1},{13,5},{2,10},{6,14},... | collective-permute-start | bytes 196616 | tf_op jit(solution)/shard_map/ppermute | solution.py:331
  28.9 2.5 %collective-permute-done.6 = bf16[16,2048]{1,0:T(8,128)(2,1)S(1)} collective-permute-done((bf16[16,2048]{1,0:T(8,128)(2,1)S(1)}, bf16[16,2048]{1,0:T(8,128)(2,1)S(1)}, u32[]{:S(2)}, u32[]{:S(2)}) %collective-permute-start.6) | collective-permute-done | bytes 65568 | tf_op jit(solution)/shard_map/ppermute | solution.py:331
  31.3 0.0 collective-permute-start.7
  31.3 2.3 %collective-permute-done.9 = bf16[16,2048]{1,0:T(8,128)(2,1)S(1)} collective-permute-done((bf16[16,2048]{1,0:T(8,128)(2,1)S(1)}, bf16[16,2048]{1,0:T(8,128)(2,1)S(1)}, u32[]{:S(2)}, u32[]{:S(2)}) %collective-permute-start.9) | collective-permute-done | bytes 65568 | tf_op jit(solution)/shard_map/ppermute | solution.py:331
  33.7 0.7 %collective-permute-start.10 = (bf16[16,2048]{1,0:T(8,128)(2,1)S(1)}, bf16[16,2048]{1,0:T(8,128)(2,1)S(1)}, u32[]{:S(2)}, u32[]{:S(2)}) collective-permute-start(bf16[16,2048]{1,0:T(8,128)(2,1)S(1)} %add_convert_fusion), channel_id=1, source_target_pairs={{0,8},{4,12},{8,0},{12,4},{1,9},{5,13},{9,1},{13,5},{2,10},{6,14},... | collective-permute-start | bytes 196616 | tf_op jit(solution)/shard_map/ppermute | solution.py:331
  34.3 2.0 %input_gradient.1 = bf16[512,2048]{1,0:T(8,128)(2,1)} custom-call(f32[4,512]{1,0:T(4,128)S(1)} %get-tuple-element.23.mask_ref, bf16[16,512]{1,0:T(8,128)(2,1)S(1)} %get-tuple-element.30.low_ref, bf16[32,2048]{1,0:T(8,128)(2,1)S(1)} %get-tuple-element.26.refs_0_, bf16[32,2048]{1,0:T(8,128)(2,1)S(1)} %collective-permute-done.refs_1_, ...), custom_call_target="tpu_custom_call" | custom-call | flops 1000000000 | bytes 4194304 | tf_op jit(solution)/shard_map/input_gradient/pallas_call | solution.py:318
  36.4 2.5 %collective-permute-done.10 = bf16[16,2048]{1,0:T(8,128)(2,1)S(1)} collective-permute-done((bf16[16,2048]{1,0:T(8,128)(2,1)S(1)}, bf16[16,2048]{1,0:T(8,128)(2,1)S(1)}, u32[]{:S(2)}, u32[]{:S(2)}) %collective-permute-start.10) | collective-permute-done | bytes 65568 | tf_op jit(solution)/shard_map/ppermute | solution.py:331
  38.9 0.8 %add_bitcast_fusion = (f32[1,16,2048]{2,1,0:T(8,128)}, f32[1,16,2048]{2,1,0:T(8,128)}) fusion(bf16[16,2048]{1,0:T(8,128)(2,1)S(1)} %collective-permute-done.10, f32[32,2048]{1,0:T(8,128)S(1)} %get-tuple-element.33, bf16[32,2048]{1,0:T(8,128)(2,1)S(1)} %collective-permute-done.7, bf16[16,2048]{1,0:T(8,128)(2,1)S(1)} %collective-permute-done.6, ...), kind=kLoop, calls=%fused_computation | loop fusion | flops 327680 | bytes 851968 | tf_op jit(solution)/shard_map/reshape | solution.py:418
  (17 shorter events, 0.1 us)
Async XLA Ops:
  0.6 6.9 %copy-start.2 = (bf16[512,2048]{1,0:T(8,128)(2,1)S(1)}, bf16[512,2048]{1,0:T(8,128)(2,1)}, u32[]{:S(2)}) copy-start(bf16[512,2048]{1,0:T(8,128)(2,1)} %q_ref.1) | copy-start | bytes 6291460
  0.6 6.9 %copy-start.3 = (bf16[512,2048]{1,0:T(8,128)(2,1)S(1)}, bf16[512,2048]{1,0:T(8,128)(2,1)}, u32[]{:S(2)}) copy-start(bf16[512,2048]{1,0:T(8,128)(2,1)} %g_ref.1) | copy-start | bytes 6291460
  0.7 6.9 %copy-start.4 = (bf16[512,256]{1,0:T(8,128)(2,1)S(1)}, bf16[512,256]{1,0:T(8,128)(2,1)}, u32[]{:S(2)}) copy-start(bf16[512,256]{1,0:T(8,128)(2,1)} %k_ref.1) | copy-start | bytes 786436
  0.7 6.9 %copy-start.5 = (bf16[512,256]{1,0:T(8,128)(2,1)S(1)}, bf16[512,256]{1,0:T(8,128)(2,1)}, u32[]{:S(2)}) copy-start(bf16[512,256]{1,0:T(8,128)(2,1)} %v_ref.1) | copy-start | bytes 786436
  1.8 15.0 %collective-permute-start = (bf16[32,2048]{1,0:T(8,128)(2,1)S(1)}, bf16[32,2048]{1,0:T(8,128)(2,1)S(1)}, u32[]{:S(2)}, u32[]{:S(2)}) collective-permute-start(bf16[32,2048]{1,0:T(8,128)(2,1)S(1)} %get-tuple-element.26.refs_0_), channel_id=1, source_target_pairs={{0,12},{4,8},{8,4},{12,0},{1,13},{5,9},{9,5},{13,1},{2,14},{6,10},... | collective-permute-start | bytes 393224 | tf_op jit(solution)/shard_map/ppermute | solution.py:331
  6.9 11.1 %collective-permute-start.1 = (bf16[32,2048]{1,0:T(8,128)(2,1)S(1)}, bf16[32,2048]{1,0:T(8,128)(2,1)S(1)}, u32[]{:S(2)}, u32[]{:S(2)}) collective-permute-start(bf16[32,2048]{1,0:T(8,128)(2,1)S(1)} %get-tuple-element.26.refs_0_), channel_id=1, source_target_pairs={{0,8},{4,12},{8,0},{12,4},{1,9},{5,13},{9,1},{13,5},{2,10},{6,14},... | collective-permute-start | bytes 393224 | tf_op jit(solution)/shard_map/ppermute | solution.py:331
  6.9 11.1 %collective-permute-start.2 = (bf16[32,2048]{1,0:T(8,128)(2,1)S(1)}, bf16[32,2048]{1,0:T(8,128)(2,1)S(1)}, u32[]{:S(2)}, u32[]{:S(2)}) collective-permute-start(bf16[32,2048]{1,0:T(8,128)(2,1)S(1)} %get-tuple-element.26.refs_0_), channel_id=1, source_target_pairs={{0,4},{4,0},{8,12},{12,8},{1,5},{5,1},{9,13},{13,9},{2,6},{6,2},{1... | collective-permute-start | bytes 393224 | tf_op jit(solution)/shard_map/ppermute | solution.py:331
  7.5 10.4 %copy-start = (bf16[512,2048]{1,0:T(8,128)(2,1)S(1)}, bf16[512,2048]{1,0:T(8,128)(2,1)}, u32[]{:S(2)}) copy-start(bf16[512,2048]{1,0:T(8,128)(2,1)} %refs_4_.1) | copy-start | bytes 6291460
  17.9 5.4 %copy-start.1 = (bf16[2048,512]{1,0:T(8,128)(2,1)S(1)}, bf16[2048,512]{1,0:T(8,128)(2,1)}, u32[]{:S(2)}) copy-start(bf16[2048,512]{1,0:T(8,128)(2,1)} %get-tuple-element.29.refs_5_) | copy-start | bytes 6291460
  19.1 3.7 %collective-permute-start.3 = (bf16[32,512]{1,0:T(8,128)(2,1)S(1)}, bf16[32,512]{1,0:T(8,128)(2,1)S(1)}, u32[]{:S(2)}, u32[]{:S(2)}) collective-permute-start(bf16[32,512]{1,0:T(8,128)(2,1)S(1)} %get-tuple-element.28), channel_id=1, source_target_pairs={{0,3},{1,2},{2,1},{3,0},{4,7},{5,6},{6,5},{7,4},{8,11},{9,10},{10,... | collective-permute-start | bytes 98312 | tf_op jit(solution)/shard_map/ppermute | solution.py:331
  19.4 3.9 %collective-permute-start.4 = (bf16[32,512]{1,0:T(8,128)(2,1)S(1)}, bf16[32,512]{1,0:T(8,128)(2,1)S(1)}, u32[]{:S(2)}, u32[]{:S(2)}) collective-permute-start(bf16[32,512]{1,0:T(8,128)(2,1)S(1)} %get-tuple-element.28), channel_id=1, source_target_pairs={{0,2},{1,3},{2,0},{3,1},{4,6},{5,7},{6,4},{7,5},{8,10},{9,11},{10,... | collective-permute-start | bytes 98312 | tf_op jit(solution)/shard_map/ppermute | solution.py:331
  20.7 2.6 %collective-permute-start.5 = (bf16[32,512]{1,0:T(8,128)(2,1)S(1)}, bf16[32,512]{1,0:T(8,128)(2,1)S(1)}, u32[]{:S(2)}, u32[]{:S(2)}) collective-permute-start(bf16[32,512]{1,0:T(8,128)(2,1)S(1)} %get-tuple-element.28), channel_id=1, source_target_pairs={{0,1},{1,0},{2,3},{3,2},{4,5},{5,4},{6,7},{7,6},{8,9},{9,8},{10,11... | collective-permute-start | bytes 98312 | tf_op jit(solution)/shard_map/ppermute | solution.py:331
  24.4 6.9 %collective-permute-start.6 = (bf16[16,2048]{1,0:T(8,128)(2,1)S(1)}, bf16[16,2048]{1,0:T(8,128)(2,1)S(1)}, u32[]{:S(2)}, u32[]{:S(2)}) collective-permute-start(bf16[16,2048]{1,0:T(8,128)(2,1)S(1)} %get-tuple-element.34), channel_id=1, source_target_pairs={{0,12},{4,8},{8,4},{12,0},{1,13},{5,9},{9,5},{13,1},{2,14},{6,10},... | collective-permute-start | bytes 196616 | tf_op jit(solution)/shard_map/ppermute | solution.py:331
  26.9 6.7 %collective-permute-start.9 = (bf16[16,2048]{1,0:T(8,128)(2,1)S(1)}, bf16[16,2048]{1,0:T(8,128)(2,1)S(1)}, u32[]{:S(2)}, u32[]{:S(2)}) collective-permute-start(bf16[16,2048]{1,0:T(8,128)(2,1)S(1)} %get-tuple-element.40), channel_id=1, source_target_pairs={{0,4},{4,0},{8,12},{12,8},{1,5},{5,1},{9,13},{13,9},{2,6},{6,2},{1... | collective-permute-start | bytes 196616 | tf_op jit(solution)/shard_map/ppermute | solution.py:331
  26.9 9.5 %collective-permute-start.8 = (bf16[16,2048]{1,0:T(8,128)(2,1)S(1)}, bf16[16,2048]{1,0:T(8,128)(2,1)S(1)}, u32[]{:S(2)}, u32[]{:S(2)}) collective-permute-start(bf16[16,2048]{1,0:T(8,128)(2,1)S(1)} %get-tuple-element.37), channel_id=1, source_target_pairs={{0,8},{4,12},{8,0},{12,4},{1,9},{5,13},{9,1},{13,5},{2,10},{6,14},... | collective-permute-start | bytes 196616 | tf_op jit(solution)/shard_map/ppermute | solution.py:331
  31.3 7.5 %collective-permute-start.7 = (bf16[32,2048]{1,0:T(8,128)(2,1)S(1)}, bf16[32,2048]{1,0:T(8,128)(2,1)S(1)}, u32[]{:S(2)}, u32[]{:S(2)}) collective-permute-start(bf16[32,2048]{1,0:T(8,128)(2,1)S(1)} %get-tuple-element.36), channel_id=1, source_target_pairs={{0,4},{4,0},{8,12},{12,8},{1,5},{5,1},{9,13},{13,9},{2,6},{6,2},{1... | collective-permute-start | bytes 393224 | tf_op jit(solution)/shard_map/ppermute | solution.py:331
  33.7 5.2 %collective-permute-start.10 = (bf16[16,2048]{1,0:T(8,128)(2,1)S(1)}, bf16[16,2048]{1,0:T(8,128)(2,1)S(1)}, u32[]{:S(2)}, u32[]{:S(2)}) collective-permute-start(bf16[16,2048]{1,0:T(8,128)(2,1)S(1)} %add_convert_fusion), channel_id=1, source_target_pairs={{0,8},{4,12},{8,0},{12,4},{1,9},{5,13},{9,1},{13,5},{2,10},{6,14},... | collective-permute-start | bytes 196616 | tf_op jit(solution)/shard_map/ppermute | solution.py:331

commit v12 on v8

--- a/solution.py
+++ b/solution.py
@@ -410,7 +410,7 @@
     )
     down_gradient = own_terms[:share] + near_terms[:share].astype(jnp.float32)
     up_gradient = own_terms[share:] + near_terms[share:].astype(jnp.float32)
-    for part in far_terms[::-1]:
+    for part in far_terms:
         down_gradient = down_gradient + part.astype(jnp.float32)
     for part in paired:
         up_gradient = up_gradient + part.astype(jnp.float32)

time: 37.9 us -> 37.8 us (level)
  waiting for transfers between devices: 7.39 us -> 6.37 us
  starting transfers between devices: 14.3 us -> 15.3 us
    ppermute x11, waiting for transfers between devices: 7.39 us -> 6.37 us  [swap(): return lax.ppermute(array, axis, [(i, i ^ distance) for i in range(size)])]
    ppermute x11, starting transfers between devices: 14.3 us -> 15.3 us  [swap(): return lax.ppermute(array, axis, [(i, i ^ distance) for i in range(size)])]
where the time goes in v12:
time: 37.8 us; the launch traced here: 37.7 us
  starting transfers between devices  15.3 us (40%)
  Pallas kernels  14.5 us (38%)
  waiting for transfers between devices  6.37 us (17%)
  other arithmetic  0.78 us (2%)
  between operations  0.72 us (2%)
    ppermute x11, starting transfers between devices, swap(): return lax.ppermute(array, axis, [(i, i ^ distance) for i in range(size)])  15.3 us
    pallas_call x1, Pallas kernels, attention_backward(): pl.pallas_call(attention_kernel, in_specs=[vmem] * 5, out_specs=[pl.Block...  9.16 us
    ppermute x11, waiting for transfers between devices, swap(): return lax.ppermute(array, axis, [(i, i ^ distance) for i in range(size)])  6.37 us
    pallas_call x3, Pallas kernels, call(): pl.pallas_call(kernel, in_specs=[pl.BlockSpec(memory_space=pltpu.VMEM)] *...  4.28 us
    pallas_call x1, Pallas kernels, pack(): pl.pallas_call(functools.partial(pack_kernel, row_count, peers), in_specs...  1.07 us
  transfers between devices with their start and end apart: 11, of which 6 were waited for; matrix products, arithmetic and copies ran while one was open for 0% of the time, Pallas kernels for 30%

profile of v12, /device:TPU:0, one launch (start us, length us, event | category | flops | bytes accessed | tf_op | source)
XLA Modules:
  0.0 37.7 jit_solution(17988144428579272069)
XLA Ops:
  0.7 1.1 %pack.1 = (bf16[32,2048]{1,0:T(8,128)(2,1)S(1)}, f32[1152,128]{1,0:T(8,128)S(1)}, f32[4,512]{1,0:T(4,128)S(1)}) custom-call(s32[1,8]{1,0:T(1,128)} %len_hbm.1, s32[1,8]{1,0:T(1,128)} %adapter_hbm.1, s32[4]{0:T(128)} %slot_hbm.1, bf16[16,2048]{1,0:T(8,128)(2,1)} %bitcast.6, bf16[16,2048]{1,0:T(8,128)(2,1)} %bitcast.7), custom_call_target="tpu_custom_call" | custom-call | flops 10000000000 | bytes 1048576 | tf_op jit(solution)/shard_map/pack/pallas_call | solution.py:112
  1.8 5.1 %collective-permute-start = (bf16[32,2048]{1,0:T(8,128)(2,1)S(1)}, bf16[32,2048]{1,0:T(8,128)(2,1)S(1)}, u32[]{:S(2)}, u32[]{:S(2)}) collective-permute-start(bf16[32,2048]{1,0:T(8,128)(2,1)S(1)} %get-tuple-element.26.refs_0_), channel_id=1, source_target_pairs={{0,12},{4,8},{8,4},{12,0},{1,13},{5,9},{9,5},{13,1},{2,14},{6,10},... | collective-permute-start | bytes 393224 | tf_op jit(solution)/shard_map/ppermute | solution.py:331
  6.9 0.0 collective-permute-start.1
  6.9 0.6 %collective-permute-start.2 = (bf16[32,2048]{1,0:T(8,128)(2,1)S(1)}, bf16[32,2048]{1,0:T(8,128)(2,1)S(1)}, u32[]{:S(2)}, u32[]{:S(2)}) collective-permute-start(bf16[32,2048]{1,0:T(8,128)(2,1)S(1)} %get-tuple-element.26.refs_0_), channel_id=1, source_target_pairs={{0,4},{4,0},{8,12},{12,8},{1,5},{5,1},{9,13},{13,9},{2,6},{6,2},{1... | collective-permute-start | bytes 393224 | tf_op jit(solution)/shard_map/ppermute | solution.py:331
  7.5 0.0 copy-start
  7.5 9.2 %attention_backward.1 = (bf16[2048,512]{1,0:T(8,128)(2,1)}, bf16[512,256]{1,0:T(8,128)(2,1)}, bf16[512,256]{1,0:T(8,128)(2,1)}, bf16[2048,512]{1,0:T(8,128)(2,1)S(1)}) custom-call(f32[1152,128]{1,0:T(8,128)S(1)} %get-tuple-element.24.bias_ref, bf16[512,2048]{1,0:T(8,128)(2,1)S(1)} %copy-done.2, bf16[512,2048]{1,0:T(8,128)(2,1)S(1)} %copy-done.3, ...), custom_call_target="tpu_custom_call" | custom-call | flops 8000000000 | bytes 8388608 | tf_op jit(solution)/shard_map/attention_backward/pallas_call | solution.py:230
  16.7 0.0 collective-permute-done.refs_1_
  16.7 1.2 %collective-permute-done.1.refs_2_ = bf16[32,2048]{1,0:T(8,128)(2,1)S(1)} collective-permute-done((bf16[32,2048]{1,0:T(8,128)(2,1)S(1)}, bf16[32,2048]{1,0:T(8,128)(2,1)S(1)}, u32[]{:S(2)}, u32[]{:S(2)}) %collective-permute-start.1) | collective-permute-done | bytes 131104 | tf_op jit(solution)/shard_map/ppermute | solution.py:331
  18.0 1.1 %low.1 = (f32[32,512]{1,0:T(8,128)S(1)}, bf16[32,512]{1,0:T(8,128)(2,1)S(1)}) custom-call(f32[4,512]{1,0:T(4,128)S(1)} %get-tuple-element.23.mask_ref, bf16[512,2048]{1,0:T(8,128)(2,1)S(1)} %copy-done, bf16[2048,512]{1,0:T(8,128)(2,1)S(1)} %get-tuple-element.25.gq_ref, bf16[32,2048]{1,0:T(8,128)(2,1)S(1)} %get-tuple-element.26.refs_0_, ...), custom_call_target="tpu_custom_call" | custom-call | flops 1000000000 | bytes 4194304 | tf_op jit(solution)/shard_map/low/pallas_call | solution.py:318
  19.1 0.3 collective-permute-start.3
  19.4 1.3 %collective-permute-start.4 = (bf16[32,512]{1,0:T(8,128)(2,1)S(1)}, bf16[32,512]{1,0:T(8,128)(2,1)S(1)}, u32[]{:S(2)}, u32[]{:S(2)}) collective-permute-start(bf16[32,512]{1,0:T(8,128)(2,1)S(1)} %get-tuple-element.28), channel_id=1, source_target_pairs={{0,2},{1,3},{2,0},{3,1},{4,6},{5,7},{6,4},{7,5},{8,10},{9,11},{10,... | collective-permute-start | bytes 98312 | tf_op jit(solution)/shard_map/ppermute | solution.py:331
  20.7 0.3 collective-permute-start.5
  21.0 1.8 %collective-permute-done.3.refs_1_ = bf16[32,512]{1,0:T(8,128)(2,1)S(1)} collective-permute-done((bf16[32,512]{1,0:T(8,128)(2,1)S(1)}, bf16[32,512]{1,0:T(8,128)(2,1)S(1)}, u32[]{:S(2)}, u32[]{:S(2)}) %collective-permute-start.3) | collective-permute-done | bytes 32800 | tf_op jit(solution)/shard_map/ppermute | solution.py:331
  22.8 0.5 %collective-permute-done.4.refs_2_ = bf16[32,512]{1,0:T(8,128)(2,1)S(1)} collective-permute-done((bf16[32,512]{1,0:T(8,128)(2,1)S(1)}, bf16[32,512]{1,0:T(8,128)(2,1)S(1)}, u32[]{:S(2)}, u32[]{:S(2)}) %collective-permute-start.4) | collective-permute-done | bytes 32800 | tf_op jit(solution)/shard_map/ppermute | solution.py:331
  23.3 1.1 %product.1 = (f32[32,2048]{1,0:T(8,128)S(1)}, bf16[32,2048]{1,0:T(8,128)(2,1)S(1)}, bf16[16,512]{1,0:T(8,128)(2,1)S(1)}, bf16[16,2048]{1,0:T(8,128)(2,1)S(1)}, f...) custom-call(f32[4,512]{1,0:T(4,128)S(1)} %get-tuple-element.23.mask_ref, ...), custom_call_target="tpu_custom_call" | custom-call | flops 1000000000 | bytes 4194304 | tf_op jit(solution)/shard_map/product/pallas_call | solution.py:318
  24.4 0.5 %collective-permute-start.6 = (bf16[16,2048]{1,0:T(8,128)(2,1)S(1)}, bf16[16,2048]{1,0:T(8,128)(2,1)S(1)}, u32[]{:S(2)}, u32[]{:S(2)}) collective-permute-start(bf16[16,2048]{1,0:T(8,128)(2,1)S(1)} %get-tuple-element.34), channel_id=1, source_target_pairs={{0,4},{4,0},{8,12},{12,8},{1,5},{5,1},{9,13},{13,9},{2,6},{6,2},{1... | collective-permute-start | bytes 196616 | tf_op jit(solution)/shard_map/ppermute | solution.py:331
  24.9 2.6 %collective-permute-start.9 = (bf16[16,2048]{1,0:T(8,128)(2,1)S(1)}, bf16[16,2048]{1,0:T(8,128)(2,1)S(1)}, u32[]{:S(2)}, u32[]{:S(2)}) collective-permute-start(bf16[16,2048]{1,0:T(8,128)(2,1)S(1)} %get-tuple-element.38), channel_id=1, source_target_pairs={{0,8},{4,12},{8,0},{12,4},{1,9},{5,13},{9,1},{13,5},{2,10},{6,14},... | collective-permute-start | bytes 196616 | tf_op jit(solution)/shard_map/ppermute | solution.py:331
  27.5 1.4 %collective-permute-start.8 = (bf16[16,2048]{1,0:T(8,128)(2,1)S(1)}, bf16[16,2048]{1,0:T(8,128)(2,1)S(1)}, u32[]{:S(2)}, u32[]{:S(2)}) collective-permute-start(bf16[16,2048]{1,0:T(8,128)(2,1)S(1)} %get-tuple-element.37), channel_id=1, source_target_pairs={{0,12},{4,8},{8,4},{12,0},{1,13},{5,9},{9,5},{13,1},{2,14},{6,10},... | collective-permute-start | bytes 196616 | tf_op jit(solution)/shard_map/ppermute | solution.py:331
  28.9 0.7 %collective-permute-done.6 = bf16[16,2048]{1,0:T(8,128)(2,1)S(1)} collective-permute-done((bf16[16,2048]{1,0:T(8,128)(2,1)S(1)}, bf16[16,2048]{1,0:T(8,128)(2,1)S(1)}, u32[]{:S(2)}, u32[]{:S(2)}) %collective-permute-start.6) | collective-permute-done | bytes 65568 | tf_op jit(solution)/shard_map/ppermute | solution.py:331
  29.6 3.1 %collective-permute-start.10 = (bf16[16,2048]{1,0:T(8,128)(2,1)S(1)}, bf16[16,2048]{1,0:T(8,128)(2,1)S(1)}, u32[]{:S(2)}, u32[]{:S(2)}) collective-permute-start(bf16[16,2048]{1,0:T(8,128)(2,1)S(1)} %add_convert_fusion), channel_id=1, source_target_pairs={{0,8},{4,12},{8,0},{12,4},{1,9},{5,13},{9,1},{13,5},{2,10},{6,14},... | collective-permute-start | bytes 196616 | tf_op jit(solution)/shard_map/ppermute | solution.py:331
  32.7 2.0 %input_gradient.1 = bf16[512,2048]{1,0:T(8,128)(2,1)} custom-call(f32[4,512]{1,0:T(4,128)S(1)} %get-tuple-element.23.mask_ref, bf16[16,512]{1,0:T(8,128)(2,1)S(1)} %get-tuple-element.30.low_ref, bf16[32,2048]{1,0:T(8,128)(2,1)S(1)} %get-tuple-element.26.refs_0_, bf16[32,2048]{1,0:T(8,128)(2,1)S(1)} %collective-permute-done.refs_1_, ...), custom_call_target="tpu_custom_call" | custom-call | flops 1000000000 | bytes 4194304 | tf_op jit(solution)/shard_map/input_gradient/pallas_call | solution.py:318
  34.8 1.6 %collective-permute-done.10 = bf16[16,2048]{1,0:T(8,128)(2,1)S(1)} collective-permute-done((bf16[16,2048]{1,0:T(8,128)(2,1)S(1)}, bf16[16,2048]{1,0:T(8,128)(2,1)S(1)}, u32[]{:S(2)}, u32[]{:S(2)}) %collective-permute-start.10) | collective-permute-done | bytes 65568 | tf_op jit(solution)/shard_map/ppermute | solution.py:331
  36.4 0.5 %collective-permute-done.7 = bf16[32,2048]{1,0:T(8,128)(2,1)S(1)} collective-permute-done((bf16[32,2048]{1,0:T(8,128)(2,1)S(1)}, bf16[32,2048]{1,0:T(8,128)(2,1)S(1)}, u32[]{:S(2)}, u32[]{:S(2)}) %collective-permute-start.7) | collective-permute-done | bytes 131104 | tf_op jit(solution)/shard_map/ppermute | solution.py:331
  36.9 0.8 %add_bitcast_fusion = (f32[1,16,2048]{2,1,0:T(8,128)}, f32[1,16,2048]{2,1,0:T(8,128)}) fusion(bf16[16,2048]{1,0:T(8,128)(2,1)S(1)} %collective-permute-done.10, f32[32,2048]{1,0:T(8,128)S(1)} %get-tuple-element.33, bf16[32,2048]{1,0:T(8,128)(2,1)S(1)} %collective-permute-done.7, bf16[16,2048]{1,0:T(8,128)(2,1)S(1)} %collective-permute-done.9, ...), kind=kLoop, calls=%fused_computation | loop fusion | flops 327680 | bytes 851968 | tf_op jit(solution)/shard_map/reshape | solution.py:418
  (17 shorter events, 0.1 us)
Async XLA Ops:
  0.6 6.9 %copy-start.2 = (bf16[512,2048]{1,0:T(8,128)(2,1)S(1)}, bf16[512,2048]{1,0:T(8,128)(2,1)}, u32[]{:S(2)}) copy-start(bf16[512,2048]{1,0:T(8,128)(2,1)} %q_ref.1) | copy-start | bytes 6291460
  0.6 6.9 %copy-start.3 = (bf16[512,2048]{1,0:T(8,128)(2,1)S(1)}, bf16[512,2048]{1,0:T(8,128)(2,1)}, u32[]{:S(2)}) copy-start(bf16[512,2048]{1,0:T(8,128)(2,1)} %g_ref.1) | copy-start | bytes 6291460
  0.7 6.9 %copy-start.4 = (bf16[512,256]{1,0:T(8,128)(2,1)S(1)}, bf16[512,256]{1,0:T(8,128)(2,1)}, u32[]{:S(2)}) copy-start(bf16[512,256]{1,0:T(8,128)(2,1)} %k_ref.1) | copy-start | bytes 786436
  0.7 6.9 %copy-start.5 = (bf16[512,256]{1,0:T(8,128)(2,1)S(1)}, bf16[512,256]{1,0:T(8,128)(2,1)}, u32[]{:S(2)}) copy-start(bf16[512,256]{1,0:T(8,128)(2,1)} %v_ref.1) | copy-start | bytes 786436
  1.8 15.0 %collective-permute-start = (bf16[32,2048]{1,0:T(8,128)(2,1)S(1)}, bf16[32,2048]{1,0:T(8,128)(2,1)S(1)}, u32[]{:S(2)}, u32[]{:S(2)}) collective-permute-start(bf16[32,2048]{1,0:T(8,128)(2,1)S(1)} %get-tuple-element.26.refs_0_), channel_id=1, source_target_pairs={{0,12},{4,8},{8,4},{12,0},{1,13},{5,9},{9,5},{13,1},{2,14},{6,10},... | collective-permute-start | bytes 393224 | tf_op jit(solution)/shard_map/ppermute | solution.py:331
  6.9 11.1 %collective-permute-start.1 = (bf16[32,2048]{1,0:T(8,128)(2,1)S(1)}, bf16[32,2048]{1,0:T(8,128)(2,1)S(1)}, u32[]{:S(2)}, u32[]{:S(2)}) collective-permute-start(bf16[32,2048]{1,0:T(8,128)(2,1)S(1)} %get-tuple-element.26.refs_0_), channel_id=1, source_target_pairs={{0,8},{4,12},{8,0},{12,4},{1,9},{5,13},{9,1},{13,5},{2,10},{6,14},... | collective-permute-start | bytes 393224 | tf_op jit(solution)/shard_map/ppermute | solution.py:331
  6.9 11.1 %collective-permute-start.2 = (bf16[32,2048]{1,0:T(8,128)(2,1)S(1)}, bf16[32,2048]{1,0:T(8,128)(2,1)S(1)}, u32[]{:S(2)}, u32[]{:S(2)}) collective-permute-start(bf16[32,2048]{1,0:T(8,128)(2,1)S(1)} %get-tuple-element.26.refs_0_), channel_id=1, source_target_pairs={{0,4},{4,0},{8,12},{12,8},{1,5},{5,1},{9,13},{13,9},{2,6},{6,2},{1... | collective-permute-start | bytes 393224 | tf_op jit(solution)/shard_map/ppermute | solution.py:331
  7.5 10.4 %copy-start = (bf16[512,2048]{1,0:T(8,128)(2,1)S(1)}, bf16[512,2048]{1,0:T(8,128)(2,1)}, u32[]{:S(2)}) copy-start(bf16[512,2048]{1,0:T(8,128)(2,1)} %refs_4_.1) | copy-start | bytes 6291460
  17.9 5.4 %copy-start.1 = (bf16[2048,512]{1,0:T(8,128)(2,1)S(1)}, bf16[2048,512]{1,0:T(8,128)(2,1)}, u32[]{:S(2)}) copy-start(bf16[2048,512]{1,0:T(8,128)(2,1)} %get-tuple-element.29.refs_5_) | copy-start | bytes 6291460
  19.1 3.7 %collective-permute-start.3 = (bf16[32,512]{1,0:T(8,128)(2,1)S(1)}, bf16[32,512]{1,0:T(8,128)(2,1)S(1)}, u32[]{:S(2)}, u32[]{:S(2)}) collective-permute-start(bf16[32,512]{1,0:T(8,128)(2,1)S(1)} %get-tuple-element.28), channel_id=1, source_target_pairs={{0,3},{1,2},{2,1},{3,0},{4,7},{5,6},{6,5},{7,4},{8,11},{9,10},{10,... | collective-permute-start | bytes 98312 | tf_op jit(solution)/shard_map/ppermute | solution.py:331
  19.4 3.9 %collective-permute-start.4 = (bf16[32,512]{1,0:T(8,128)(2,1)S(1)}, bf16[32,512]{1,0:T(8,128)(2,1)S(1)}, u32[]{:S(2)}, u32[]{:S(2)}) collective-permute-start(bf16[32,512]{1,0:T(8,128)(2,1)S(1)} %get-tuple-element.28), channel_id=1, source_target_pairs={{0,2},{1,3},{2,0},{3,1},{4,6},{5,7},{6,4},{7,5},{8,10},{9,11},{10,... | collective-permute-start | bytes 98312 | tf_op jit(solution)/shard_map/ppermute | solution.py:331
  20.7 2.6 %collective-permute-start.5 = (bf16[32,512]{1,0:T(8,128)(2,1)S(1)}, bf16[32,512]{1,0:T(8,128)(2,1)S(1)}, u32[]{:S(2)}, u32[]{:S(2)}) collective-permute-start(bf16[32,512]{1,0:T(8,128)(2,1)S(1)} %get-tuple-element.28), channel_id=1, source_target_pairs={{0,1},{1,0},{2,3},{3,2},{4,5},{5,4},{6,7},{7,6},{8,9},{9,8},{10,11... | collective-permute-start | bytes 98312 | tf_op jit(solution)/shard_map/ppermute | solution.py:331
  24.4 5.2 %collective-permute-start.6 = (bf16[16,2048]{1,0:T(8,128)(2,1)S(1)}, bf16[16,2048]{1,0:T(8,128)(2,1)S(1)}, u32[]{:S(2)}, u32[]{:S(2)}) collective-permute-start(bf16[16,2048]{1,0:T(8,128)(2,1)S(1)} %get-tuple-element.34), channel_id=1, source_target_pairs={{0,4},{4,0},{8,12},{12,8},{1,5},{5,1},{9,13},{13,9},{2,6},{6,2},{1... | collective-permute-start | bytes 196616 | tf_op jit(solution)/shard_map/ppermute | solution.py:331
  24.9 9.9 %collective-permute-start.9 = (bf16[16,2048]{1,0:T(8,128)(2,1)S(1)}, bf16[16,2048]{1,0:T(8,128)(2,1)S(1)}, u32[]{:S(2)}, u32[]{:S(2)}) collective-permute-start(bf16[16,2048]{1,0:T(8,128)(2,1)S(1)} %get-tuple-element.38), channel_id=1, source_target_pairs={{0,8},{4,12},{8,0},{12,4},{1,9},{5,13},{9,1},{13,5},{2,10},{6,14},... | collective-permute-start | bytes 196616 | tf_op jit(solution)/shard_map/ppermute | solution.py:331
  27.5 7.3 %collective-permute-start.8 = (bf16[16,2048]{1,0:T(8,128)(2,1)S(1)}, bf16[16,2048]{1,0:T(8,128)(2,1)S(1)}, u32[]{:S(2)}, u32[]{:S(2)}) collective-permute-start(bf16[16,2048]{1,0:T(8,128)(2,1)S(1)} %get-tuple-element.37), channel_id=1, source_target_pairs={{0,12},{4,8},{8,4},{12,0},{1,13},{5,9},{9,5},{13,1},{2,14},{6,10},... | collective-permute-start | bytes 196616 | tf_op jit(solution)/shard_map/ppermute | solution.py:331
  29.6 7.3 %collective-permute-start.7 = (bf16[32,2048]{1,0:T(8,128)(2,1)S(1)}, bf16[32,2048]{1,0:T(8,128)(2,1)S(1)}, u32[]{:S(2)}, u32[]{:S(2)}) collective-permute-start(bf16[32,2048]{1,0:T(8,128)(2,1)S(1)} %get-tuple-element.36), channel_id=1, source_target_pairs={{0,4},{4,0},{8,12},{12,8},{1,5},{5,1},{9,13},{13,9},{2,6},{6,2},{1... | collective-permute-start | bytes 393224 | tf_op jit(solution)/shard_map/ppermute | solution.py:331
  29.6 6.8 %collective-permute-start.10 = (bf16[16,2048]{1,0:T(8,128)(2,1)S(1)}, bf16[16,2048]{1,0:T(8,128)(2,1)S(1)}, u32[]{:S(2)}, u32[]{:S(2)}) collective-permute-start(bf16[16,2048]{1,0:T(8,128)(2,1)S(1)} %add_convert_fusion), channel_id=1, source_target_pairs={{0,8},{4,12},{8,0},{12,4},{1,9},{5,13},{9,1},{13,5},{2,10},{6,14},... | collective-permute-start | bytes 196616 | tf_op jit(solution)/shard_map/ppermute | solution.py:331
